TPU v7x, 768 devices: a whole 4x8x12 slice. The times are simulated.
768 devices in a mesh: stratum: 16 (over y_hi, x, core), inner: 48 (over z, y_lo).
Axes of the slice: x: 4, y: 8 (y_hi: 2, y_lo: 4; y = y_hi * 4 + y_lo), z: 12, core: 2. Of those that a mesh axis runs over, the one named last changes fastest.
Arguments:
- user_factors: float32 [393216, 256], P(('stratum', 'inner')), may hold values from -2 to 2
- item_factors: float32 [12288, 256], P(('stratum', 'inner')), may hold values from -3 to 3
- item_accum: float32 [12288, 256], P(('stratum', 'inner')), may hold values from 0.5 to 4
- tile_values: bfloat16 [2, 6144, 128, 128], P(None, ('stratum', 'inner')), may hold values from -6 to 6
- tile_rows: int32 [2, 6144], P(None, ('stratum', 'inner')), may hold values from 0 to 3
- tile_cols: int32 [2, 6144], P(None, ('stratum', 'inner')), may hold values from 0 to 5
- tile_count: int32 [2, 768], P(None, ('stratum', 'inner')), may hold values from 2 to 8, as said below
- neg_ids: int32 [2, 3072], P(None, ('stratum', 'inner')), may hold values from 0 to 15
Outputs:
- users_out: float32 [393216, 256], P(('stratum', 'inner'))
- items_out: float32 [12288, 256], P(('stratum', 'inner'))
- accum_out: float32 [12288, 256], P(('stratum', 'inner'))
Inputs may be any that keep to these rules, and one draw needn't show every extreme that they name: Only the first tile_count slots of a device's list are live in a sub-epoch; in every sub-epoch some device fills all 8 slots.
All inputs are finite; a program needn't handle non-finite values.
Results may differ from a plain program's by a relative error of at most 0.00115.
The roundings to bfloat16 on the way count: a program that leaves them out, or rounds other values in their place, can miss the bound.
Values may be sent and summed in bfloat16 or wider, within the bound.
No kernel may reach another device: no remote copies, remote signals or barrier semaphores. Data moves between devices by JAX's collectives and lax.ppermute only.
A program may use at most 32 MiB of HBM per device.

v0:
```python
import jax
import jax.numpy as jnp
from jax import lax
from jax.sharding import PartitionSpec as P

LR_USER = 0.005
LR_ITEM = 0.05
LAMBDA = 64.0


def passed_along(block, axis, distance):
    devices = range(lax.axis_size(axis))
    route = [((i - distance) % len(devices), i) for i in devices]
    return lax.ppermute(block, axis, route)


def tile_grads(user_bf, block, values, rows, cols, count):
    slots = values.shape[0]
    tile_u = values.shape[1]
    tile_i = values.shape[2]
    rank = user_bf.shape[1]
    user_tiles = user_bf.reshape(-1, tile_u, rank)[rows]
    item_tiles = block.reshape(-1, tile_i, rank)[cols]
    scores = jnp.einsum("ntr,nir->nti", user_tiles, item_tiles, preferred_element_type=jnp.float32)
    live = jnp.arange(slots) < count
    errors = jnp.where(live[:, None, None], scores - values.astype(jnp.float32), 0.0).astype(
        jnp.bfloat16
    )
    user_part = jnp.einsum("nti,nir->ntr", errors, item_tiles, preferred_element_type=jnp.float32)
    item_part = jnp.einsum("nti,ntr->nir", errors, user_tiles, preferred_element_type=jnp.float32)
    row_hot = (jnp.arange(user_bf.shape[0] // tile_u)[:, None] == rows[None, :]).astype(jnp.float32)
    col_hot = (jnp.arange(block.shape[0] // tile_i)[:, None] == cols[None, :]).astype(jnp.float32)
    grad_users = jnp.einsum("bn,ntr->btr", row_hot, user_part, precision=lax.Precision.HIGHEST)
    grad_items = jnp.einsum("cn,nir->cir", col_hot, item_part, precision=lax.Precision.HIGHEST)
    return (grad_users.reshape(-1, rank), grad_items.reshape(-1, rank))


def gramian(picked, total):
    local_part = jnp.einsum("nr,ns->rs", picked, picked, preferred_element_type=jnp.float32)
    summed = lax.psum(local_part, ("stratum", "inner"))
    return summed / total


def shards(
    user_factors, item_factors, item_accum, tile_values, tile_rows, tile_cols, tile_count, neg_ids
):
    users = user_factors
    own_rows = item_factors.shape[0]
    total = lax.axis_size("stratum") * lax.axis_size("inner") * neg_ids.shape[1]
    held, accum = (
        lax.all_gather(item_factors, "inner", axis=0, tiled=True),
        lax.all_gather(item_accum, "inner", axis=0, tiled=True),
    )
    offset = lax.axis_index("inner") * own_rows
    for step in range(tile_values.shape[0]):
        block = held.astype(jnp.bfloat16)
        owned = lax.dynamic_slice_in_dim(block, offset, own_rows, 0)
        gram = gramian(owned[neg_ids[step]], total)
        grad_users, grad_items = tile_grads(
            users.astype(jnp.bfloat16),
            block,
            tile_values[step],
            tile_rows[step],
            tile_cols[step],
            tile_count[step, 0],
        )
        grad_users = grad_users + LAMBDA * jnp.dot(
            users, gram, precision=lax.Precision.HIGHEST, preferred_element_type=jnp.float32
        )
        users = users - LR_USER * grad_users
        gradient = lax.psum(grad_items, "inner")
        accum = accum + gradient * gradient
        held = held - LR_ITEM * gradient / jnp.sqrt(accum)
        held, accum = passed_along((held, accum), "stratum", -1)
    held = lax.dynamic_slice_in_dim(held, offset, own_rows, 0)
    accum = lax.dynamic_slice_in_dim(accum, offset, own_rows, 0)
    return (users, held, accum)


def solution(mesh):
    return jax.shard_map(
        shards,
        mesh=mesh,
        in_specs=(
            P(("stratum", "inner"), None),
            P(("stratum", "inner"), None),
            P(("stratum", "inner"), None),
            P(None, ("stratum", "inner"), None, None),
            P(None, ("stratum", "inner")),
            P(None, ("stratum", "inner")),
            P(None, ("stratum", "inner")),
            P(None, ("stratum", "inner")),
        ),
        out_specs=(
            P(("stratum", "inner"), None),
            P(("stratum", "inner"), None),
            P(("stratum", "inner"), None),
        ),
        check_vma=False,
    )
```

profile of v0, /device:TPU:7, one launch (start us, length us, event | category | flops | bytes accessed | tf_op | source)
XLA Modules:
  0.0 1598.1 jit_solution(3757582705303592092)
XLA Ops:
  7.2 1.3 fusion.42
  8.5 0.7 iota_compare_fusion.5
  9.2 0.7 copy-done.5
  9.9 1.1 convert_element_type.34
  11.0 108.2 %all_gather.6 = f32[768,256]{1,0:T(8,128)S(1)} all-gather(f32[16,256]{1,0:T(8,128)S(1)} %copy-done.2), channel_id=1, replica_groups=mesh['stratum'=16,'inner'=48] {'inner'}, dimensions={0}, use_global_device_ids=true | all-gather | bytes 802816 | tf_op jit(solution)/shard_map/all_gather | solution.py:51
  119.3 0.6 gather_fusion
  119.9 0.6 gather_fusion.1
  120.5 0.4 copy-done.7
  120.9 0.3 fusion.9
  121.2 0.3 fusion.46
  121.6 1.2 fusion.13
  122.8 1.1 copy.19
  124.0 0.6 copy-done.6
  124.7 94.0 %all_gather.7 = f32[768,256]{1,0:T(8,128)S(1)} all-gather(f32[16,256]{1,0:T(8,128)S(1)} %copy-done.3), channel_id=1, replica_groups=mesh['stratum'=16,'inner'=48] {'inner'}, dimensions={0}, use_global_device_ids=true | all-gather | bytes 802816 | tf_op jit(solution)/shard_map/all_gather | solution.py:52
  218.7 343.8 %all-reduce.5.cloned.1.call-done = f32[768,256]{1,0:T(8,128)} async-done(((f32[768,256]{1,0:T(8,128)}), f32[768,256]{1,0:T(8,128)}) %all-reduce.5.cloned.1.call-update) | async-done | bytes 786448 | tf_op jit(solution)/shard_map/psum | solution.py:71
  562.5 2.4 multiply_subtract_fusion.1
  564.9 35.7 %collective-permute-start = (f32[768,256]{1,0:T(8,128)}, f32[768,256]{1,0:T(8,128)S(1)}, u32[]{:S(2)}, u32[]{:S(2)}) collective-permute-start(f32[768,256]{1,0:T(8,128)} %get-tuple-element.13), channel_id=1, source_target_pairs={{48,0},{96,48},{144,96},{192,144},{240,192},{288,240},{336,288},{3... | collective-permute-start | bytes 2359304 | tf_op jit(solution)/shard_map/ppermute | solution.py:14
  600.6 0.6 gather_fusion.2
  601.1 0.9 fusion.45
  602.4 1.2 fusion.15
  603.5 16.8 %collective-permute-done = f32[768,256]{1,0:T(8,128)S(1)} collective-permute-done((f32[768,256]{1,0:T(8,128)}, f32[768,256]{1,0:T(8,128)S(1)}, u32[]{:S(2)}, u32[]{:S(2)}) %collective-permute-start) | collective-permute-done | bytes 786464 | tf_op jit(solution)/shard_map/ppermute | solution.py:14
  620.4 0.6 gather_fusion.5
  620.9 0.9 fusion.48
  621.9 0.7 iota_compare_fusion.4
  623.2 1.9 collective-permute-start.1
  625.1 0.6 gather_fusion.4
  625.7 459.0 %all-reduce.9.cloned.1.call-done = (f32[256,256]{1,0:T(8,128)}, f32[256,256]{1,0:T(8,128)}) async-done(((f32[256,256]{1,0:T(8,128)}, f32[256,256]{1,0:T(8,128)}), (f32[256,256]{1,0:T(8,128)}, f32[256,256]{1,0:T(8,128)})) %all-reduce.9.cloned.1.call-update) | async-done | bytes 524304 | tf_op jit(solution)/shard_map/psum | solution.py:40
  1084.7 2.8 fusion.43
  1087.5 1.1 copy.31
  1088.6 0.6 gather_fusion.3
  1089.1 0.4 copy-done.8
  1089.6 0.3 fusion.10
  1089.9 0.3 fusion.49
  1090.2 1.2 fusion.11
  1091.4 1.1 copy.22
  1092.6 422.7 %all-reduce.7.cloned.1.call-done = f32[768,256]{1,0:T(8,128)} async-done(((f32[768,256]{1,0:T(8,128)}), f32[768,256]{1,0:T(8,128)}) %all-reduce.7.cloned.1.call-update) | async-done | bytes 786448 | tf_op jit(solution)/shard_map/psum | solution.py:71
  1515.2 2.7 multiply_subtract_fusion
  1517.9 35.7 %collective-permute-start.2 = (f32[768,256]{1,0:T(8,128)}, f32[768,256]{1,0:T(8,128)}, u32[]{:S(2)}, u32[]{:S(2)}) collective-permute-start(f32[768,256]{1,0:T(8,128)} %get-tuple-element.11), channel_id=1, source_target_pairs={{48,0},{96,48},{144,96},{192,144},{240,192},{288,240},{336,288},{3... | collective-permute-start | bytes 2359304 | tf_op jit(solution)/shard_map/ppermute | solution.py:14
  1553.6 1.9 collective-permute-start.3
  1555.8 0.4 copy.27
  1556.2 0.6 fusion.30
  1556.8 0.3 copy-done.1
  1557.1 0.7 fusion.4
  1557.9 1.0 copy.23
  1558.9 23.0 %collective-permute-done.2 = f32[768,256]{1,0:T(8,128)} collective-permute-done((f32[768,256]{1,0:T(8,128)}, f32[768,256]{1,0:T(8,128)}, u32[]{:S(2)}, u32[]{:S(2)}) %collective-permute-start.2) | collective-permute-done | bytes 786464 | tf_op jit(solution)/shard_map/ppermute | solution.py:14
  1581.8 1.3 constant_dynamic-slice_fusion.1
  1583.2 7.1 collective-permute-done.3
  1590.3 1.3 constant_dynamic-slice_fusion
  (39 shorter events, 1.5 us)
Async XLA Ops:
  7.2 555.3 %all-reduce.5.cloned.1.call-start = ((), (), s32[]{:S(2)}) async-start(), calls=%async_computation | async-start | bytes 1572864 | tf_op jit(solution)/shard_map/psum | solution.py:71
  8.5 0.7 copy-start.4
  9.2 0.7 copy-start.5
  9.9 1.1 copy-start.2
  119.9 1.0 copy-start.7
  123.9 0.7 copy-start.6
  123.9 960.8 %all-reduce.9.cloned.1.call-start = ((), (), s32[]{:S(2)}) async-start(), calls=%async_computation.2 | async-start | bytes 1048576 | tf_op jit(solution)/shard_map/psum | solution.py:40
  124.0 0.7 copy-start.3
  564.9 55.4 %collective-permute-start = (f32[768,256]{1,0:T(8,128)}, f32[768,256]{1,0:T(8,128)S(1)}, u32[]{:S(2)}, u32[]{:S(2)}) collective-permute-start(f32[768,256]{1,0:T(8,128)} %get-tuple-element.13), channel_id=1, source_target_pairs={{48,0},{96,48},{144,96},{192,144},{240,192},{288,240},{336,288},{3... | collective-permute-start | bytes 2359304 | tf_op jit(solution)/shard_map/ppermute | solution.py:14
  620.3 2.3 copy-start
  621.9 893.4 %all-reduce.7.cloned.1.call-start = ((), (), s32[]{:S(2)}) async-start(), calls=%async_computation.1 | async-start | bytes 1572864 | tf_op jit(solution)/shard_map/psum | solution.py:71
  623.2 469.4 %collective-permute-start.1 = (f32[768,256]{1,0:T(8,128)}, f32[768,256]{1,0:T(8,128)}, u32[]{:S(2)}, u32[]{:S(2)}) collective-permute-start(f32[768,256]{1,0:T(8,128)} %get-tuple-element.14), channel_id=1, source_target_pairs={{48,0},{96,48},{144,96},{192,144},{240,192},{288,240},{336,288},{3... | collective-permute-start | bytes 2359304 | tf_op jit(solution)/shard_map/ppermute | solution.py:14
  1088.5 1.0 copy-start.8
  1517.9 63.9 %collective-permute-start.2 = (f32[768,256]{1,0:T(8,128)}, f32[768,256]{1,0:T(8,128)}, u32[]{:S(2)}, u32[]{:S(2)}) collective-permute-start(f32[768,256]{1,0:T(8,128)} %get-tuple-element.11), channel_id=1, source_target_pairs={{48,0},{96,48},{144,96},{192,144},{240,192},{288,240},{336,288},{3... | collective-permute-start | bytes 2359304 | tf_op jit(solution)/shard_map/ppermute | solution.py:14
  1553.6 36.7 %collective-permute-start.3 = (f32[768,256]{1,0:T(8,128)}, f32[768,256]{1,0:T(8,128)}, u32[]{:S(2)}, u32[]{:S(2)}) collective-permute-start(f32[768,256]{1,0:T(8,128)} %get-tuple-element.12), channel_id=1, source_target_pairs={{48,0},{96,48},{144,96},{192,144},{240,192},{288,240},{336,288},{3... | collective-permute-start | bytes 2359304 | tf_op jit(solution)/shard_map/ppermute | solution.py:14
  1556.2 1.0 copy-start.1
Sparse Core Ops, SparseCore 0:
  124.0 438.4 all-reduce.4
  622.0 462.6 all-reduce.8
  1092.7 422.5 all-reduce.6
where the time goes:
time: 1600 us
  waiting for transfers between devices  1270 us (79%)
  blocking collectives  202 us (13%)
  starting transfers between devices  75.3 us (5%)
    psum x2, waiting for transfers between devices, shards(): gradient = lax.psum(grad_items, 'inner')  766 us
    psum x1, waiting for transfers between devices, gramian(): summed = lax.psum(local_part, ('stratum', 'inner'))  459 us
    all_gather x1, blocking collectives, shards(): lax.all_gather(item_factors, 'inner', axis=0, tiled=True)  108 us
    all_gather x1, blocking collectives, shards(): lax.all_gather(item_accum, 'inner', axis=0, tiled=True)  94 us
    ppermute x4, starting transfers between devices, passed_along(): return lax.ppermute(block, axis, route)  75.1 us
    ppermute x4, waiting for transfers between devices, passed_along(): return lax.ppermute(block, axis, route)  46.8 us
  transfers between devices with their start and end apart: 7, of which 6 were waited for; matrix products, arithmetic and copies ran while one was open for 1% of the time, Pallas kernels for 0%

commit v1 on v0

v1 whole, which is shorter than its diff:
```python
import functools

import jax
import jax.numpy as jnp
from jax import lax
from jax.experimental import pallas as pl
from jax.experimental.pallas import tpu as pltpu
from jax.sharding import PartitionSpec as P

LR_USER = 0.005
LR_ITEM = 0.05
LAMBDA = 64.0

LANES = 128
F32 = jnp.float32
BF16 = jnp.bfloat16
F16 = jnp.float16

GRAD_SCALE = 2.0**-6
ROOT_SCALE = 2.0**-9
ITEM_SCALE = 2.0**12
GRAM_SCALE = 2.0**12
GRAM_LOCAL_SCALE = 2.0**10
GRAM_INNER_SCALE = 2.0**6

VMEM = pltpu.VMEM
SMEM = pltpu.SMEM


def contract(a, b, dims):
    return lax.dot_general(a, b, ((dims[:1], dims[1:]), ((), ())), preferred_element_type=F32)


def halves(x):
    return jnp.concatenate([x[:, :LANES], x[:, LANES:]], axis=0)


def widths(x):
    rows = x.shape[0] // 2
    return jnp.concatenate([x[:rows], x[rows:]], axis=1)


def picked_rows(items, ids_ref, step):
    count = ids_ref.shape[1]
    row = lax.broadcasted_iota(jnp.int32, (8, items.shape[0]), 0)
    col = lax.broadcasted_iota(jnp.int32, (8, items.shape[0]), 1)
    hot = jnp.zeros((8, items.shape[0]), F32)
    for n in range(count):
        hot = jnp.where((row == n) & (col == ids_ref[step, n]), 1.0, hot)
    return contract(hot.astype(BF16), items, (1, 0))


def gram_parts(rows):
    left, right = rows[:, :LANES], rows[:, LANES:]
    top = contract(left, rows, (0, 0))
    low = contract(right, right, (0, 0))
    return jnp.concatenate([top[:, :LANES], top[:, LANES:], low], axis=0)


def whole_gram(parts):
    a, b, c = parts[:LANES], parts[LANES : 2 * LANES], parts[2 * LANES :]
    return jnp.concatenate(
        [jnp.concatenate([a, b], axis=1), jnp.concatenate([b.T, c], axis=1)], axis=0
    )


def split(x):
    high = x.astype(BF16)
    return high, (x - high.astype(F32)).astype(BF16)


def times_gram(users, gram):
    uh, ul = split(users)
    gh, gl = split(gram)
    return contract(uh, gh, (1, 0)) + (contract(ul, gh, (1, 0)) + contract(uh, gl, (1, 0)))


def slot_grads(step, users_bf, block, values, rows, cols, count, grad_users, sums):
    slots, tile_u, tile_i = values.shape[1:]
    chunk = 16
    live = count[step, 0]
    for k in range(slots):
        row = pl.multiple_of(rows[step, k] * tile_u, tile_u)
        col = cols[step, k]
        user_tile = users_bf[pl.ds(row, tile_u), :]
        item_tile = block[pl.ds(pl.multiple_of(col * tile_i, tile_i), tile_i), :]
        scores = contract(user_tile, item_tile, (1, 1))
        err = jnp.where(k < live, scores - values[step, k].astype(F32), 0.0).astype(BF16)
        grad_users[pl.ds(row, tile_u), :] += contract(err, item_tile, (1, 0))
        part = contract(err, user_tile, (0, 0))
        at = pl.ds(col * (tile_i // chunk), tile_i // chunk)
        sums[at, 0:chunk, :] += part[:, :LANES].reshape(-1, chunk, LANES)
        sums[at, chunk : 2 * chunk, :] += part[:, LANES:].reshape(-1, chunk, LANES)


def first_kernel(block, users, own, values, rows, cols, count, ids, sums, users_out, users_bf, grad_users):
    chunks = sums.shape[0]
    users_bf[...] = users[...].astype(BF16)
    grad_users[...] = jnp.zeros_like(grad_users)
    sums[...] = jnp.zeros_like(sums)
    slot_grads(0, users_bf, block, values, rows, cols, count, grad_users, sums)
    sums[:, 0:32, :] = sums[:, 0:32, :] * GRAD_SCALE
    picks = picked_rows(own[...].astype(BF16), ids, 0).astype(BF16)
    sums[:, 32:, :] = (gram_parts(picks) * GRAM_LOCAL_SCALE).reshape(chunks, -1, LANES)
    users_out[...] = users[...] - LR_USER * grad_users[...]


def update(held, accum, gradient):
    accum = accum + gradient * gradient
    return held - LR_ITEM * gradient / jnp.sqrt(accum), accum


def item_kernel(total, held, accum, out):
    rows = held.shape[0]
    gradient = widths(total[...] * (1.0 / GRAD_SCALE))
    out[0:rows, :], out[rows:, :] = update(held[...], accum[...], gradient)


def meet_kernel(state, ids, out):
    rows = state.shape[0] // 2
    picks = picked_rows(state[0:rows, :].astype(BF16), ids, 1)
    out[...] = halves(picks[0:4, :])


def gather_kernel(total, negs, met, state, gram_part, out):
    chunks = out.shape[0]
    piece = gram_part.shape[0]
    rows = state.shape[0] // 2
    items = halves(state[0:rows, :].astype(BF16).astype(F32)) * ITEM_SCALE
    out[:, 0:32, :] = jnp.broadcast_to(items[None], (chunks, 32, LANES))
    full = gram_part[...] * (GRAM_SCALE / GRAM_LOCAL_SCALE / total)
    out[:, 32 : 32 + piece, :] = jnp.broadcast_to(full[None], (chunks, piece, LANES))
    left = met[:, 0:negs, :].reshape(-1, LANES)
    right = met[:, negs:, :].reshape(-1, LANES)
    picks = jnp.concatenate([left, right], axis=1).astype(BF16)
    out[:, 32 + piece :, :] = (gram_parts(picks) * GRAM_INNER_SCALE).reshape(chunks, piece, LANES)


def second_kernel(
    total, got, users, mid, values, rows, cols, count, sums, users_out, mid_out, users_bf, grad_users, block
):
    chunks = sums.shape[0]
    piece = sums.shape[1] - 32
    left = (got[:, 0:16, :] * (1.0 / ITEM_SCALE)).astype(BF16).reshape(-1, LANES)
    right = (got[:, 16:32, :] * (1.0 / ITEM_SCALE)).astype(BF16).reshape(-1, LANES)
    block[:, :LANES] = left
    block[:, LANES:] = right
    gram = whole_gram(got[:, 32 : 32 + piece, :].reshape(-1, LANES) * (1.0 / GRAM_SCALE))
    now = mid[...] - (LR_USER * LAMBDA) * times_gram(users[...], gram)
    mid_out[...] = now
    users_bf[...] = now.astype(BF16)
    grad_users[...] = jnp.zeros_like(grad_users)
    sums[...] = jnp.zeros_like(sums)
    slot_grads(1, users_bf, block, values, rows, cols, count, grad_users, sums)
    raw = sums[:, 0:32, :]
    root = jnp.sqrt(jnp.abs(raw)) * ROOT_SCALE
    sums[:, 0:32, :] = jnp.where(raw < 0.0, -root, root)
    full = jnp.sum(got[:, 32 + piece :, :], axis=0) * (GRAM_SCALE / GRAM_INNER_SCALE / total)
    sums[:, 32:, :] = jnp.broadcast_to(full[None], (chunks, piece, LANES))
    users_out[...] = now - LR_USER * grad_users[...]


def last_items_kernel(total, state, out):
    rows = state.shape[0] // 2
    out[0:rows, :], out[rows:, :] = update(state[0:rows, :], state[rows:, :], widths(total[...]))


def last_users_kernel(got, users, mid, out):
    gram = whole_gram(got[...].reshape(-1, LANES) * (1.0 / GRAM_SCALE))
    out[...] = users[...] - (LR_USER * LAMBDA) * times_gram(mid[...], gram)


def call(kernel, out_shape, specs, *args, scratch=()):
    return pl.pallas_call(
        kernel,
        out_shape=out_shape,
        in_specs=specs,
        out_specs=jax.tree.map(lambda _: pl.BlockSpec(memory_space=VMEM), out_shape),
        scratch_shapes=scratch,
        compiler_params=pltpu.CompilerParams(vmem_limit_bytes=40 * 2**20),
    )(*args)


def exchanged(x, axis):
    return lax.all_to_all(x, axis, 0, 0, tiled=True)


def shards(
    user_factors, item_factors, item_accum, tile_values, tile_rows, tile_cols, tile_count, neg_ids
):
    strata = lax.axis_size("stratum")
    inners = lax.axis_size("inner")
    own, rank = item_factors.shape
    negs = neg_ids.shape[1]
    total = float(strata * inners * negs)
    piece = 3 * LANES // inners
    users_shape = jax.ShapeDtypeStruct(user_factors.shape, F32)
    state_shape = jax.ShapeDtypeStruct((2 * own, rank), F32)
    users_scratch = [pltpu.VMEM(user_factors.shape, BF16), pltpu.VMEM(user_factors.shape, F32)]
    sums_shape = jax.ShapeDtypeStruct((inners, 2 * own + piece, LANES), F32)
    vm = pl.BlockSpec(memory_space=VMEM)
    sm = pl.BlockSpec(memory_space=SMEM)
    onward = [((s + 1) % strata, s) for s in range(strata)]

    held_bf = jnp.broadcast_to(item_factors.astype(BF16)[None], (inners, own, rank))
    block = exchanged(held_bf, "inner").reshape(inners * own, rank)
    sums, mid = call(
        first_kernel,
        (sums_shape, users_shape),
        [vm, vm, vm, vm, sm, sm, sm, sm],
        block, user_factors, item_factors, tile_values, tile_rows, tile_cols, tile_count, neg_ids,
        scratch=users_scratch,
    )
    got = jnp.sum(exchanged(sums.astype(F16), "inner").astype(F32), axis=0)
    state = call(item_kernel, state_shape, [vm, vm, vm], got[: 2 * own], item_factors, item_accum)
    state = lax.ppermute(state, "stratum", onward)
    picks = call(meet_kernel, jax.ShapeDtypeStruct((2 * negs, LANES), F32), [vm, sm], state, neg_ids)
    sent = jnp.concatenate([got[2 * own :], picks], axis=0)
    met = exchanged(jnp.broadcast_to(sent[None], (strata,) + sent.shape), "stratum")
    payload = call(
        functools.partial(gather_kernel, total, negs),
        jax.ShapeDtypeStruct((inners, 2 * own + 2 * piece, LANES), F32),
        [vm, vm, vm],
        met[:, piece:], state, jnp.sum(met[:, :piece], axis=0),
    )
    got = exchanged(payload.astype(F16), "inner").astype(F32)
    sums, users, mid = call(
        functools.partial(second_kernel, total),
        (sums_shape, users_shape, users_shape),
        [vm, vm, vm, vm, sm, sm, sm],
        got, user_factors, mid, tile_values, tile_rows, tile_cols, tile_count,
        scratch=users_scratch + [pltpu.VMEM((inners * own, rank), BF16)],
    )
    got = exchanged(sums.astype(F16), "inner").astype(F32)
    root = got[:, : 2 * own]
    gradient = jnp.sum(root * jnp.abs(root), axis=0) * (ROOT_SCALE**-2)
    state = call(last_items_kernel, state_shape, [vm, vm], gradient, state)
    state = lax.ppermute(state, "stratum", onward)
    users = call(last_users_kernel, users_shape, [vm, vm, vm], got[:, 2 * own :], users, mid)
    return (users, state[:own], state[own:])


def solution(mesh):
    devices = P(("stratum", "inner"), None)
    slots = P(None, ("stratum", "inner"))
    return jax.shard_map(
        shards,
        mesh=mesh,
        in_specs=(
            devices,
            devices,
            devices,
            P(None, ("stratum", "inner"), None, None),
            slots,
            slots,
            slots,
            slots,
        ),
        out_specs=(devices, devices, devices),
        check_vma=False,
    )
```

time: 1600 us -> 177 us (0.11)
  waiting for transfers between devices: 1270 us -> 31.1 us
  blocking collectives: 202 us -> 106 us
  starting transfers between devices: 75.3 us -> 28.1 us
    psum x3 -> x0, waiting for transfers between devices: 1230 us -> none  [the longest x2 766 us: shards(): gradient = lax.psum(grad_items, 'inner')]
    all_gather x2 -> x0, blocking collectives: 202 us -> none  [the longest x1 108 us: shards(): lax.all_gather(item_factors, 'inner', axis=0, tiled=True)]
    all_to_all x0 -> x4, blocking collectives: none -> 106 us  [exchanged(): return lax.all_to_all(x, axis, 0, 0, tiled=True)]
    ppermute x4 -> x2, starting transfers between devices: 75.1 us -> 9.55 us  [shards(): state = lax.ppermute(state, 'stratum', onward)]
    ppermute x4 -> x2, waiting for transfers between devices: 46.8 us -> 11.7 us  [shards(): state = lax.ppermute(state, 'stratum', onward)]
    all_to_all x0 -> x1, waiting for transfers between devices: none -> 19.4 us  [exchanged(): return lax.all_to_all(x, axis, 0, 0, tiled=True)]
    all_to_all x0 -> x1, starting transfers between devices: none -> 18.6 us  [exchanged(): return lax.all_to_all(x, axis, 0, 0, tiled=True)]
  transfers between devices with their start and end apart: 7 -> 3, of which waited for: 6 -> 3; matrix products, arithmetic and copies ran while one was open for 1% -> 0% of each run, Pallas kernels for 0% -> 1%
where the time goes in v1:
time: 177 us
  blocking collectives  106 us (60%)
  waiting for transfers between devices  31.1 us (18%)
  starting transfers between devices  28.1 us (16%)
  Pallas kernels  7.68 us (4%)
    all_to_all x4, blocking collectives, exchanged(): return lax.all_to_all(x, axis, 0, 0, tiled=True)  106 us
    all_to_all x1, waiting for transfers between devices, exchanged(): return lax.all_to_all(x, axis, 0, 0, tiled=True)  19.4 us
    all_to_all x1, starting transfers between devices, exchanged(): return lax.all_to_all(x, axis, 0, 0, tiled=True)  18.6 us
    ppermute x2, waiting for transfers between devices, shards(): state = lax.ppermute(state, 'stratum', onward)  11.7 us
    ppermute x2, starting transfers between devices, shards(): state = lax.ppermute(state, 'stratum', onward)  9.55 us
    pallas_call x7, Pallas kernels, call(): pl.pallas_call(kernel, out_shape=out_shape, in_specs=specs, out_specs=jax...  7.68 us
  transfers between devices with their start and end apart: 3, of which 3 were waited for; matrix products, arithmetic and copies ran while one was open for 0% of the time, Pallas kernels for 1%

profile of v1, /device:TPU:7, one launch (start us, length us, event | category | flops | bytes accessed | tf_op | source)
XLA Modules:
  0.0 176.5 jit_solution(16647329655639462417)
XLA Ops:
  0.6 0.0 copy-start.2
  0.6 0.0 copy-start.7
  0.7 0.0 copy-start.6
  0.7 0.0 copy-start.5
  0.7 0.0 copy-start.4
  0.7 0.0 copy-start.1
  0.7 0.0 copy-start
  0.7 0.8 convert_element_type.21
  1.5 0.8 broadcast_in_dim.4
  2.3 18.6 %all-to-all-start = ((bf16[48,16,256]{2,1,0:T(8,128)(2,1)}), bf16[48,16,256]{2,1,0:T(8,128)(2,1)S(1)}, u32[]{:S(2)}, u32[]{:S(2)}) async-start(bf16[48,16,256]{2,1,0:T(8,128)(2,1)} %broadcast_in_dim.4), calls=%async_computation | async-start | bytes 786432 | tf_op jit(solution)/shard_map/all_to_all | solution.py:185
  20.9 0.0 copy-done.7
  20.9 0.1 copy.11.count
  21.0 19.4 %all-to-all-done = bf16[48,16,256]{2,1,0:T(8,128)(2,1)S(1)} async-done(((bf16[48,16,256]{2,1,0:T(8,128)(2,1)}), bf16[48,16,256]{2,1,0:T(8,128)(2,1)S(1)}, u32[]{:S(2)}, u32[]{:S(2)}) %all-to-all-start) | async-done | bytes 393248 | tf_op jit(solution)/shard_map/all_to_all | solution.py:185
  40.4 0.0 copy-done.2
  40.4 0.0 copy-done.6
  40.4 0.0 copy-done.5
  40.4 0.0 copy-done.4
  40.5 0.0 copy-done.1
  40.5 0.0 copy-done
  40.5 2.2 %shard_map.103 = (f32[48,40,128]{2,1,0:T(8,128)S(1)}, f32[512,256]{1,0:T(8,128)S(1)}) custom-call(bf16[768,256]{1,0:T(8,128)(2,1)S(1)} %bitcast.1, f32[512,256]{1,0:T(8,128)S(1)} %copy-done, f32[16,256]{1,0:T(8,128)S(1)} %copy-done.2, bf16[2,8,128,128]{3,2,1,0:T(8,128)(2,1)S(1)} %copy-done.1, s32[2,8]{1,0:T(2,128)S(1)} %copy-done.4, s32[2,8]{1,0:T(2,128)S(1)} %copy-done.5, ...), custom_call_target="tpu_custom_call" | custom-call | tf_op jit(solution)/shard_map/pallas_call | solution.py:174
  42.6 0.0 copy-start.3
  42.7 0.1 convert_element_type.22
  42.7 28.5 %all_to_all.25 = f16[48,40,128]{2,1,0:T(8,128)(2,1)S(1)} all-to-all(f16[48,40,128]{2,1,0:T(8,128)(2,1)S(1)} %convert_element_type.22), channel_id=1, replica_groups=mesh['stratum'=16,'inner'=48] {'inner'}, dimensions={0} | all-to-all | bytes 983040 | tf_op jit(solution)/shard_map/all_to_all | solution.py:185
  71.3 0.1 convert_reduce_fusion
  71.4 0.0 copy-done.3
  71.4 4.8 %collective-permute-start = (f32[32,256]{1,0:T(8,128)S(1)}, f32[32,256]{1,0:T(8,128)S(1)}, u32[]{:S(2)}, u32[]{:S(2)}) collective-permute-start(f32[32,256]{1,0:T(8,128)S(1)} %shard_map.104), channel_id=1, source_target_pairs={{48,0},{96,48},{144,96},{192,144},{240,192},{288,240},{336,288},{3... | collective-permute-start | bytes 98312 | tf_op jit(solution)/shard_map/ppermute | solution.py:216
  76.2 6.5 %collective-permute-done.state = f32[32,256]{1,0:T(8,128)S(1)} collective-permute-done((f32[32,256]{1,0:T(8,128)S(1)}, f32[32,256]{1,0:T(8,128)S(1)}, u32[]{:S(2)}, u32[]{:S(2)}) %collective-permute-start) | collective-permute-done | bytes 32800 | tf_op jit(solution)/shard_map/ppermute | solution.py:216
  82.7 0.7 shard_map.105
  83.3 15.3 %all_to_all.26 = f32[16,16,128]{2,1,0:T(8,128)S(1)} all-to-all(f32[16,16,128]{2,1,0:T(8,128)S(1)} %broadcast_in_dim.5), channel_id=1, replica_groups=mesh['stratum'=16,'inner'=48] {'stratum'}, dimensions={0} | all-to-all | bytes 262144 | tf_op jit(solution)/shard_map/all_to_all | solution.py:185
  98.6 0.2 shard_map.106
  98.9 0.1 convert_element_type.24
  99.0 33.1 %all_to_all.27 = f16[48,48,128]{2,1,0:T(8,128)(2,1)S(1)} all-to-all(f16[48,48,128]{2,1,0:T(8,128)(2,1)S(1)} %convert_element_type.24), channel_id=1, replica_groups=mesh['stratum'=16,'inner'=48] {'inner'}, dimensions={0} | all-to-all | bytes 1179648 | tf_op jit(solution)/shard_map/all_to_all | solution.py:185
  132.1 0.1 convert_element_type.25.got
  132.1 3.4 %shard_map.107 = (f32[48,40,128]{2,1,0:T(8,128)S(1)}, f32[512,256]{1,0:T(8,128)S(1)}, f32[512,256]{1,0:T(8,128)S(1)}) custom-call(f32[48,48,128]{2,1,0:T(8,128)S(1)} %convert_element_type.25.got, f32[512,256]{1,0:T(8,128)S(1)} %copy-done, f32[512,256]{1,0:T(8,128)S(1)} %get-tuple-element.9.mid, bf16[2,8,128,128]{3,2,1,0:T(8,128)(2,1)S(1)} %copy-done.1, ...), custom_call_target="tpu_custom_call" | custom-call | tf_op jit(solution)/shard_map/pallas_call | solution.py:174
  135.5 0.1 convert_element_type.26
  135.6 28.9 %all_to_all.28 = f16[48,40,128]{2,1,0:T(8,128)(2,1)S(1)} all-to-all(f16[48,40,128]{2,1,0:T(8,128)(2,1)S(1)} %convert_element_type.26), channel_id=1, replica_groups=mesh['stratum'=16,'inner'=48] {'inner'}, dimensions={0} | all-to-all | bytes 983040 | tf_op jit(solution)/shard_map/all_to_all | solution.py:185
  164.5 0.1 convert_element_type.27
  164.5 0.1 fusion
  164.7 4.8 %collective-permute-start.1 = (f32[32,256]{1,0:T(8,128)S(1)}, f32[32,256]{1,0:T(8,128)S(1)}, u32[]{:S(2)}, u32[]{:S(2)}) collective-permute-start(f32[32,256]{1,0:T(8,128)S(1)} %shard_map.109), channel_id=1, source_target_pairs={{48,0},{96,48},{144,96},{192,144},{240,192},{288,240},{336,288},{3... | collective-permute-start | bytes 98312 | tf_op jit(solution)/shard_map/ppermute | solution.py:238
  169.5 1.2 shard_map.108
  170.7 5.2 %collective-permute-done.1 = f32[32,256]{1,0:T(8,128)S(1)} collective-permute-done((f32[32,256]{1,0:T(8,128)S(1)}, f32[32,256]{1,0:T(8,128)S(1)}, u32[]{:S(2)}, u32[]{:S(2)}) %collective-permute-start.1) | collective-permute-done | bytes 32800 | tf_op jit(solution)/shard_map/ppermute | solution.py:238
  175.9 0.6 fusion.1
  (9 shorter events, 0.1 us)
Async XLA Ops:
  0.6 39.8 %copy-start.2 = (f32[16,256]{1,0:T(8,128)S(1)}, f32[16,256]{1,0:T(8,128)}, u32[]{:S(2)}) copy-start(f32[16,256]{1,0:T(8,128)} %held.1) | copy-start | bytes 49156
  0.6 20.2 %copy-start.7 = (s32[2,1]{0,1:T(1,128)S(1)}, s32[2,1]{0,1:T(1,128)}, u32[]{:S(2)}) copy-start(s32[2,1]{0,1:T(1,128)} %param.14) | copy-start | bytes 28
  0.7 39.8 %copy-start.6 = (s32[2,4]{1,0:T(2,128)S(1)}, s32[2,4]{1,0:T(2,128)}, u32[]{:S(2)}) copy-start(s32[2,4]{1,0:T(2,128)} %ids.3) | copy-start | bytes 100
  0.7 39.8 %copy-start.5 = (s32[2,8]{1,0:T(2,128)S(1)}, s32[2,8]{1,0:T(2,128)}, u32[]{:S(2)}) copy-start(s32[2,8]{1,0:T(2,128)} %cols.3) | copy-start | bytes 196
  0.7 39.8 %copy-start.4 = (s32[2,8]{1,0:T(2,128)S(1)}, s32[2,8]{1,0:T(2,128)}, u32[]{:S(2)}) copy-start(s32[2,8]{1,0:T(2,128)} %rows.3) | copy-start | bytes 196
  0.7 39.8 %copy-start.1 = (bf16[2,8,128,128]{3,2,1,0:T(8,128)(2,1)S(1)}, bf16[2,8,128,128]{3,2,1,0:T(8,128)(2,1)}, u32[]{:S(2)}) copy-start(bf16[2,8,128,128]{3,2,1,0:T(8,128)(2,1)} %values.3) | copy-start | bytes 1572868
  0.7 39.8 %copy-start = (f32[512,256]{1,0:T(8,128)S(1)}, f32[512,256]{1,0:T(8,128)}, u32[]{:S(2)}) copy-start(f32[512,256]{1,0:T(8,128)} %users.3) | copy-start | bytes 1572868
  2.3 38.1 %all-to-all-start = ((bf16[48,16,256]{2,1,0:T(8,128)(2,1)}), bf16[48,16,256]{2,1,0:T(8,128)(2,1)S(1)}, u32[]{:S(2)}, u32[]{:S(2)}) async-start(bf16[48,16,256]{2,1,0:T(8,128)(2,1)} %broadcast_in_dim.4), calls=%async_computation | async-start | bytes 786432 | tf_op jit(solution)/shard_map/all_to_all | solution.py:185
  42.6 28.7 %copy-start.3 = (f32[16,256]{1,0:T(8,128)S(1)}, f32[16,256]{1,0:T(8,128)}, u32[]{:S(2)}) copy-start(f32[16,256]{1,0:T(8,128)} %accum.1) | copy-start | bytes 49156
  71.4 11.3 %collective-permute-start = (f32[32,256]{1,0:T(8,128)S(1)}, f32[32,256]{1,0:T(8,128)S(1)}, u32[]{:S(2)}, u32[]{:S(2)}) collective-permute-start(f32[32,256]{1,0:T(8,128)S(1)} %shard_map.104), channel_id=1, source_target_pairs={{48,0},{96,48},{144,96},{192,144},{240,192},{288,240},{336,288},{3... | collective-permute-start | bytes 98312 | tf_op jit(solution)/shard_map/ppermute | solution.py:216
  164.7 11.3 %collective-permute-start.1 = (f32[32,256]{1,0:T(8,128)S(1)}, f32[32,256]{1,0:T(8,128)S(1)}, u32[]{:S(2)}, u32[]{:S(2)}) collective-permute-start(f32[32,256]{1,0:T(8,128)S(1)} %shard_map.109), channel_id=1, source_target_pairs={{48,0},{96,48},{144,96},{192,144},{240,192},{288,240},{336,288},{3... | collective-permute-start | bytes 98312 | tf_op jit(solution)/shard_map/ppermute | solution.py:238

commit v2 on v1

--- a/solution.py
+++ b/solution.py
@@ -21,6 +21,7 @@
 ITEM_SCALE = 2.0**12
 GRAM_SCALE = 2.0**12
 GRAM_LOCAL_SCALE = 2.0**10
+GRAM_STRATUM_SCALE = 2.0**5
 GRAM_INNER_SCALE = 2.0**6
 
 VMEM = pltpu.VMEM
@@ -50,10 +51,9 @@
     return contract(hot.astype(BF16), items, (1, 0))
 
 
-def gram_parts(rows):
-    left, right = rows[:, :LANES], rows[:, LANES:]
-    top = contract(left, rows, (0, 0))
-    low = contract(right, right, (0, 0))
+def gram_parts(weighed, rows):
+    top = contract(weighed[:, :LANES], rows, (0, 0))
+    low = contract(weighed[:, LANES:], rows[:, LANES:], (0, 0))
     return jnp.concatenate([top[:, :LANES], top[:, LANES:], low], axis=0)
 
 
@@ -101,7 +101,7 @@
     slot_grads(0, users_bf, block, values, rows, cols, count, grad_users, sums)
     sums[:, 0:32, :] = sums[:, 0:32, :] * GRAD_SCALE
     picks = picked_rows(own[...].astype(BF16), ids, 0).astype(BF16)
-    sums[:, 32:, :] = (gram_parts(picks) * GRAM_LOCAL_SCALE).reshape(chunks, -1, LANES)
+    sums[:, 32:, :] = (gram_parts(picks, picks) * GRAM_LOCAL_SCALE).reshape(chunks, -1, LANES)
     users_out[...] = users[...] - LR_USER * grad_users[...]
 
 
@@ -110,30 +110,52 @@
     return held - LR_ITEM * gradient / jnp.sqrt(accum), accum
 
 
-def item_kernel(total, held, accum, out):
+def pick_counts(ids_ref, step):
+    row = lax.broadcasted_iota(jnp.int32, (8, LANES), 0)
+    lane = lax.broadcasted_iota(jnp.int32, (8, LANES), 1)
+    row = jnp.where(lane < LANES // 2, row, row + 8)
+    counts = jnp.zeros((8, LANES), F32)
+    for n in range(ids_ref.shape[1]):
+        counts = counts + jnp.where(row == ids_ref[step, n], 1.0, 0.0)
+    return counts
+
+
+def item_kernel(got, held, accum, ids, state, out):
     rows = held.shape[0]
-    gradient = widths(total[...] * (1.0 / GRAD_SCALE))
-    out[0:rows, :], out[rows:, :] = update(held[...], accum[...], gradient)
-
-
-def meet_kernel(state, ids, out):
-    rows = state.shape[0] // 2
-    picks = picked_rows(state[0:rows, :].astype(BF16), ids, 1)
-    out[...] = halves(picks[0:4, :])
-
-
-def gather_kernel(total, negs, met, state, gram_part, out):
+    piece = got.shape[1] - 2 * rows
+    total = jnp.sum(got[...], axis=0)
+    gradient = widths(total[0 : 2 * rows] * (1.0 / GRAD_SCALE))
+    new, state[rows:, :] = update(held[...], accum[...], gradient)
+    state[0:rows, :] = new
+    strata = out.shape[0]
+    sent = jnp.concatenate(
+        [
+            halves(new.astype(BF16).astype(F32)) * ITEM_SCALE,
+            pick_counts(ids, 1),
+            total[2 * rows :] * (GRAM_STRATUM_SCALE / GRAM_LOCAL_SCALE),
+        ],
+        axis=0,
+    )
+    out[...] = jnp.broadcast_to(sent[None], (strata, 2 * rows + 8 + piece, LANES))
+
+
+def gather_kernel(total, met, out):
     chunks = out.shape[0]
-    piece = gram_part.shape[0]
-    rows = state.shape[0] // 2
-    items = halves(state[0:rows, :].astype(BF16).astype(F32)) * ITEM_SCALE
-    out[:, 0:32, :] = jnp.broadcast_to(items[None], (chunks, 32, LANES))
-    full = gram_part[...] * (GRAM_SCALE / GRAM_LOCAL_SCALE / total)
+    strata = met.shape[0]
+    piece = met.shape[1] - 40
+    after = lax.rem(lax.axis_index("stratum") + 1, strata)
+    items = met[pl.ds(after, 1), 0:32, :]
+    out[:, 0:32, :] = jnp.broadcast_to(items, (chunks, 32, LANES))
+    full = jnp.sum(met[:, 40:, :], axis=0) * (GRAM_SCALE / GRAM_STRATUM_SCALE / total)
     out[:, 32 : 32 + piece, :] = jnp.broadcast_to(full[None], (chunks, piece, LANES))
-    left = met[:, 0:negs, :].reshape(-1, LANES)
-    right = met[:, negs:, :].reshape(-1, LANES)
-    picks = jnp.concatenate([left, right], axis=1).astype(BF16)
-    out[:, 32 + piece :, :] = (gram_parts(picks) * GRAM_INNER_SCALE).reshape(chunks, piece, LANES)
+    counts = jnp.concatenate([met[-1:, 32:40, :], met[:-1, 32:40, :]], axis=0)
+    counts = jnp.concatenate([counts[:, :, 0:1], counts[:, :, 64:65]], axis=1)
+    rows = [met[:, 0:16, :] * (1.0 / ITEM_SCALE), met[:, 16:32, :] * (1.0 / ITEM_SCALE)]
+    weighed = jnp.concatenate([(r * counts).reshape(-1, LANES) for r in rows], axis=1)
+    plain = jnp.concatenate([r.reshape(-1, LANES) for r in rows], axis=1).astype(BF16)
+    high, low = split(weighed)
+    parts = gram_parts(jnp.concatenate([high, low], axis=0), jnp.concatenate([plain, plain], axis=0))
+    out[:, 32 + piece :, :] = (parts * GRAM_INNER_SCALE).reshape(chunks, piece, LANES)
 
 
 def second_kernel(
@@ -211,19 +233,23 @@
         block, user_factors, item_factors, tile_values, tile_rows, tile_cols, tile_count, neg_ids,
         scratch=users_scratch,
     )
-    got = jnp.sum(exchanged(sums.astype(F16), "inner").astype(F32), axis=0)
-    state = call(item_kernel, state_shape, [vm, vm, vm], got[: 2 * own], item_factors, item_accum)
+    got = exchanged(sums.astype(F16), "inner").astype(F32)
+    state, sent = call(
+        item_kernel,
+        (state_shape, jax.ShapeDtypeStruct((strata, 2 * own + 8 + piece, LANES), F32)),
+        [vm, vm, vm, sm],
+        got, item_factors, item_accum, neg_ids,
+    )
+    met = exchanged(sent.astype(F16), "stratum").astype(F32)
+    payload = call(
+        functools.partial(gather_kernel, total),
+        jax.ShapeDtypeStruct((inners, 2 * own + 2 * piece, LANES), F32),
+        [vm],
+        met,
+    ).astype(F16)
+    payload, state = lax.optimization_barrier((payload, state))
     state = lax.ppermute(state, "stratum", onward)
-    picks = call(meet_kernel, jax.ShapeDtypeStruct((2 * negs, LANES), F32), [vm, sm], state, neg_ids)
-    sent = jnp.concatenate([got[2 * own :], picks], axis=0)
-    met = exchanged(jnp.broadcast_to(sent[None], (strata,) + sent.shape), "stratum")
-    payload = call(
-        functools.partial(gather_kernel, total, negs),
-        jax.ShapeDtypeStruct((inners, 2 * own + 2 * piece, LANES), F32),
-        [vm, vm, vm],
-        met[:, piece:], state, jnp.sum(met[:, :piece], axis=0),
-    )
-    got = exchanged(payload.astype(F16), "inner").astype(F32)
+    got = exchanged(payload, "inner").astype(F32)
     sums, users, mid = call(
         functools.partial(second_kernel, total),
         (sums_shape, users_shape, users_shape),

time: 177 us -> 171 us (0.966)
  blocking collectives: 106 us -> 80.6 us
  waiting for transfers between devices: 31.1 us -> 43.4 us
  starting transfers between devices: 28.1 us -> 33.4 us
    all_to_all x4 -> x3, blocking collectives: 106 us -> 80.6 us  [exchanged(): return lax.all_to_all(x, axis, 0, 0, tiled=True)]
    all_to_all x1 -> x2, waiting for transfers between devices: 19.4 us -> 38.5 us  [exchanged(): return lax.all_to_all(x, axis, 0, 0, tiled=True)]
    ppermute x2, waiting for transfers between devices: 11.7 us -> 4.83 us  [shards(): state = lax.ppermute(state, 'stratum', onward)]
    all_to_all x1 -> x2, starting transfers between devices: 18.6 us -> 25.2 us  [exchanged(): return lax.all_to_all(x, axis, 0, 0, tiled=True)]
    pallas_call x7 -> x6, Pallas kernels: 7.68 us -> 7.86 us  [call(): pl.pallas_call(kernel, out_shape=out_shape, in_specs=specs, out_specs=jax...]
  transfers between devices with their start and end apart: 3 -> 4, of which waited for: 3 -> 3; matrix products, arithmetic and copies ran while one was open for 0% -> 0% of each run, Pallas kernels for 1% -> 1%
where the time goes in v2:
time: 171 us; the launch traced here: 170 us
  blocking collectives  80.6 us (47%)
  waiting for transfers between devices  43.4 us (25%)
  starting transfers between devices  33.4 us (20%)
  Pallas kernels  7.86 us (5%)
  other arithmetic  2.18 us (1%)
    all_to_all x3, blocking collectives, exchanged(): return lax.all_to_all(x, axis, 0, 0, tiled=True)  80.6 us
    all_to_all x2, waiting for transfers between devices, exchanged(): return lax.all_to_all(x, axis, 0, 0, tiled=True)  38.5 us
    all_to_all x2, starting transfers between devices, exchanged(): return lax.all_to_all(x, axis, 0, 0, tiled=True)  25.2 us
    ppermute x2, starting transfers between devices, shards(): state = lax.ppermute(state, 'stratum', onward)  8.2 us
    pallas_call x6, Pallas kernels, call(): pl.pallas_call(kernel, out_shape=out_shape, in_specs=specs, out_specs=jax...  7.86 us
    ppermute x2, waiting for transfers between devices, shards(): state = lax.ppermute(state, 'stratum', onward)  4.83 us
  transfers between devices with their start and end apart: 4, of which 3 were waited for; matrix products, arithmetic and copies ran while one was open for 0% of the time, Pallas kernels for 1%

profile of v2, /device:TPU:7, one launch (start us, length us, event | category | flops | bytes accessed | tf_op | source)
XLA Modules:
  0.0 169.8 jit_solution(10972234885505266889)
XLA Ops:
  0.6 0.0 copy-start.2
  0.6 0.0 copy-start.7
  0.7 0.0 copy-start.4
  0.7 0.0 copy-start.6
  0.7 0.0 copy-start.5
  0.7 0.0 copy-start.1
  0.7 0.0 copy-start
  0.7 0.8 convert_element_type.27
  1.5 0.8 broadcast_in_dim.2
  2.3 18.6 %all-to-all-start = ((bf16[48,16,256]{2,1,0:T(8,128)(2,1)}), bf16[48,16,256]{2,1,0:T(8,128)(2,1)S(1)}, u32[]{:S(2)}, u32[]{:S(2)}) async-start(bf16[48,16,256]{2,1,0:T(8,128)(2,1)} %broadcast_in_dim.2), calls=%async_computation | async-start | bytes 786432 | tf_op jit(solution)/shard_map/all_to_all | solution.py:207
  20.9 0.0 copy-done.7
  20.9 0.1 copy.11.count
  21.0 19.4 %all-to-all-done = bf16[48,16,256]{2,1,0:T(8,128)(2,1)S(1)} async-done(((bf16[48,16,256]{2,1,0:T(8,128)(2,1)}), bf16[48,16,256]{2,1,0:T(8,128)(2,1)S(1)}, u32[]{:S(2)}, u32[]{:S(2)}) %all-to-all-start) | async-done | bytes 393248 | tf_op jit(solution)/shard_map/all_to_all | solution.py:207
  40.4 0.0 copy-done.2
  40.4 0.0 copy-done.4
  40.4 0.0 copy-done.6
  40.4 0.0 copy-done.5
  40.5 0.0 copy-done.1
  40.5 0.0 copy-done
  40.5 2.2 %shard_map.103 = (f32[48,40,128]{2,1,0:T(8,128)S(1)}, f32[512,256]{1,0:T(8,128)S(1)}) custom-call(bf16[768,256]{1,0:T(8,128)(2,1)S(1)} %bitcast.1, f32[512,256]{1,0:T(8,128)S(1)} %copy-done, f32[16,256]{1,0:T(8,128)S(1)} %copy-done.2, bf16[2,8,128,128]{3,2,1,0:T(8,128)(2,1)S(1)} %copy-done.1, s32[2,8]{1,0:T(2,128)S(1)} %copy-done.5, s32[2,8]{1,0:T(2,128)S(1)} %copy-done.6, ...), custom_call_target="tpu_custom_call" | custom-call | tf_op jit(solution)/shard_map/pallas_call | solution.py:196
  42.6 0.1 convert_element_type.28
  42.7 0.0 copy-start.3
  42.7 28.5 %all_to_all.25 = f16[48,40,128]{2,1,0:T(8,128)(2,1)S(1)} all-to-all(f16[48,40,128]{2,1,0:T(8,128)(2,1)S(1)} %convert_element_type.28), channel_id=1, replica_groups=mesh['stratum'=16,'inner'=48] {'inner'}, dimensions={0} | all-to-all | bytes 983040 | tf_op jit(solution)/shard_map/all_to_all | solution.py:207
  71.3 0.1 convert_element_type.29.got
  71.3 0.0 copy-done.3
  71.3 0.7 shard_map.104
  72.0 19.5 %all_to_all.26 = f16[16,48,128]{2,1,0:T(8,128)(2,1)S(1)} all-to-all(f16[16,48,128]{2,1,0:T(8,128)(2,1)S(1)} %convert_element_type.30), channel_id=1, replica_groups=mesh['stratum'=16,'inner'=48] {'stratum'}, dimensions={0} | all-to-all | bytes 393216 | tf_op jit(solution)/shard_map/all_to_all | solution.py:207
  91.6 0.4 shard_map.105
  92.0 0.1 convert_element_type.32
  92.1 32.5 %all_to_all.27 = f16[48,48,128]{2,1,0:T(8,128)(2,1)S(1)} all-to-all(f16[48,48,128]{2,1,0:T(8,128)(2,1)S(1)} %convert_element_type.32), channel_id=1, replica_groups=mesh['stratum'=16,'inner'=48] {'inner'}, dimensions={0} | all-to-all | bytes 1179648 | tf_op jit(solution)/shard_map/all_to_all | solution.py:207
  124.7 0.1 convert_element_type.33.got
  124.8 3.4 %shard_map.106 = (f32[48,40,128]{2,1,0:T(8,128)S(1)}, f32[512,256]{1,0:T(8,128)S(1)}, f32[512,256]{1,0:T(8,128)S(1)}) custom-call(f32[48,48,128]{2,1,0:T(8,128)S(1)} %convert_element_type.33.got, f32[512,256]{1,0:T(8,128)S(1)} %copy-done, f32[512,256]{1,0:T(8,128)S(1)} %get-tuple-element.16.mid, bf16[2,8,128,128]{3,2,1,0:T(8,128)(2,1)S(1)} %copy-done.1, ...), custom_call_target="tpu_custom_call" | custom-call | tf_op jit(solution)/shard_map/pallas_call | solution.py:196
  128.1 0.8 convert_element_type.34
  129.0 6.6 %all-to-all-start.4 = ((f16[48,40,128]{2,1,0:T(8,128)(2,1)}), f16[48,40,128]{2,1,0:T(8,128)(2,1)S(1)}, u32[]{:S(2)}, u32[]{:S(2)}) async-start(f16[48,40,128]{2,1,0:T(8,128)(2,1)} %convert_element_type.34), calls=%async_computation.4 | async-start | bytes 983040 | tf_op jit(solution)/shard_map/all_to_all | solution.py:207
  135.6 3.0 %collective-permute-start = (f32[32,256]{1,0:T(8,128)S(1)}, f32[32,256]{1,0:T(8,128)S(1)}, u32[]{:S(2)}, u32[]{:S(2)}) collective-permute-start(f32[32,256]{1,0:T(8,128)S(1)} %get-tuple-element.20), channel_id=1, source_target_pairs={{48,0},{96,48},{144,96},{192,144},{240,192},{288,240},{336,288},{3... | collective-permute-start | bytes 98312 | tf_op jit(solution)/shard_map/ppermute | solution.py:251
  138.6 19.1 %all-to-all-done.4 = f16[48,40,128]{2,1,0:T(8,128)(2,1)S(1)} async-done(((f16[48,40,128]{2,1,0:T(8,128)(2,1)}), f16[48,40,128]{2,1,0:T(8,128)(2,1)S(1)}, u32[]{:S(2)}, u32[]{:S(2)}) %all-to-all-start.4) | async-done | bytes 491552 | tf_op jit(solution)/shard_map/all_to_all | solution.py:207
  157.7 0.1 convert_element_type.35
  157.8 0.1 fusion
  157.9 0.0 collective-permute-done.state
  157.9 5.2 %collective-permute-start.1 = (f32[32,256]{1,0:T(8,128)S(1)}, f32[32,256]{1,0:T(8,128)S(1)}, u32[]{:S(2)}, u32[]{:S(2)}) collective-permute-start(f32[32,256]{1,0:T(8,128)S(1)} %shard_map.108), channel_id=1, source_target_pairs={{48,0},{96,48},{144,96},{192,144},{240,192},{288,240},{336,288},{3... | collective-permute-start | bytes 98312 | tf_op jit(solution)/shard_map/ppermute | solution.py:264
  163.1 1.2 shard_map.107
  164.4 4.8 %collective-permute-done.1 = f32[32,256]{1,0:T(8,128)S(1)} collective-permute-done((f32[32,256]{1,0:T(8,128)S(1)}, f32[32,256]{1,0:T(8,128)S(1)}, u32[]{:S(2)}, u32[]{:S(2)}) %collective-permute-start.1) | collective-permute-done | bytes 32800 | tf_op jit(solution)/shard_map/ppermute | solution.py:264
  169.2 0.6 fusion.1
  (5 shorter events, 0.1 us)
Async XLA Ops:
  0.6 39.8 %copy-start.2 = (f32[16,256]{1,0:T(8,128)S(1)}, f32[16,256]{1,0:T(8,128)}, u32[]{:S(2)}) copy-start(f32[16,256]{1,0:T(8,128)} %held.1) | copy-start | bytes 49156
  0.6 20.2 %copy-start.7 = (s32[2,1]{0,1:T(1,128)S(1)}, s32[2,1]{0,1:T(1,128)}, u32[]{:S(2)}) copy-start(s32[2,1]{0,1:T(1,128)} %param.14) | copy-start | bytes 28
  0.7 39.8 %copy-start.4 = (s32[2,4]{1,0:T(2,128)S(1)}, s32[2,4]{1,0:T(2,128)}, u32[]{:S(2)}) copy-start(s32[2,4]{1,0:T(2,128)} %ids.3) | copy-start | bytes 100
  0.7 39.8 %copy-start.6 = (s32[2,8]{1,0:T(2,128)S(1)}, s32[2,8]{1,0:T(2,128)}, u32[]{:S(2)}) copy-start(s32[2,8]{1,0:T(2,128)} %cols.3) | copy-start | bytes 196
  0.7 39.8 %copy-start.5 = (s32[2,8]{1,0:T(2,128)S(1)}, s32[2,8]{1,0:T(2,128)}, u32[]{:S(2)}) copy-start(s32[2,8]{1,0:T(2,128)} %rows.3) | copy-start | bytes 196
  0.7 39.8 %copy-start.1 = (bf16[2,8,128,128]{3,2,1,0:T(8,128)(2,1)S(1)}, bf16[2,8,128,128]{3,2,1,0:T(8,128)(2,1)}, u32[]{:S(2)}) copy-start(bf16[2,8,128,128]{3,2,1,0:T(8,128)(2,1)} %values.3) | copy-start | bytes 1572868
  0.7 39.8 %copy-start = (f32[512,256]{1,0:T(8,128)S(1)}, f32[512,256]{1,0:T(8,128)}, u32[]{:S(2)}) copy-start(f32[512,256]{1,0:T(8,128)} %users.3) | copy-start | bytes 1572868
  2.3 38.1 %all-to-all-start = ((bf16[48,16,256]{2,1,0:T(8,128)(2,1)}), bf16[48,16,256]{2,1,0:T(8,128)(2,1)S(1)}, u32[]{:S(2)}, u32[]{:S(2)}) async-start(bf16[48,16,256]{2,1,0:T(8,128)(2,1)} %broadcast_in_dim.2), calls=%async_computation | async-start | bytes 786432 | tf_op jit(solution)/shard_map/all_to_all | solution.py:207
  42.7 28.6 %copy-start.3 = (f32[16,256]{1,0:T(8,128)S(1)}, f32[16,256]{1,0:T(8,128)}, u32[]{:S(2)}) copy-start(f32[16,256]{1,0:T(8,128)} %accum.1) | copy-start | bytes 49156
  129.0 28.8 %all-to-all-start.4 = ((f16[48,40,128]{2,1,0:T(8,128)(2,1)}), f16[48,40,128]{2,1,0:T(8,128)(2,1)S(1)}, u32[]{:S(2)}, u32[]{:S(2)}) async-start(f16[48,40,128]{2,1,0:T(8,128)(2,1)} %convert_element_type.34), calls=%async_computation.4 | async-start | bytes 983040 | tf_op jit(solution)/shard_map/all_to_all | solution.py:207
  135.6 22.3 %collective-permute-start = (f32[32,256]{1,0:T(8,128)S(1)}, f32[32,256]{1,0:T(8,128)S(1)}, u32[]{:S(2)}, u32[]{:S(2)}) collective-permute-start(f32[32,256]{1,0:T(8,128)S(1)} %get-tuple-element.20), channel_id=1, source_target_pairs={{48,0},{96,48},{144,96},{192,144},{240,192},{288,240},{336,288},{3... | collective-permute-start | bytes 98312 | tf_op jit(solution)/shard_map/ppermute | solution.py:251
  157.9 11.3 %collective-permute-start.1 = (f32[32,256]{1,0:T(8,128)S(1)}, f32[32,256]{1,0:T(8,128)S(1)}, u32[]{:S(2)}, u32[]{:S(2)}) collective-permute-start(f32[32,256]{1,0:T(8,128)S(1)} %shard_map.108), channel_id=1, source_target_pairs={{48,0},{96,48},{144,96},{192,144},{240,192},{288,240},{336,288},{3... | collective-permute-start | bytes 98312 | tf_op jit(solution)/shard_map/ppermute | solution.py:264

commit v3 on v2

--- a/solution.py
+++ b/solution.py
@@ -12,17 +12,22 @@
 LAMBDA = 64.0
 
 LANES = 128
+NEAR = 4
 F32 = jnp.float32
 BF16 = jnp.bfloat16
 F16 = jnp.float16
 
 GRAD_SCALE = 2.0**-6
+GRAD_SUM_SCALE = 2.0**-8
 ROOT_SCALE = 2.0**-9
+ROOT_SUM_SCALE = 2.0**-10
 ITEM_SCALE = 2.0**12
 GRAM_SCALE = 2.0**12
 GRAM_LOCAL_SCALE = 2.0**10
+GRAM_NEAR_SCALE = 2.0**8
 GRAM_STRATUM_SCALE = 2.0**5
 GRAM_INNER_SCALE = 2.0**6
+GRAM_TAIL_SCALE = 2.0**3
 
 VMEM = pltpu.VMEM
 SMEM = pltpu.SMEM
@@ -75,9 +80,10 @@
     return contract(uh, gh, (1, 0)) + (contract(ul, gh, (1, 0)) + contract(uh, gl, (1, 0)))
 
 
-def slot_grads(step, users_bf, block, values, rows, cols, count, grad_users, sums):
+def slot_grads(step, stride, users_bf, block, values, rows, cols, count, grad_users, sums):
     slots, tile_u, tile_i = values.shape[1:]
     chunk = 16
+    fars = tile_i // chunk // NEAR
     live = count[step, 0]
     for k in range(slots):
         row = pl.multiple_of(rows[step, k] * tile_u, tile_u)
@@ -88,20 +94,28 @@
         err = jnp.where(k < live, scores - values[step, k].astype(F32), 0.0).astype(BF16)
         grad_users[pl.ds(row, tile_u), :] += contract(err, item_tile, (1, 0))
         part = contract(err, user_tile, (0, 0))
-        at = pl.ds(col * (tile_i // chunk), tile_i // chunk)
-        sums[at, 0:chunk, :] += part[:, :LANES].reshape(-1, chunk, LANES)
-        sums[at, chunk : 2 * chunk, :] += part[:, LANES:].reshape(-1, chunk, LANES)
+        for near in range(NEAR):
+            for far in range(fars):
+                at = pl.multiple_of((col * fars + far) * stride, 8)
+                rows_of = part[(far * NEAR + near) * chunk :][:chunk]
+                sums[near, pl.ds(at, chunk), :] += rows_of[:, :LANES]
+                sums[near, pl.ds(at + chunk, chunk), :] += rows_of[:, LANES:]
 
 
 def first_kernel(block, users, own, values, rows, cols, count, ids, sums, users_out, users_bf, grad_users):
-    chunks = sums.shape[0]
+    fars = block.shape[0] // (16 * NEAR)
+    stride = sums.shape[1] // fars
     users_bf[...] = users[...].astype(BF16)
     grad_users[...] = jnp.zeros_like(grad_users)
     sums[...] = jnp.zeros_like(sums)
-    slot_grads(0, users_bf, block, values, rows, cols, count, grad_users, sums)
-    sums[:, 0:32, :] = sums[:, 0:32, :] * GRAD_SCALE
+    slot_grads(0, stride, users_bf, block, values, rows, cols, count, grad_users, sums)
     picks = picked_rows(own[...].astype(BF16), ids, 0).astype(BF16)
-    sums[:, 32:, :] = (gram_parts(picks, picks) * GRAM_LOCAL_SCALE).reshape(chunks, -1, LANES)
+    parts = (gram_parts(picks, picks) * GRAM_LOCAL_SCALE).reshape(fars, NEAR, -1, LANES)
+    for far in range(fars):
+        for near in range(NEAR):
+            at = far * stride
+            sums[near, at : at + 32, :] = sums[near, at : at + 32, :] * GRAD_SCALE
+            sums[near, at + 32 : at + stride, :] = parts[far, near]
     users_out[...] = users[...] - LR_USER * grad_users[...]
 
 
@@ -124,7 +138,7 @@
     rows = held.shape[0]
     piece = got.shape[1] - 2 * rows
     total = jnp.sum(got[...], axis=0)
-    gradient = widths(total[0 : 2 * rows] * (1.0 / GRAD_SCALE))
+    gradient = widths(total[0 : 2 * rows] * (1.0 / GRAD_SUM_SCALE))
     new, state[rows:, :] = update(held[...], accum[...], gradient)
     state[0:rows, :] = new
     strata = out.shape[0]
@@ -132,7 +146,7 @@
         [
             halves(new.astype(BF16).astype(F32)) * ITEM_SCALE,
             pick_counts(ids, 1),
-            total[2 * rows :] * (GRAM_STRATUM_SCALE / GRAM_LOCAL_SCALE),
+            total[2 * rows :] * (GRAM_STRATUM_SCALE / GRAM_NEAR_SCALE),
         ],
         axis=0,
     )
@@ -143,6 +157,7 @@
     chunks = out.shape[0]
     strata = met.shape[0]
     piece = met.shape[1] - 40
+    fars = chunks
     after = lax.rem(lax.axis_index("stratum") + 1, strata)
     items = met[pl.ds(after, 1), 0:32, :]
     out[:, 0:32, :] = jnp.broadcast_to(items, (chunks, 32, LANES))
@@ -155,40 +170,47 @@
     plain = jnp.concatenate([r.reshape(-1, LANES) for r in rows], axis=1).astype(BF16)
     high, low = split(weighed)
     parts = gram_parts(jnp.concatenate([high, low], axis=0), jnp.concatenate([plain, plain], axis=0))
-    out[:, 32 + piece :, :] = (parts * GRAM_INNER_SCALE).reshape(chunks, piece, LANES)
+    out[:, 32 + piece :, :] = (parts * GRAM_INNER_SCALE).reshape(fars, NEAR * piece, LANES)
 
 
 def second_kernel(
     total, got, users, mid, values, rows, cols, count, sums, users_out, mid_out, users_bf, grad_users, block
 ):
-    chunks = sums.shape[0]
-    piece = sums.shape[1] - 32
-    left = (got[:, 0:16, :] * (1.0 / ITEM_SCALE)).astype(BF16).reshape(-1, LANES)
-    right = (got[:, 16:32, :] * (1.0 / ITEM_SCALE)).astype(BF16).reshape(-1, LANES)
-    block[:, :LANES] = left
-    block[:, LANES:] = right
-    gram = whole_gram(got[:, 32 : 32 + piece, :].reshape(-1, LANES) * (1.0 / GRAM_SCALE))
+    fars = block.shape[0] // (16 * NEAR)
+    piece = sums.shape[1] - 32 * fars
+    stride = 32 + piece
+    parts = []
+    for far in range(fars):
+        for near in range(NEAR):
+            to = (far * NEAR + near) * 16
+            rows_of = got[near, far * stride : (far + 1) * stride, :]
+            block[to : to + 16, :LANES] = (rows_of[0:16] * (1.0 / ITEM_SCALE)).astype(BF16)
+            block[to : to + 16, LANES:] = (rows_of[16:32] * (1.0 / ITEM_SCALE)).astype(BF16)
+            parts.append(rows_of[32:])
+    gram = whole_gram(jnp.concatenate(parts, axis=0) * (1.0 / GRAM_SCALE))
     now = mid[...] - (LR_USER * LAMBDA) * times_gram(users[...], gram)
     mid_out[...] = now
     users_bf[...] = now.astype(BF16)
     grad_users[...] = jnp.zeros_like(grad_users)
     sums[...] = jnp.zeros_like(sums)
-    slot_grads(1, users_bf, block, values, rows, cols, count, grad_users, sums)
-    raw = sums[:, 0:32, :]
+    slot_grads(1, 32, users_bf, block, values, rows, cols, count, grad_users, sums)
+    raw = sums[:, : 32 * fars, :]
     root = jnp.sqrt(jnp.abs(raw)) * ROOT_SCALE
-    sums[:, 0:32, :] = jnp.where(raw < 0.0, -root, root)
-    full = jnp.sum(got[:, 32 + piece :, :], axis=0) * (GRAM_SCALE / GRAM_INNER_SCALE / total)
-    sums[:, 32:, :] = jnp.broadcast_to(full[None], (chunks, piece, LANES))
+    sums[:, : 32 * fars, :] = jnp.where(raw < 0.0, -root, root)
+    full = jnp.sum(got[:, fars * stride :, :], axis=0) * (GRAM_SCALE / GRAM_TAIL_SCALE / total)
+    sums[:, 32 * fars :, :] = jnp.broadcast_to(full[None], (NEAR, piece, LANES))
     users_out[...] = now - LR_USER * grad_users[...]
 
 
-def last_items_kernel(total, state, out):
+def last_items_kernel(got, state, out):
     rows = state.shape[0] // 2
-    out[0:rows, :], out[rows:, :] = update(state[0:rows, :], state[rows:, :], widths(total[...]))
+    root = got[:, : 2 * rows, :]
+    gradient = widths(jnp.sum(root * jnp.abs(root), axis=0) * ROOT_SUM_SCALE**-2)
+    out[0:rows, :], out[rows:, :] = update(state[0:rows, :], state[rows:, :], gradient)
 
 
 def last_users_kernel(got, users, mid, out):
-    gram = whole_gram(got[...].reshape(-1, LANES) * (1.0 / GRAM_SCALE))
+    gram = whole_gram(got[:, 32:, :].reshape(-1, LANES) * (1.0 / GRAM_SCALE))
     out[...] = users[...] - (LR_USER * LAMBDA) * times_gram(mid[...], gram)
 
 
@@ -211,72 +233,91 @@
     user_factors, item_factors, item_accum, tile_values, tile_rows, tile_cols, tile_count, neg_ids
 ):
     strata = lax.axis_size("stratum")
-    inners = lax.axis_size("inner")
+    fars = lax.axis_size("far")
+    inners = fars * NEAR
     own, rank = item_factors.shape
-    negs = neg_ids.shape[1]
-    total = float(strata * inners * negs)
+    total = float(strata * inners * neg_ids.shape[1])
     piece = 3 * LANES // inners
+    pair = 2 * own
     users_shape = jax.ShapeDtypeStruct(user_factors.shape, F32)
-    state_shape = jax.ShapeDtypeStruct((2 * own, rank), F32)
+    state_shape = jax.ShapeDtypeStruct((pair, rank), F32)
     users_scratch = [pltpu.VMEM(user_factors.shape, BF16), pltpu.VMEM(user_factors.shape, F32)]
-    sums_shape = jax.ShapeDtypeStruct((inners, 2 * own + piece, LANES), F32)
     vm = pl.BlockSpec(memory_space=VMEM)
     sm = pl.BlockSpec(memory_space=SMEM)
     onward = [((s + 1) % strata, s) for s in range(strata)]
 
     held_bf = jnp.broadcast_to(item_factors.astype(BF16)[None], (inners, own, rank))
-    block = exchanged(held_bf, "inner").reshape(inners * own, rank)
+    block = exchanged(held_bf, ("far", "near")).reshape(inners * own, rank)
     sums, mid = call(
         first_kernel,
-        (sums_shape, users_shape),
+        (jax.ShapeDtypeStruct((NEAR, fars * (pair + piece), LANES), F32), users_shape),
         [vm, vm, vm, vm, sm, sm, sm, sm],
         block, user_factors, item_factors, tile_values, tile_rows, tile_cols, tile_count, neg_ids,
         scratch=users_scratch,
     )
-    got = exchanged(sums.astype(F16), "inner").astype(F32)
+    got = exchanged(sums.astype(F16), "near").astype(F32)
+    got = (jnp.sum(got, axis=0) * 0.25).astype(F16).reshape(fars, pair + piece, LANES)
+    got = exchanged(got, "far").astype(F32)
     state, sent = call(
         item_kernel,
-        (state_shape, jax.ShapeDtypeStruct((strata, 2 * own + 8 + piece, LANES), F32)),
+        (state_shape, jax.ShapeDtypeStruct((strata, pair + 8 + piece, LANES), F32)),
         [vm, vm, vm, sm],
         got, item_factors, item_accum, neg_ids,
     )
     met = exchanged(sent.astype(F16), "stratum").astype(F32)
     payload = call(
         functools.partial(gather_kernel, total),
-        jax.ShapeDtypeStruct((inners, 2 * own + 2 * piece, LANES), F32),
+        jax.ShapeDtypeStruct((fars, pair + piece + NEAR * piece, LANES), F32),
         [vm],
         met,
     ).astype(F16)
+    got = exchanged(payload, "far")
+    both = got[:, : pair + piece].reshape(1, -1, LANES)
+    tail = jnp.sum(got[:, pair + piece :].astype(F32), axis=0) * (GRAM_TAIL_SCALE / GRAM_INNER_SCALE)
+    payload = jnp.concatenate(
+        [jnp.broadcast_to(both, (NEAR,) + both.shape[1:]), tail.astype(F16).reshape(NEAR, piece, LANES)],
+        axis=1,
+    )
     payload, state = lax.optimization_barrier((payload, state))
     state = lax.ppermute(state, "stratum", onward)
-    got = exchanged(payload, "inner").astype(F32)
+    got = exchanged(payload, "near").astype(F32)
     sums, users, mid = call(
         functools.partial(second_kernel, total),
-        (sums_shape, users_shape, users_shape),
+        (jax.ShapeDtypeStruct((NEAR, fars * pair + piece, LANES), F32), users_shape, users_shape),
         [vm, vm, vm, vm, sm, sm, sm],
         got, user_factors, mid, tile_values, tile_rows, tile_cols, tile_count,
         scratch=users_scratch + [pltpu.VMEM((inners * own, rank), BF16)],
     )
-    got = exchanged(sums.astype(F16), "inner").astype(F32)
-    root = got[:, : 2 * own]
-    gradient = jnp.sum(root * jnp.abs(root), axis=0) * (ROOT_SCALE**-2)
-    state = call(last_items_kernel, state_shape, [vm, vm], gradient, state)
+    got = exchanged(sums.astype(F16), "near")
+    root = got[:, : fars * pair].astype(F32)
+    square = jnp.sum(root * jnp.abs(root), axis=0)
+    root = jnp.sqrt(jnp.abs(square)) * (ROOT_SUM_SCALE / ROOT_SCALE)
+    root = jnp.where(square < 0.0, -root, root).astype(F16).reshape(fars, pair, LANES)
+    tails = got[:, fars * pair :].reshape(1, NEAR * piece, LANES)
+    payload = jnp.concatenate([root, jnp.broadcast_to(tails, (fars,) + tails.shape[1:])], axis=1)
+    got = exchanged(payload, "far").astype(F32)
+    state = call(last_items_kernel, state_shape, [vm, vm], got, state)
     state = lax.ppermute(state, "stratum", onward)
-    users = call(last_users_kernel, users_shape, [vm, vm, vm], got[:, 2 * own :], users, mid)
+    users = call(last_users_kernel, users_shape, [vm, vm, vm], got, users, mid)
     return (users, state[:own], state[own:])
 
 
 def solution(mesh):
-    devices = P(("stratum", "inner"), None)
-    slots = P(None, ("stratum", "inner"))
+    strata, inners = mesh.devices.shape
+    fine = jax.sharding.Mesh(
+        mesh.devices.reshape(strata, inners // NEAR, NEAR), ("stratum", "far", "near")
+    )
+    every = ("stratum", "far", "near")
+    devices = P(every, None)
+    slots = P(None, every)
     return jax.shard_map(
         shards,
-        mesh=mesh,
+        mesh=fine,
         in_specs=(
             devices,
             devices,
             devices,
-            P(None, ("stratum", "inner"), None, None),
+            P(None, every, None, None),
             slots,
             slots,
             slots,

time: 171 us -> 173 us (1.012)
  blocking collectives: 80.6 us -> 94.7 us
  waiting for transfers between devices: 43.4 us -> 30.4 us
    all_to_all x3 -> x6, blocking collectives: 80.6 us -> 94.7 us  [exchanged(): return lax.all_to_all(x, axis, 0, 0, tiled=True)]
    all_to_all x2, waiting for transfers between devices: 38.5 us -> 26.2 us  [exchanged(): return lax.all_to_all(x, axis, 0, 0, tiled=True)]
    ppermute x2, starting transfers between devices: 8.2 us -> 10.3 us  [shards(): state = lax.ppermute(state, 'stratum', onward)]
    all_to_all x2, starting transfers between devices: 25.2 us -> 23.4 us  [exchanged(): return lax.all_to_all(x, axis, 0, 0, tiled=True)]
  transfers between devices with their start and end apart: 4 -> 4, of which waited for: 3 -> 4; matrix products, arithmetic and copies ran while one was open for 0% -> 0% of each run, Pallas kernels for 1% -> 1%
where the time goes in v3:
time: 173 us; the launch traced here: 172 us
  blocking collectives  94.7 us (55%)
  starting transfers between devices  33.7 us (19%)
  waiting for transfers between devices  30.4 us (18%)
  Pallas kernels  7.76 us (4%)
  local copies, waits for them, and re-layouts  2.33 us (1%)
  other arithmetic  2.27 us (1%)
    all_to_all x6, blocking collectives, exchanged(): return lax.all_to_all(x, axis, 0, 0, tiled=True)  94.7 us
    all_to_all x2, waiting for transfers between devices, exchanged(): return lax.all_to_all(x, axis, 0, 0, tiled=True)  26.2 us
    all_to_all x2, starting transfers between devices, exchanged(): return lax.all_to_all(x, axis, 0, 0, tiled=True)  23.4 us
    ppermute x2, starting transfers between devices, shards(): state = lax.ppermute(state, 'stratum', onward)  10.3 us
    pallas_call x6, Pallas kernels, call(): pl.pallas_call(kernel, out_shape=out_shape, in_specs=specs, out_specs=jax...  7.76 us
    ppermute x2, waiting for transfers between devices, shards(): state = lax.ppermute(state, 'stratum', onward)  4.18 us
  transfers between devices with their start and end apart: 4, of which 4 were waited for; matrix products, arithmetic and copies ran while one was open for 0% of the time, Pallas kernels for 1%

profile of v3, /device:TPU:7, one launch (start us, length us, event | category | flops | bytes accessed | tf_op | source)
XLA Modules:
  0.0 172.0 jit_solution(12615713623835529087)
XLA Ops:
  0.6 0.7 convert_element_type.54
  1.4 0.0 copy-start
  1.4 0.0 copy-start.1
  1.4 0.8 broadcast_in_dim.20
  2.1 0.0 copy-start.7
  2.1 0.0 copy-start.2
  2.1 18.7 %all-to-all-start = ((bf16[48,16,256]{2,1,0:T(8,128)(2,1)}), bf16[48,16,256]{2,1,0:T(8,128)(2,1)S(1)}, u32[]{:S(2)}, u32[]{:S(2)}) async-start(bf16[48,16,256]{2,1,0:T(8,128)(2,1)} %broadcast_in_dim.20), calls=%async_computation | async-start | bytes 786432 | tf_op jit(solution)/shard_map/all_to_all | solution.py:229
  20.9 0.0 copy-done.7
  20.9 0.0 copy-start.5
  20.9 0.0 copy-start.6
  20.9 0.1 copy.11.count
  21.0 0.0 copy-start.4
  21.0 19.4 %all-to-all-done = bf16[48,16,256]{2,1,0:T(8,128)(2,1)S(1)} async-done(((bf16[48,16,256]{2,1,0:T(8,128)(2,1)}), bf16[48,16,256]{2,1,0:T(8,128)(2,1)S(1)}, u32[]{:S(2)}, u32[]{:S(2)}) %all-to-all-start) | async-done | bytes 393248 | tf_op jit(solution)/shard_map/all_to_all | solution.py:229
  40.4 0.0 copy-done
  40.4 0.0 copy-done.1
  40.4 0.0 copy-done.2
  40.4 0.0 copy-done.5
  40.4 0.0 copy-done.6
  40.4 0.0 copy-done.4
  40.4 2.2 %shard_map.103 = (f32[4,480,128]{2,1,0:T(8,128)S(1)}, f32[512,256]{1,0:T(8,128)S(1)}) custom-call(bf16[768,256]{1,0:T(8,128)(2,1)S(1)} %bitcast.9, f32[512,256]{1,0:T(8,128)S(1)} %copy-done, f32[16,256]{1,0:T(8,128)S(1)} %copy-done.2, bf16[2,8,128,128]{3,2,1,0:T(8,128)(2,1)S(1)} %copy-done.1, s32[2,8]{1,0:T(2,128)S(1)} %copy-done.5, s32[2,8]{1,0:T(2,128)S(1)} %copy-done.6, ...), custom_call_target="tpu_custom_call" | custom-call | tf_op jit(solution)/shard_map/pallas_call | solution.py:218
  42.6 0.1 convert_element_type.55
  42.7 15.3 %all_to_all.40 = f16[4,480,128]{2,1,0:T(8,128)(2,1)S(1)} all-to-all(f16[4,480,128]{2,1,0:T(8,128)(2,1)S(1)} %convert_element_type.55), channel_id=1, replica_groups=mesh['stratum'=16,'far'=12,'near'=4] {'near'}, dimensions={0} | all-to-all | bytes 983040 | tf_op jit(solution)/shard_map/all_to_all | solution.py:229
  58.0 0.1 convert_reduce_fusion
  58.1 15.0 %all_to_all.41 = f16[12,40,128]{2,1,0:T(8,128)(2,1)S(1)} all-to-all(f16[12,40,128]{2,1,0:T(8,128)(2,1)S(1)} %bitcast.12), channel_id=1, replica_groups=mesh['stratum'=16,'far'=12,'near'=4] {'far'}, dimensions={0} | all-to-all | bytes 245760 | tf_op jit(solution)/shard_map/all_to_all | solution.py:229
  73.1 0.0 copy-start.3
  73.1 0.7 copy-done.3
  73.8 0.6 shard_map.104
  74.5 19.2 %all_to_all.42 = f16[16,48,128]{2,1,0:T(8,128)(2,1)S(1)} all-to-all(f16[16,48,128]{2,1,0:T(8,128)(2,1)S(1)} %convert_element_type.60), channel_id=1, replica_groups=mesh['stratum'=16,'far'=12,'near'=4] {'stratum'}, dimensions={0} | all-to-all | bytes 393216 | tf_op jit(solution)/shard_map/all_to_all | solution.py:229
  93.7 0.4 shard_map.105
  94.1 16.2 %all_to_all.43 = f16[12,72,128]{2,1,0:T(8,128)(2,1)S(1)} all-to-all(f16[12,72,128]{2,1,0:T(8,128)(2,1)S(1)} %convert_element_type.62), channel_id=1, replica_groups=mesh['stratum'=16,'far'=12,'near'=4] {'far'}, dimensions={0} | all-to-all | bytes 442368 | tf_op jit(solution)/shard_map/all_to_all | solution.py:229
  110.4 0.1 broadcast_in_dim.22
  110.5 0.1 pad_maximum_fusion
  110.7 15.7 %all_to_all.44 = f16[4,488,128]{2,1,0:T(8,128)(2,1)S(1)} all-to-all(f16[4,488,128]{2,1,0:T(8,128)(2,1)S(1)} %pad_maximum_fusion), channel_id=1, replica_groups=mesh['stratum'=16,'far'=12,'near'=4] {'near'}, dimensions={0} | all-to-all | bytes 999424 | tf_op jit(solution)/shard_map/all_to_all | solution.py:229
  126.3 0.1 convert_element_type.66.got
  126.4 3.3 %shard_map.106 = (f32[4,392,128]{2,1,0:T(8,128)S(1)}, f32[512,256]{1,0:T(8,128)S(1)}, f32[512,256]{1,0:T(8,128)S(1)}) custom-call(f32[4,488,128]{2,1,0:T(8,128)S(1)} %convert_element_type.66.got, f32[512,256]{1,0:T(8,128)S(1)} %copy-done, f32[512,256]{1,0:T(8,128)S(1)} %get-tuple-element.16.mid, bf16[2,8,128,128]{3,2,1,0:T(8,128)(2,1)S(1)} %copy-done.1, ...), custom_call_target="tpu_custom_call" | custom-call | tf_op jit(solution)/shard_map/pallas_call | solution.py:218
  129.7 0.1 convert_element_type.67
  129.7 13.3 %all_to_all.45 = f16[4,392,128]{2,1,0:T(8,128)(2,1)S(1)} all-to-all(f16[4,392,128]{2,1,0:T(8,128)(2,1)S(1)} %convert_element_type.67), channel_id=1, replica_groups=mesh['stratum'=16,'far'=12,'near'=4] {'near'}, dimensions={0} | all-to-all | bytes 802816 | tf_op jit(solution)/shard_map/all_to_all | solution.py:229
  143.1 0.1 fusion
  143.2 0.1 sqrt_multiply_fusion
  143.4 0.7 pad_maximum_fusion.1
  144.1 4.7 %all-to-all-start.7 = ((f16[12,64,128]{2,1,0:T(8,128)(2,1)}), f16[12,64,128]{2,1,0:T(8,128)(2,1)S(1)}, u32[]{:S(2)}, u32[]{:S(2)}) async-start(f16[12,64,128]{2,1,0:T(8,128)(2,1)} %pad_maximum_fusion.1), calls=%async_computation.7 | async-start | bytes 393216 | tf_op jit(solution)/shard_map/all_to_all | solution.py:229
  148.8 4.3 %collective-permute-start = (f32[32,256]{1,0:T(8,128)S(1)}, f32[32,256]{1,0:T(8,128)S(1)}, u32[]{:S(2)}, u32[]{:S(2)}) collective-permute-start(f32[32,256]{1,0:T(8,128)S(1)} %get-tuple-element.20), channel_id=1, source_target_pairs={{48,0},{96,48},{144,96},{192,144},{240,192},{288,240},{336,288},{3... | collective-permute-start | bytes 98312 | tf_op jit(solution)/shard_map/ppermute | solution.py:282
  153.1 6.8 %all-to-all-done.7 = f16[12,64,128]{2,1,0:T(8,128)(2,1)S(1)} async-done(((f16[12,64,128]{2,1,0:T(8,128)(2,1)}), f16[12,64,128]{2,1,0:T(8,128)(2,1)S(1)}, u32[]{:S(2)}, u32[]{:S(2)}) %all-to-all-start.7) | async-done | bytes 196640 | tf_op jit(solution)/shard_map/all_to_all | solution.py:229
  159.9 0.2 collective-permute-done.state
  160.1 6.0 %collective-permute-start.1 = (f32[32,256]{1,0:T(8,128)S(1)}, f32[32,256]{1,0:T(8,128)S(1)}, u32[]{:S(2)}, u32[]{:S(2)}) collective-permute-start(f32[32,256]{1,0:T(8,128)S(1)} %shard_map.108), channel_id=1, source_target_pairs={{48,0},{96,48},{144,96},{192,144},{240,192},{288,240},{336,288},{3... | collective-permute-start | bytes 98312 | tf_op jit(solution)/shard_map/ppermute | solution.py:300
  166.1 1.2 shard_map.107
  167.3 4.0 %collective-permute-done.1 = f32[32,256]{1,0:T(8,128)S(1)} collective-permute-done((f32[32,256]{1,0:T(8,128)S(1)}, f32[32,256]{1,0:T(8,128)S(1)}, u32[]{:S(2)}, u32[]{:S(2)}) %collective-permute-start.1) | collective-permute-done | bytes 32800 | tf_op jit(solution)/shard_map/ppermute | solution.py:300
  171.3 0.6 fusion.3
  (14 shorter events, 0.4 us)
Async XLA Ops:
  1.4 39.1 %copy-start = (f32[512,256]{1,0:T(8,128)S(1)}, f32[512,256]{1,0:T(8,128)}, u32[]{:S(2)}) copy-start(f32[512,256]{1,0:T(8,128)} %users.3) | copy-start | bytes 1572868
  1.4 39.1 %copy-start.1 = (bf16[2,8,128,128]{3,2,1,0:T(8,128)(2,1)S(1)}, bf16[2,8,128,128]{3,2,1,0:T(8,128)(2,1)}, u32[]{:S(2)}) copy-start(bf16[2,8,128,128]{3,2,1,0:T(8,128)(2,1)} %values.3) | copy-start | bytes 1572868
  2.1 18.7 %copy-start.7 = (s32[2,1]{0,1:T(1,128)S(1)}, s32[2,1]{0,1:T(1,128)}, u32[]{:S(2)}) copy-start(s32[2,1]{0,1:T(1,128)} %param.14) | copy-start | bytes 28
  2.1 38.3 %copy-start.2 = (f32[16,256]{1,0:T(8,128)S(1)}, f32[16,256]{1,0:T(8,128)}, u32[]{:S(2)}) copy-start(f32[16,256]{1,0:T(8,128)} %held.1) | copy-start | bytes 49156
  2.1 38.3 %all-to-all-start = ((bf16[48,16,256]{2,1,0:T(8,128)(2,1)}), bf16[48,16,256]{2,1,0:T(8,128)(2,1)S(1)}, u32[]{:S(2)}, u32[]{:S(2)}) async-start(bf16[48,16,256]{2,1,0:T(8,128)(2,1)} %broadcast_in_dim.20), calls=%async_computation | async-start | bytes 786432 | tf_op jit(solution)/shard_map/all_to_all | solution.py:229
  20.9 19.6 %copy-start.5 = (s32[2,8]{1,0:T(2,128)S(1)}, s32[2,8]{1,0:T(2,128)}, u32[]{:S(2)}) copy-start(s32[2,8]{1,0:T(2,128)} %rows.3) | copy-start | bytes 196
  20.9 19.5 %copy-start.6 = (s32[2,8]{1,0:T(2,128)S(1)}, s32[2,8]{1,0:T(2,128)}, u32[]{:S(2)}) copy-start(s32[2,8]{1,0:T(2,128)} %cols.3) | copy-start | bytes 196
  21.0 19.5 %copy-start.4 = (s32[2,4]{1,0:T(2,128)S(1)}, s32[2,4]{1,0:T(2,128)}, u32[]{:S(2)}) copy-start(s32[2,4]{1,0:T(2,128)} %ids.3) | copy-start | bytes 100
  73.1 0.7 copy-start.3
  144.1 15.7 %all-to-all-start.7 = ((f16[12,64,128]{2,1,0:T(8,128)(2,1)}), f16[12,64,128]{2,1,0:T(8,128)(2,1)S(1)}, u32[]{:S(2)}, u32[]{:S(2)}) async-start(f16[12,64,128]{2,1,0:T(8,128)(2,1)} %pad_maximum_fusion.1), calls=%async_computation.7 | async-start | bytes 393216 | tf_op jit(solution)/shard_map/all_to_all | solution.py:229
  148.8 11.3 %collective-permute-start = (f32[32,256]{1,0:T(8,128)S(1)}, f32[32,256]{1,0:T(8,128)S(1)}, u32[]{:S(2)}, u32[]{:S(2)}) collective-permute-start(f32[32,256]{1,0:T(8,128)S(1)} %get-tuple-element.20), channel_id=1, source_target_pairs={{48,0},{96,48},{144,96},{192,144},{240,192},{288,240},{336,288},{3... | collective-permute-start | bytes 98312 | tf_op jit(solution)/shard_map/ppermute | solution.py:282
  160.1 11.3 %collective-permute-start.1 = (f32[32,256]{1,0:T(8,128)S(1)}, f32[32,256]{1,0:T(8,128)S(1)}, u32[]{:S(2)}, u32[]{:S(2)}) collective-permute-start(f32[32,256]{1,0:T(8,128)S(1)} %shard_map.108), channel_id=1, source_target_pairs={{48,0},{96,48},{144,96},{192,144},{240,192},{288,240},{336,288},{3... | collective-permute-start | bytes 98312 | tf_op jit(solution)/shard_map/ppermute | solution.py:300

commit v4 on v2

v4 whole, which is shorter than its diff:
```python
import functools

import jax
import jax.numpy as jnp
from jax import lax
from jax.experimental import pallas as pl
from jax.experimental.pallas import tpu as pltpu
from jax.sharding import PartitionSpec as P

LR_USER = 0.005
LR_ITEM = 0.05
LAMBDA = 64.0

LANES = 128
F32 = jnp.float32
BF16 = jnp.bfloat16
F16 = jnp.float16

GRAD_SCALE = 2.0**-6
ROOT_SCALE = 2.0**-9
ITEM_SCALE = 2.0**12
GRAM_SCALE = 2.0**12
GRAM_STRATUM_SCALE = 2.0**5
GRAM_INNER_SCALE = 2.0**6

ROWS = 16
PAIR = 2 * ROWS
PACKED = 2 * LANES + 1

VMEM = pltpu.VMEM
SMEM = pltpu.SMEM


def contract(a, b, dims):
    return lax.dot_general(a, b, ((dims[:1], dims[1:]), ((), ())), preferred_element_type=F32)


def halves(x):
    return jnp.concatenate([x[:, :LANES], x[:, LANES:]], axis=0)


def widths(x):
    rows = x.shape[0] // 2
    return jnp.concatenate([x[:rows], x[rows:]], axis=1)


def piece_rows(chunks):
    return 2 * (-(-PACKED // (2 * chunks)))


def packed_gram(weighed, rows):
    gram = contract(weighed, rows, (0, 0))
    upper, beside, lower = gram[:LANES, :LANES], gram[:LANES, LANES:], gram[LANES:, LANES:]
    row = lax.broadcasted_iota(jnp.int32, (LANES, LANES), 0)
    col = lax.broadcasted_iota(jnp.int32, (LANES, LANES), 1)
    both = jnp.where(col >= row, upper, lower)
    return both, beside, jnp.sum(jnp.where(col == row, lower, 0.0), axis=0, keepdims=True)


def put_packed(packed, weighed, rows, scale):
    both, beside, diagonal = packed_gram(weighed, rows)
    packed[...] = jnp.zeros_like(packed)
    packed[0:LANES, :] = both * scale
    packed[LANES : 2 * LANES, :] = beside * scale
    packed[2 * LANES : 2 * LANES + 1, :] = diagonal * scale


def whole_gram(packed, scale):
    both = packed[0:LANES, :] * scale
    beside = packed[LANES : 2 * LANES, :] * scale
    diagonal = packed[2 * LANES : 2 * LANES + 1, :] * scale
    row = lax.broadcasted_iota(jnp.int32, (LANES, LANES), 0)
    col = lax.broadcasted_iota(jnp.int32, (LANES, LANES), 1)
    above = jnp.where(col > row, both, 0.0)
    below = jnp.where(col < row, both, 0.0)
    upper = above + above.T + jnp.where(col == row, both, 0.0)
    lower = below + below.T + jnp.where(col == row, diagonal, 0.0)
    return jnp.concatenate(
        [jnp.concatenate([upper, beside], axis=1), jnp.concatenate([beside.T, lower], axis=1)], axis=0
    )


def split(x):
    high = x.astype(BF16)
    return high, (x - high.astype(F32)).astype(BF16)


def times_gram(users, gram):
    uh, ul = split(users)
    gh, gl = split(gram)
    return contract(uh, gh, (1, 0)) + (contract(ul, gh, (1, 0)) + contract(uh, gl, (1, 0)))


def pick_row(ids_ref, step):
    row = lax.broadcasted_iota(jnp.int32, (2, LANES), 0)
    lane = lax.broadcasted_iota(jnp.int32, (2, LANES), 1)
    counts = jnp.zeros((2, LANES), F32)
    for n in range(ids_ref.shape[1]):
        counts = counts + jnp.where((lane == ids_ref[step, n]) & (row == 0), 1.0, 0.0)
    return counts


def start_kernel(held, ids, out):
    stride = PAIR + 2
    rows = halves(held[...].astype(BF16))
    counts = pick_row(ids, 0).astype(BF16)
    for chunk in range(out.shape[0] // stride):
        at = chunk * stride
        out[at : at + PAIR, :] = rows
        out[at + PAIR : at + stride, :] = counts


def item_grads(step, users_bf, block, values, rows, cols, count, errors, scale, add):
    slots, tile_u, tile_i = values.shape[1:]
    live = count[step, 0]
    for k in range(slots):
        row = pl.multiple_of(rows[step, k] * tile_u, tile_u)
        col = cols[step, k]
        user_tile = users_bf[pl.ds(row, tile_u), :]
        item_tile = block[pl.ds(pl.multiple_of(col * tile_i, tile_i), tile_i), :]
        scores = contract(user_tile, item_tile, (1, 1))
        err = jnp.where(k < live, scores - values[step, k].astype(F32), 0.0).astype(BF16)
        errors[k] = err
        if scale is not None:
            err = err * jnp.asarray(scale, BF16)
        add(col, contract(err, user_tile, (0, 0)))


def user_grads(step, block, rows, cols, errors, grad_users):
    slots, tile_u, tile_i = errors.shape
    grad_users[...] = jnp.zeros_like(grad_users)
    for k in range(slots):
        row = pl.multiple_of(rows[step, k] * tile_u, tile_u)
        col = pl.multiple_of(cols[step, k] * tile_i, tile_i)
        grad_users[pl.ds(row, tile_u), :] += contract(errors[k], block[pl.ds(col, tile_i), :], (1, 0))


def first_kernel(got, users, values, rows, cols, count, sums, block, errors, users_bf):
    stride = PAIR + 2
    for chunk in range(block.shape[0] // ROWS):
        to, at = chunk * ROWS, chunk * stride
        block[to : to + ROWS, :LANES] = got[at : at + ROWS, :]
        block[to : to + ROWS, LANES:] = got[at + ROWS : at + PAIR, :]
    users_bf[...] = users[...].astype(BF16)
    sums[...] = jnp.zeros_like(sums)

    def add(col, part):
        chunks = part.shape[0] // ROWS
        at = pl.ds(col * chunks, chunks)
        sums[at, 0:ROWS, :] += part[:, :LANES].reshape(chunks, ROWS, LANES)
        sums[at, ROWS:PAIR, :] += part[:, LANES:].reshape(chunks, ROWS, LANES)

    item_grads(0, users_bf, block, values, rows, cols, count, errors, GRAD_SCALE, add)


def first_users_kernel(got, block, users, rows, cols, errors, users_out, piece_out, counts, packed, pieces, grad_users):
    stride = PAIR + 2
    chunks = block.shape[0] // ROWS
    user_grads(0, block, rows, cols, errors, grad_users)
    users_out[...] = users[...] - LR_USER * grad_users[...]
    for chunk in range(chunks):
        at = chunk * stride + PAIR
        counts[chunk : chunk + 1, :] = got[at : at + 2, :].astype(F32)[0:1]
    shape = (chunks, ROWS, LANES)
    own = lax.broadcasted_iota(jnp.int32, shape, 1) == lax.broadcasted_iota(jnp.int32, shape, 2)
    weight = jnp.sum(jnp.where(own, counts[...][:, None, :], 0.0), axis=2, keepdims=True)
    plain = block[...]
    left = (plain[:, :LANES].astype(F32).reshape(shape) * weight).reshape(-1, LANES)
    right = (plain[:, LANES:].astype(F32).reshape(shape) * weight).reshape(-1, LANES)
    high, low = split(jnp.concatenate([left, right], axis=1))
    put_packed(
        packed,
        jnp.concatenate([high, low], axis=0),
        jnp.concatenate([plain, plain], axis=0),
        GRAM_STRATUM_SCALE,
    )
    piece = packed.shape[0] // chunks
    for chunk in range(chunks):
        pieces[chunk, 0:piece, :] = packed[chunk * piece : (chunk + 1) * piece, :]
    piece_out[...] = pieces[lax.axis_index("inner")]


def update(held, accum, gradient):
    accum = accum + gradient * gradient
    return held - LR_ITEM * gradient / jnp.sqrt(accum), accum


def pick_counts(ids_ref, step):
    row = lax.broadcasted_iota(jnp.int32, (8, LANES), 0)
    lane = lax.broadcasted_iota(jnp.int32, (8, LANES), 1)
    row = jnp.where(lane < LANES // 2, row, row + 8)
    counts = jnp.zeros((8, LANES), F32)
    for n in range(ids_ref.shape[1]):
        counts = counts + jnp.where(row == ids_ref[step, n], 1.0, 0.0)
    return counts


def item_kernel(got, held, accum, gram_piece, ids, state, out):
    strata = out.shape[0]
    gradient = widths(jnp.sum(got[...], axis=0) * (1.0 / GRAD_SCALE))
    new, state[ROWS:, :] = update(held[...], accum[...], gradient)
    state[0:ROWS, :] = new
    items = halves(new.astype(BF16).astype(F32)) * ITEM_SCALE
    sent = jnp.concatenate([items, pick_counts(ids, 1), gram_piece[...]], axis=0)
    out[...] = jnp.broadcast_to(sent[None], (strata,) + sent.shape)


def gather_kernel(total, met, out, packed):
    strata = met.shape[0]
    chunks = lax.axis_size("inner")
    piece = packed.shape[0] // chunks
    stride = PAIR + 2 * piece
    after = lax.rem(lax.axis_index("stratum") + 1, strata)
    items = met[pl.ds(after, 1), 0:PAIR, :][0]
    full = jnp.sum(met[:, 40:, :], axis=0)[0:piece] * (GRAM_SCALE / GRAM_STRATUM_SCALE / total)
    counts = jnp.concatenate([met[-1:, 32:40, :], met[:-1, 32:40, :]], axis=0)
    counts = jnp.concatenate([counts[:, :, 0:1], counts[:, :, 64:65]], axis=1)
    rows = [met[:, 0:ROWS, :] * (1.0 / ITEM_SCALE), met[:, ROWS:PAIR, :] * (1.0 / ITEM_SCALE)]
    weighed = jnp.concatenate([(r * counts).reshape(-1, LANES) for r in rows], axis=1)
    plain = jnp.concatenate([r.reshape(-1, LANES) for r in rows], axis=1).astype(BF16)
    high, low = split(weighed)
    put_packed(
        packed,
        jnp.concatenate([high, low], axis=0),
        jnp.concatenate([plain, plain], axis=0),
        GRAM_INNER_SCALE,
    )
    for chunk in range(chunks):
        at = chunk * stride
        out[at : at + PAIR, :] = items
        out[at + PAIR : at + PAIR + piece, :] = full
        out[at + PAIR + piece : at + stride, :] = packed[chunk * piece : (chunk + 1) * piece, :]


def second_kernel(
    total, got, users, mid, values, rows, cols, count, sums, mid_out, block, errors, packed, users_bf, grads
):
    chunks = block.shape[0] // ROWS
    piece = packed.shape[0] // chunks
    stride = PAIR + 2 * piece
    full = jnp.zeros((piece, LANES), F32)
    for chunk in range(chunks):
        to, at = chunk * ROWS, chunk * stride
        block[to : to + ROWS, :LANES] = (got[at : at + ROWS, :] * (1.0 / ITEM_SCALE)).astype(BF16)
        block[to : to + ROWS, LANES:] = (got[at + ROWS : at + PAIR, :] * (1.0 / ITEM_SCALE)).astype(BF16)
        packed[chunk * piece : (chunk + 1) * piece, :] = got[at + PAIR : at + PAIR + piece, :]
        full = full + got[at + PAIR + piece : at + stride, :]
    gram = whole_gram(packed, 1.0 / GRAM_SCALE)
    now = mid[...] - (LR_USER * LAMBDA) * times_gram(users[...], gram)
    mid_out[...] = now
    users_bf[...] = now.astype(BF16)
    grads[...] = jnp.zeros_like(grads)

    def add(col, part):
        at = pl.multiple_of(col * part.shape[0], part.shape[0])
        grads[pl.ds(at, part.shape[0]), :] += part

    item_grads(1, users_bf, block, values, rows, cols, count, errors, None, add)
    full = full * (GRAM_SCALE / GRAM_INNER_SCALE / total)
    for chunk in range(chunks):
        at = chunk * (PAIR + piece)
        raw = halves(grads[chunk * ROWS : (chunk + 1) * ROWS, :])
        root = jnp.sqrt(jnp.abs(raw)) * ROOT_SCALE
        sums[at : at + PAIR, :] = jnp.where(raw < 0.0, -root, root)
        sums[at + PAIR : at + PAIR + piece, :] = full


def second_users_kernel(block, now, rows, cols, errors, users_out, grad_users):
    user_grads(1, block, rows, cols, errors, grad_users)
    users_out[...] = now[...] - LR_USER * grad_users[...]


def last_items_kernel(chunks, got, state, out):
    stride = got.shape[0] // chunks
    total = jnp.zeros((PAIR, LANES), F32)
    for chunk in range(chunks):
        root = got[chunk * stride : chunk * stride + PAIR, :]
        total = total + root * jnp.abs(root)
    out[0:ROWS, :], out[ROWS:, :] = update(
        state[0:ROWS, :], state[ROWS:, :], widths(total * ROOT_SCALE**-2)
    )


def last_users_kernel(chunks, got, users, mid, out, packed):
    stride = got.shape[0] // chunks
    piece = stride - PAIR
    for chunk in range(chunks):
        packed[chunk * piece : (chunk + 1) * piece, :] = got[chunk * stride + PAIR : (chunk + 1) * stride, :]
    gram = whole_gram(packed, 1.0 / GRAM_SCALE)
    out[...] = users[...] - (LR_USER * LAMBDA) * times_gram(mid[...], gram)


def call(kernel, out_shape, specs, *args, scratch=()):
    return pl.pallas_call(
        kernel,
        out_shape=out_shape,
        in_specs=specs,
        out_specs=jax.tree.map(lambda _: pl.BlockSpec(memory_space=VMEM), out_shape),
        scratch_shapes=scratch,
        compiler_params=pltpu.CompilerParams(vmem_limit_bytes=40 * 2**20),
    )(*args)


def exchanged(x, axis):
    return lax.all_to_all(x, axis, 0, 0, tiled=True)


def chunks_exchanged(flat, chunks):
    paired = flat.reshape(chunks, -1, 2, LANES)
    return exchanged(paired, "inner").reshape(flat.shape)


def shards(
    user_factors, item_factors, item_accum, tile_values, tile_rows, tile_cols, tile_count, neg_ids
):
    strata = lax.axis_size("stratum")
    inners = lax.axis_size("inner")
    rank = item_factors.shape[1]
    total = float(strata * inners * neg_ids.shape[1])
    piece = piece_rows(inners)
    padded = -(-piece // 8) * 8
    onward = [((s + 1) % strata, s) for s in range(strata)]
    vm = pl.BlockSpec(memory_space=VMEM)
    sm = pl.BlockSpec(memory_space=SMEM)
    shape = jax.ShapeDtypeStruct
    users_shape = shape(user_factors.shape, F32)
    users_f32 = pltpu.VMEM(user_factors.shape, F32)
    users_bf = pltpu.VMEM(user_factors.shape, BF16)
    state_shape = shape((PAIR, rank), F32)
    block_shape = shape((inners * ROWS, rank), BF16)
    errors_shape = shape(tile_values.shape[1:], BF16)
    packed = pltpu.VMEM((inners * piece, LANES), F32)

    sent = call(start_kernel, shape((inners * (PAIR + 2), LANES), BF16), [vm, sm], item_factors, neg_ids)
    got = chunks_exchanged(sent, inners)
    sums, block, errors = call(
        first_kernel,
        (shape((inners, PAIR, LANES), F32), block_shape, errors_shape),
        [vm, vm, vm, sm, sm, sm],
        got, user_factors, tile_values, tile_rows, tile_cols, tile_count,
        scratch=[users_bf],
    )
    sums = exchanged(sums.astype(F16), "inner").astype(F32)
    mid, gram_piece = call(
        first_users_kernel,
        (users_shape, shape((padded, LANES), F32)),
        [vm, vm, vm, sm, sm, vm],
        got, block, user_factors, tile_rows, tile_cols, errors,
        scratch=[
            pltpu.VMEM((inners, LANES), F32),
            packed,
            pltpu.VMEM((inners, padded, LANES), F32),
            users_f32,
        ],
    )
    state, sent = call(
        item_kernel,
        (state_shape, shape((strata, PAIR + 8 + padded, LANES), F32)),
        [vm, vm, vm, vm, sm],
        sums, item_factors, item_accum, gram_piece, neg_ids,
    )
    met = exchanged(sent.astype(F16), "stratum").astype(F32)
    sent = call(
        functools.partial(gather_kernel, total),
        shape((inners * (PAIR + 2 * piece), LANES), F32),
        [vm],
        met,
        scratch=[packed],
    ).astype(F16)
    got = chunks_exchanged(sent, inners).astype(F32)
    sums, mid, block, errors = call(
        functools.partial(second_kernel, total),
        (shape((inners * (PAIR + piece), LANES), F32), users_shape, block_shape, errors_shape),
        [vm, vm, vm, vm, sm, sm, sm],
        got, user_factors, mid, tile_values, tile_rows, tile_cols, tile_count,
        scratch=[packed, users_bf, pltpu.VMEM(block_shape.shape, F32)],
    )
    sums, state = lax.optimization_barrier((sums.astype(F16), state))
    state = lax.ppermute(state, "stratum", onward)
    got = chunks_exchanged(sums, inners).astype(F32)
    users = call(
        second_users_kernel, users_shape, [vm, vm, sm, sm, vm],
        block, mid, tile_rows, tile_cols, errors, scratch=[users_f32],
    )
    state = call(functools.partial(last_items_kernel, inners), state_shape, [vm, vm], got, state)
    state = lax.ppermute(state, "stratum", onward)
    users = call(
        functools.partial(last_users_kernel, inners), users_shape, [vm, vm, vm],
        got, users, mid, scratch=[packed],
    )
    return (users, state[:ROWS], state[ROWS:])


def solution(mesh):
    devices = P(("stratum", "inner"), None)
    slots = P(None, ("stratum", "inner"))
    return jax.shard_map(
        shards,
        mesh=mesh,
        in_specs=(
            devices,
            devices,
            devices,
            P(None, ("stratum", "inner"), None, None),
            slots,
            slots,
            slots,
            slots,
        ),
        out_specs=(devices, devices, devices),
        check_vma=False,
    )
```

time: 171 us -> 168 us (0.982)
  blocking collectives: 80.6 us -> 50.5 us
  waiting for transfers between devices: 43.4 us -> 61.1 us
  starting transfers between devices: 33.4 us -> 39.6 us
  Pallas kernels: 7.86 us -> 10.8 us
    all_to_all x3 -> x2, blocking collectives: 80.6 us -> 50.5 us  [exchanged(): return lax.all_to_all(x, axis, 0, 0, tiled=True)]
    all_to_all x2 -> x3, waiting for transfers between devices: 38.5 us -> 56.4 us  [exchanged(): return lax.all_to_all(x, axis, 0, 0, tiled=True)]
    all_to_all x2 -> x3, starting transfers between devices: 25.2 us -> 31.7 us  [exchanged(): return lax.all_to_all(x, axis, 0, 0, tiled=True)]
    pallas_call x6 -> x9, Pallas kernels: 7.86 us -> 10.8 us  [call(): pl.pallas_call(kernel, out_shape=out_shape, in_specs=specs, out_specs=jax...]
  transfers between devices with their start and end apart: 4 -> 5, of which waited for: 3 -> 4; matrix products, arithmetic and copies ran while one was open for 0% -> 0% of each run, Pallas kernels for 1% -> 2%
where the time goes in v4:
time: 168 us; the launch traced here: 167 us
  waiting for transfers between devices  61.1 us (36%)
  blocking collectives  50.5 us (30%)
  starting transfers between devices  39.6 us (24%)
  Pallas kernels  10.8 us (6%)
  local copies, waits for them, and re-layouts  2.22 us (1%)
  other arithmetic  2.01 us (1%)
    all_to_all x3, waiting for transfers between devices, exchanged(): return lax.all_to_all(x, axis, 0, 0, tiled=True)  56.4 us
    all_to_all x2, blocking collectives, exchanged(): return lax.all_to_all(x, axis, 0, 0, tiled=True)  50.5 us
    all_to_all x3, starting transfers between devices, exchanged(): return lax.all_to_all(x, axis, 0, 0, tiled=True)  31.7 us
    pallas_call x9, Pallas kernels, call(): pl.pallas_call(kernel, out_shape=out_shape, in_specs=specs, out_specs=jax...  10.8 us
    ppermute x2, starting transfers between devices, shards(): state = lax.ppermute(state, 'stratum', onward)  7.93 us
    ppermute x2, waiting for transfers between devices, shards(): state = lax.ppermute(state, 'stratum', onward)  4.66 us
  transfers between devices with their start and end apart: 5, of which 4 were waited for; matrix products, arithmetic and copies ran while one was open for 0% of the time, Pallas kernels for 2%

profile of v4, /device:TPU:7, one launch (start us, length us, event | category | flops | bytes accessed | tf_op | source)
XLA Modules:
  0.0 167.0 jit_solution(11396420501653047544)
XLA Ops:
  0.6 0.0 copy-start
  0.6 0.0 copy-start.1
  0.7 0.0 copy-start.2
  0.7 0.8 copy-done.2
  1.5 0.0 copy-start.7
  1.5 0.7 copy-done.7
  2.1 0.0 copy-start.9
  2.1 0.0 copy-start.5
  2.1 1.4 shard_map.103
  3.5 18.6 %all-to-all-start = ((bf16[48,17,2,128]{3,2,1,0:T(2,128)(2,1)}), bf16[48,17,2,128]{3,2,1,0:T(2,128)(2,1)S(1)}, u32[]{:S(2)}, u32[]{:S(2)}) async-start(bf16[48,17,2,128]{3,2,1,0:T(2,128)(2,1)} %bitcast), calls=%async_computation | async-start | bytes 835584 | tf_op jit(solution)/shard_map/all_to_all | solution.py:305
  22.1 0.0 copy-done.9
  22.1 0.1 copy.11.count
  22.2 20.1 %all-to-all-done = bf16[48,17,2,128]{3,2,1,0:T(2,128)(2,1)S(1)} async-done(((bf16[48,17,2,128]{3,2,1,0:T(2,128)(2,1)}), bf16[48,17,2,128]{3,2,1,0:T(2,128)(2,1)S(1)}, u32[]{:S(2)}, u32[]{:S(2)}) %all-to-all-start) | async-done | bytes 417824 | tf_op jit(solution)/shard_map/all_to_all | solution.py:305
  42.4 0.0 copy-done
  42.4 0.0 copy-done.1
  42.4 0.0 copy-done.5
  42.4 0.0 copy-done.6
  42.4 1.5 shard_map.104
  43.9 0.8 convert_element_type.28
  44.7 6.4 %all-to-all-start.1 = ((f16[48,32,128]{2,1,0:T(8,128)(2,1)}), f16[48,32,128]{2,1,0:T(8,128)(2,1)S(1)}, u32[]{:S(2)}, u32[]{:S(2)}) async-start(f16[48,32,128]{2,1,0:T(8,128)(2,1)} %convert_element_type.28), calls=%async_computation.1 | async-start | bytes 786432 | tf_op jit(solution)/shard_map/all_to_all | solution.py:305
  51.2 0.0 copy-start.3
  51.2 0.0 copy-start.4
  51.2 0.0 copy-start.8
  51.2 1.3 shard_map.105
  52.5 17.8 %all-to-all-done.1 = f16[48,32,128]{2,1,0:T(8,128)(2,1)S(1)} async-done(((f16[48,32,128]{2,1,0:T(8,128)(2,1)}), f16[48,32,128]{2,1,0:T(8,128)(2,1)S(1)}, u32[]{:S(2)}, u32[]{:S(2)}) %all-to-all-start.1) | async-done | bytes 393248 | tf_op jit(solution)/shard_map/all_to_all | solution.py:305
  70.3 0.1 convert_element_type.29.got
  70.4 0.0 copy-done.3
  70.4 0.0 copy-done.4
  70.4 0.0 copy-done.8
  70.5 0.7 shard_map.106
  71.2 19.7 %all_to_all.25 = f16[16,48,128]{2,1,0:T(8,128)(2,1)S(1)} all-to-all(f16[16,48,128]{2,1,0:T(8,128)(2,1)S(1)} %convert_element_type.30), channel_id=1, replica_groups=mesh['stratum'=16,'inner'=48] {'stratum'}, dimensions={0} | all-to-all | bytes 393216 | tf_op jit(solution)/shard_map/all_to_all | solution.py:305
  90.8 0.5 shard_map.107
  91.3 0.1 convert_element_type.32
  91.4 30.8 %all_to_all.26 = f16[48,22,2,128]{3,2,1,0:T(2,128)(2,1)S(1)} all-to-all(f16[48,22,2,128]{3,2,1,0:T(2,128)(2,1)S(1)} %bitcast.10), channel_id=1, replica_groups=mesh['stratum'=16,'inner'=48] {'inner'}, dimensions={0} | all-to-all | bytes 1081344 | tf_op jit(solution)/shard_map/all_to_all | solution.py:305
  122.2 0.1 convert.3.got
  122.3 3.1 %shard_map.108 = (f32[1824,128]{1,0:T(8,128)S(1)}, f32[512,256]{1,0:T(8,128)S(1)}, bf16[768,256]{1,0:T(8,128)(2,1)S(1)}, bf16[8,128,128]{2,1,0:T(8,128)(2,1)S(1)}) custom-call(f32[2112,128]{1,0:T(8,128)S(1)} %convert.3.got, f32[512,256]{1,0:T(8,128)S(1)} %copy-done, f32[512,256]{1,0:T(8,128)S(1)} %get-tuple-element.21.mid, ...), custom_call_target="tpu_custom_call" | custom-call | tf_op jit(solution)/shard_map/pallas_call | solution.py:294
  125.4 0.8 convert_element_type.35
  126.2 6.6 %all-to-all-start.4 = ((f16[48,19,2,128]{3,2,1,0:T(2,128)(2,1)}), f16[48,19,2,128]{3,2,1,0:T(2,128)(2,1)S(1)}, u32[]{:S(2)}, u32[]{:S(2)}) async-start(f16[48,19,2,128]{3,2,1,0:T(2,128)(2,1)} %bitcast.4), calls=%async_computation.4 | async-start | bytes 933888 | tf_op jit(solution)/shard_map/all_to_all | solution.py:305
  132.9 3.2 %collective-permute-start = (f32[32,256]{1,0:T(8,128)S(1)}, f32[32,256]{1,0:T(8,128)S(1)}, u32[]{:S(2)}, u32[]{:S(2)}) collective-permute-start(f32[32,256]{1,0:T(8,128)S(1)} %get-tuple-element.28), channel_id=1, source_target_pairs={{48,0},{96,48},{144,96},{192,144},{240,192},{288,240},{336,288},{3... | collective-permute-start | bytes 98312 | tf_op jit(solution)/shard_map/ppermute | solution.py:379
  136.1 18.5 %all-to-all-done.4 = f16[48,19,2,128]{3,2,1,0:T(2,128)(2,1)S(1)} async-done(((f16[48,19,2,128]{3,2,1,0:T(2,128)(2,1)}), f16[48,19,2,128]{3,2,1,0:T(2,128)(2,1)S(1)}, u32[]{:S(2)}, u32[]{:S(2)}) %all-to-all-start.4) | async-done | bytes 466976 | tf_op jit(solution)/shard_map/all_to_all | solution.py:305
  154.6 0.1 convert.2.got
  154.7 0.0 collective-permute-done.state
  154.7 0.1 shard_map.111
  154.8 4.7 %collective-permute-start.1 = (f32[32,256]{1,0:T(8,128)S(1)}, f32[32,256]{1,0:T(8,128)S(1)}, u32[]{:S(2)}, u32[]{:S(2)}) collective-permute-start(f32[32,256]{1,0:T(8,128)S(1)} %shard_map.111), channel_id=1, source_target_pairs={{48,0},{96,48},{144,96},{192,144},{240,192},{288,240},{336,288},{3... | collective-permute-start | bytes 98312 | tf_op jit(solution)/shard_map/ppermute | solution.py:386
  159.5 0.9 shard_map.109.users
  160.5 1.3 shard_map.110
  161.7 4.7 %collective-permute-done.1 = f32[32,256]{1,0:T(8,128)S(1)} collective-permute-done((f32[32,256]{1,0:T(8,128)S(1)}, f32[32,256]{1,0:T(8,128)S(1)}, u32[]{:S(2)}, u32[]{:S(2)}) %collective-permute-start.1) | collective-permute-done | bytes 32800 | tf_op jit(solution)/shard_map/ppermute | solution.py:386
  166.4 0.6 fusion
  (3 shorter events, 0.1 us)
Async XLA Ops:
  0.6 41.7 %copy-start = (f32[512,256]{1,0:T(8,128)S(1)}, f32[512,256]{1,0:T(8,128)}, u32[]{:S(2)}) copy-start(f32[512,256]{1,0:T(8,128)} %users.5) | copy-start | bytes 1572868
  0.6 41.7 %copy-start.1 = (bf16[2,8,128,128]{3,2,1,0:T(8,128)(2,1)S(1)}, bf16[2,8,128,128]{3,2,1,0:T(8,128)(2,1)}, u32[]{:S(2)}) copy-start(bf16[2,8,128,128]{3,2,1,0:T(8,128)(2,1)} %values.3) | copy-start | bytes 1572868
  0.7 0.8 copy-start.2
  1.5 0.7 copy-start.7
  2.1 20.0 %copy-start.9 = (s32[2,1]{0,1:T(1,128)S(1)}, s32[2,1]{0,1:T(1,128)}, u32[]{:S(2)}) copy-start(s32[2,1]{0,1:T(1,128)} %param.14) | copy-start | bytes 28
  2.1 40.2 %copy-start.5 = (s32[2,8]{1,0:T(2,128)S(1)}, s32[2,8]{1,0:T(2,128)}, u32[]{:S(2)}) copy-start(s32[2,8]{1,0:T(2,128)} %rows.7) | copy-start | bytes 196
  2.1 40.2 %copy-start.6 = (s32[2,8]{1,0:T(2,128)S(1)}, s32[2,8]{1,0:T(2,128)}, u32[]{:S(2)}) copy-start(s32[2,8]{1,0:T(2,128)} %cols.7) | copy-start | bytes 196
  3.5 38.8 %all-to-all-start = ((bf16[48,17,2,128]{3,2,1,0:T(2,128)(2,1)}), bf16[48,17,2,128]{3,2,1,0:T(2,128)(2,1)S(1)}, u32[]{:S(2)}, u32[]{:S(2)}) async-start(bf16[48,17,2,128]{3,2,1,0:T(2,128)(2,1)} %bitcast), calls=%async_computation | async-start | bytes 835584 | tf_op jit(solution)/shard_map/all_to_all | solution.py:305
  44.7 25.6 %all-to-all-start.1 = ((f16[48,32,128]{2,1,0:T(8,128)(2,1)}), f16[48,32,128]{2,1,0:T(8,128)(2,1)S(1)}, u32[]{:S(2)}, u32[]{:S(2)}) async-start(f16[48,32,128]{2,1,0:T(8,128)(2,1)} %convert_element_type.28), calls=%async_computation.1 | async-start | bytes 786432 | tf_op jit(solution)/shard_map/all_to_all | solution.py:305
  51.2 19.3 %copy-start.3 = (f32[16,256]{1,0:T(8,128)S(1)}, f32[16,256]{1,0:T(8,128)}, u32[]{:S(2)}) copy-start(f32[16,256]{1,0:T(8,128)} %held.3) | copy-start | bytes 49156
  51.2 19.3 %copy-start.4 = (f32[16,256]{1,0:T(8,128)S(1)}, f32[16,256]{1,0:T(8,128)}, u32[]{:S(2)}) copy-start(f32[16,256]{1,0:T(8,128)} %accum.1) | copy-start | bytes 49156
  51.2 19.3 %copy-start.8 = (s32[2,4]{1,0:T(2,128)S(1)}, s32[2,4]{1,0:T(2,128)}, u32[]{:S(2)}) copy-start(s32[2,4]{1,0:T(2,128)} %ids.3) | copy-start | bytes 100
  126.2 28.4 %all-to-all-start.4 = ((f16[48,19,2,128]{3,2,1,0:T(2,128)(2,1)}), f16[48,19,2,128]{3,2,1,0:T(2,128)(2,1)S(1)}, u32[]{:S(2)}, u32[]{:S(2)}) async-start(f16[48,19,2,128]{3,2,1,0:T(2,128)(2,1)} %bitcast.4), calls=%async_computation.4 | async-start | bytes 933888 | tf_op jit(solution)/shard_map/all_to_all | solution.py:305
  132.9 21.8 %collective-permute-start = (f32[32,256]{1,0:T(8,128)S(1)}, f32[32,256]{1,0:T(8,128)S(1)}, u32[]{:S(2)}, u32[]{:S(2)}) collective-permute-start(f32[32,256]{1,0:T(8,128)S(1)} %get-tuple-element.28), channel_id=1, source_target_pairs={{48,0},{96,48},{144,96},{192,144},{240,192},{288,240},{336,288},{3... | collective-permute-start | bytes 98312 | tf_op jit(solution)/shard_map/ppermute | solution.py:379
  154.8 11.6 %collective-permute-start.1 = (f32[32,256]{1,0:T(8,128)S(1)}, f32[32,256]{1,0:T(8,128)S(1)}, u32[]{:S(2)}, u32[]{:S(2)}) collective-permute-start(f32[32,256]{1,0:T(8,128)S(1)} %shard_map.111), channel_id=1, source_target_pairs={{48,0},{96,48},{144,96},{192,144},{240,192},{288,240},{336,288},{3... | collective-permute-start | bytes 98312 | tf_op jit(solution)/shard_map/ppermute | solution.py:386

commit v5 on v4

--- a/solution.py
+++ b/solution.py
@@ -16,7 +16,7 @@
 BF16 = jnp.bfloat16
 F16 = jnp.float16
 
-GRAD_SCALE = 2.0**-6
+GRAD_SCALE = 2.0**-7
 ROOT_SCALE = 2.0**-9
 ITEM_SCALE = 2.0**12
 GRAM_SCALE = 2.0**12
@@ -26,6 +26,9 @@
 ROWS = 16
 PAIR = 2 * ROWS
 PACKED = 2 * LANES + 1
+
+GROUP = ("far", "near")
+INNER = ("far", "near", "pair")
 
 VMEM = pltpu.VMEM
 SMEM = pltpu.SMEM
@@ -110,61 +113,92 @@
         out[at + PAIR : at + stride, :] = counts
 
 
-def item_grads(step, users_bf, block, values, rows, cols, count, errors, scale, add):
-    slots, tile_u, tile_i = values.shape[1:]
-    live = count[step, 0]
+def item_grads(users_bf, block, values, rows, cols, live, errors, owned, scale, add):
+    slots, tile_u, tile_i = errors.shape
     for k in range(slots):
-        row = pl.multiple_of(rows[step, k] * tile_u, tile_u)
-        col = cols[step, k]
+        row = pl.multiple_of(rows(k) * tile_u, tile_u)
+        col = cols(k)
         user_tile = users_bf[pl.ds(row, tile_u), :]
         item_tile = block[pl.ds(pl.multiple_of(col * tile_i, tile_i), tile_i), :]
         scores = contract(user_tile, item_tile, (1, 1))
-        err = jnp.where(k < live, scores - values[step, k].astype(F32), 0.0).astype(BF16)
+        there = k < live if owned is None else owned & (k < live)
+        err = jnp.where(there, scores - values(k).astype(F32), 0.0).astype(BF16)
         errors[k] = err
         if scale is not None:
             err = err * jnp.asarray(scale, BF16)
         add(col, contract(err, user_tile, (0, 0)))
 
 
-def user_grads(step, block, rows, cols, errors, grad_users):
+def user_grads(block, rows, cols, errors, grad_users):
     slots, tile_u, tile_i = errors.shape
     grad_users[...] = jnp.zeros_like(grad_users)
     for k in range(slots):
-        row = pl.multiple_of(rows[step, k] * tile_u, tile_u)
-        col = pl.multiple_of(cols[step, k] * tile_i, tile_i)
+        row = pl.multiple_of(rows(k) * tile_u, tile_u)
+        col = pl.multiple_of(cols(k) * tile_i, tile_i)
         grad_users[pl.ds(row, tile_u), :] += contract(errors[k], block[pl.ds(col, tile_i), :], (1, 0))
 
 
-def first_kernel(got, users, values, rows, cols, count, sums, block, errors, users_bf):
+def at_step(ref, step):
+    return lambda k: ref[step, k]
+
+
+def from_list(ref, first):
+    return lambda k: ref[first + k]
+
+
+def pair_rows(chunk, side):
+    return pl.ds(pl.multiple_of(chunk * 2 * ROWS + side * ROWS, ROWS), ROWS)
+
+
+def first_kernel(
+    got, users, their_users, values, their_values, rows, cols, count, theirs,
+    sums, block, errors, their_errors, users_bf, grads,
+):
     stride = PAIR + 2
-    for chunk in range(block.shape[0] // ROWS):
-        to, at = chunk * ROWS, chunk * stride
-        block[to : to + ROWS, :LANES] = got[at : at + ROWS, :]
-        block[to : to + ROWS, LANES:] = got[at + ROWS : at + PAIR, :]
+    chunks = got.shape[0] // stride
+    side = lax.axis_index("pair")
+    slots, tile_u, tile_i = errors.shape
+    block[...] = jnp.zeros_like(block)
+    for chunk in range(chunks):
+        at = chunk * stride
+        block[pair_rows(chunk, side), :LANES] = got[at : at + ROWS, :]
+        block[pair_rows(chunk, side), LANES:] = got[at + ROWS : at + PAIR, :]
     users_bf[...] = users[...].astype(BF16)
-    sums[...] = jnp.zeros_like(sums)
+    grads[...] = jnp.zeros_like(grads)
+    lane = lax.broadcasted_iota(jnp.int32, (tile_u, tile_i), 1)
+    owned = lax.rem(lax.div(lane, ROWS), 2) == side
 
     def add(col, part):
-        chunks = part.shape[0] // ROWS
-        at = pl.ds(col * chunks, chunks)
-        sums[at, 0:ROWS, :] += part[:, :LANES].reshape(chunks, ROWS, LANES)
-        sums[at, ROWS:PAIR, :] += part[:, LANES:].reshape(chunks, ROWS, LANES)
-
-    item_grads(0, users_bf, block, values, rows, cols, count, errors, GRAD_SCALE, add)
-
-
-def first_users_kernel(got, block, users, rows, cols, errors, users_out, piece_out, counts, packed, pieces, grad_users):
+        at = pl.multiple_of(col * part.shape[0], part.shape[0])
+        grads[pl.ds(at, part.shape[0]), :] += part
+
+    item_grads(
+        users_bf, block, lambda k: values[0, k], at_step(rows, 0), at_step(cols, 0), count[0, 0],
+        errors, owned, GRAD_SCALE, add,
+    )
+    item_grads(
+        their_users, block, lambda k: their_values[k], from_list(theirs, 0), from_list(theirs, slots),
+        theirs[2 * slots], their_errors, owned, GRAD_SCALE, add,
+    )
+    for chunk in range(chunks):
+        sums[chunk] = halves(grads[pair_rows(chunk, side), :])
+
+
+def first_users_kernel(
+    got, block, users, rows, cols, errors, theirs, their_errors,
+    users_out, their_grads, piece_out, their_piece, counts, packed, pieces, mine, grad_users,
+):
     stride = PAIR + 2
-    chunks = block.shape[0] // ROWS
-    user_grads(0, block, rows, cols, errors, grad_users)
-    users_out[...] = users[...] - LR_USER * grad_users[...]
+    chunks = got.shape[0] // stride
+    side = lax.axis_index("pair")
     for chunk in range(chunks):
         at = chunk * stride + PAIR
         counts[chunk : chunk + 1, :] = got[at : at + 2, :].astype(F32)[0:1]
+        mine[chunk * ROWS : (chunk + 1) * ROWS, :] = block[pair_rows(chunk, side), :]
     shape = (chunks, ROWS, LANES)
     own = lax.broadcasted_iota(jnp.int32, shape, 1) == lax.broadcasted_iota(jnp.int32, shape, 2)
     weight = jnp.sum(jnp.where(own, counts[...][:, None, :], 0.0), axis=2, keepdims=True)
-    plain = block[...]
+    plain = mine[...]
     left = (plain[:, :LANES].astype(F32).reshape(shape) * weight).reshape(-1, LANES)
     right = (plain[:, LANES:].astype(F32).reshape(shape) * weight).reshape(-1, LANES)
     high, low = split(jnp.concatenate([left, right], axis=1))
@@ -174,10 +208,17 @@
         jnp.concatenate([plain, plain], axis=0),
         GRAM_STRATUM_SCALE,
     )
-    piece = packed.shape[0] // chunks
-    for chunk in range(chunks):
-        pieces[chunk, 0:piece, :] = packed[chunk * piece : (chunk + 1) * piece, :]
-    piece_out[...] = pieces[lax.axis_index("inner")]
+    devices = pieces.shape[0]
+    piece = packed.shape[0] // devices
+    for device in range(devices):
+        pieces[device, 0:piece, :] = packed[device * piece : (device + 1) * piece, :]
+    me = lax.axis_index(INNER)
+    piece_out[...] = pieces[me]
+    their_piece[...] = pieces[me + 1 - 2 * side]
+    slots = errors.shape[0]
+    user_grads(block, from_list(theirs, 0), from_list(theirs, slots), their_errors, their_grads)
+    user_grads(block, at_step(rows, 0), at_step(cols, 0), errors, grad_users)
+    users_out[...] = users[...] - LR_USER * grad_users[...]
 
 
 def update(held, accum, gradient):
@@ -195,19 +236,19 @@
     return counts
 
 
-def item_kernel(got, held, accum, gram_piece, ids, state, out):
+def item_kernel(got, held, accum, gram_piece, their_piece, ids, state, out):
     strata = out.shape[0]
     gradient = widths(jnp.sum(got[...], axis=0) * (1.0 / GRAD_SCALE))
     new, state[ROWS:, :] = update(held[...], accum[...], gradient)
     state[0:ROWS, :] = new
     items = halves(new.astype(BF16).astype(F32)) * ITEM_SCALE
-    sent = jnp.concatenate([items, pick_counts(ids, 1), gram_piece[...]], axis=0)
+    sent = jnp.concatenate([items, pick_counts(ids, 1), gram_piece[...] + their_piece[...]], axis=0)
     out[...] = jnp.broadcast_to(sent[None], (strata,) + sent.shape)
 
 
 def gather_kernel(total, met, out, packed):
     strata = met.shape[0]
-    chunks = lax.axis_size("inner")
+    chunks = lax.axis_size(INNER)
     piece = packed.shape[0] // chunks
     stride = PAIR + 2 * piece
     after = lax.rem(lax.axis_index("stratum") + 1, strata)
@@ -233,7 +274,7 @@
 
 
 def second_kernel(
-    total, got, users, mid, values, rows, cols, count, sums, mid_out, block, errors, packed, users_bf, grads
+    total, got, users, mid, rest, values, rows, cols, count, sums, mid_out, block, errors, packed, users_bf, grads
 ):
     chunks = block.shape[0] // ROWS
     piece = packed.shape[0] // chunks
@@ -246,7 +287,8 @@
         packed[chunk * piece : (chunk + 1) * piece, :] = got[at + PAIR : at + PAIR + piece, :]
         full = full + got[at + PAIR + piece : at + stride, :]
     gram = whole_gram(packed, 1.0 / GRAM_SCALE)
-    now = mid[...] - (LR_USER * LAMBDA) * times_gram(users[...], gram)
+    part = mid[...] - LR_USER * rest[...]
+    now = part - (LR_USER * LAMBDA) * times_gram(users[...], gram)
     mid_out[...] = now
     users_bf[...] = now.astype(BF16)
     grads[...] = jnp.zeros_like(grads)
@@ -255,7 +297,10 @@
         at = pl.multiple_of(col * part.shape[0], part.shape[0])
         grads[pl.ds(at, part.shape[0]), :] += part
 
-    item_grads(1, users_bf, block, values, rows, cols, count, errors, None, add)
+    item_grads(
+        users_bf, block, lambda k: values[1, k], at_step(rows, 1), at_step(cols, 1), count[1, 0],
+        errors, None, None, add,
+    )
     full = full * (GRAM_SCALE / GRAM_INNER_SCALE / total)
     for chunk in range(chunks):
         at = chunk * (PAIR + piece)
@@ -266,7 +311,7 @@
 
 
 def second_users_kernel(block, now, rows, cols, errors, users_out, grad_users):
-    user_grads(1, block, rows, cols, errors, grad_users)
+    user_grads(block, at_step(rows, 1), at_step(cols, 1), errors, grad_users)
     users_out[...] = now[...] - LR_USER * grad_users[...]
 
 
@@ -297,7 +342,7 @@
         in_specs=specs,
         out_specs=jax.tree.map(lambda _: pl.BlockSpec(memory_space=VMEM), out_shape),
         scratch_shapes=scratch,
-        compiler_params=pltpu.CompilerParams(vmem_limit_bytes=40 * 2**20),
+        compiler_params=pltpu.CompilerParams(vmem_limit_bytes=44 * 2**20),
     )(*args)
 
 
@@ -305,16 +350,21 @@
     return lax.all_to_all(x, axis, 0, 0, tiled=True)
 
 
-def chunks_exchanged(flat, chunks):
-    paired = flat.reshape(chunks, -1, 2, LANES)
-    return exchanged(paired, "inner").reshape(flat.shape)
+def chunks_exchanged(flat, axis):
+    paired = flat.reshape(lax.axis_size(axis), -1, 2, LANES)
+    return exchanged(paired, axis).reshape(flat.shape)
+
+
+def swapped(x):
+    return lax.ppermute(x, "pair", [(0, 1), (1, 0)])
 
 
 def shards(
     user_factors, item_factors, item_accum, tile_values, tile_rows, tile_cols, tile_count, neg_ids
 ):
     strata = lax.axis_size("stratum")
-    inners = lax.axis_size("inner")
+    inners = lax.axis_size(INNER)
+    group = lax.axis_size(GROUP)
     rank = item_factors.shape[1]
     total = float(strata * inners * neg_ids.shape[1])
     piece = piece_rows(inners)
@@ -329,35 +379,46 @@
     state_shape = shape((PAIR, rank), F32)
     block_shape = shape((inners * ROWS, rank), BF16)
     errors_shape = shape(tile_values.shape[1:], BF16)
+    piece_shape = shape((padded, LANES), F32)
     packed = pltpu.VMEM((inners * piece, LANES), F32)
 
-    sent = call(start_kernel, shape((inners * (PAIR + 2), LANES), BF16), [vm, sm], item_factors, neg_ids)
-    got = chunks_exchanged(sent, inners)
-    sums, block, errors = call(
+    sent = call(start_kernel, shape((group * (PAIR + 2), LANES), BF16), [vm, sm], item_factors, neg_ids)
+    lists = jnp.concatenate([tile_rows[0], tile_cols[0], tile_count[0]])
+    sent, near_users, near_values, lists = lax.optimization_barrier(
+        (sent, user_factors.astype(BF16), tile_values[0], lists)
+    )
+    got = chunks_exchanged(sent, GROUP)
+    theirs = swapped(lists)
+    their_users = swapped(near_users)
+    their_values = swapped(near_values)
+    sums, block, errors, their_errors = call(
         first_kernel,
-        (shape((inners, PAIR, LANES), F32), block_shape, errors_shape),
-        [vm, vm, vm, sm, sm, sm],
-        got, user_factors, tile_values, tile_rows, tile_cols, tile_count,
-        scratch=[users_bf],
-    )
-    sums = exchanged(sums.astype(F16), "inner").astype(F32)
-    mid, gram_piece = call(
+        (shape((group, PAIR, LANES), F32), block_shape, errors_shape, errors_shape),
+        [vm, vm, vm, vm, vm, sm, sm, sm, sm],
+        got, user_factors, their_users, tile_values, their_values, tile_rows, tile_cols, tile_count, theirs,
+        scratch=[users_bf, pltpu.VMEM(block_shape.shape, F32)],
+    )
+    sums = exchanged(sums.astype(F16), GROUP).astype(F32)
+    mid, rest, gram_piece, their_piece = call(
         first_users_kernel,
-        (users_shape, shape((padded, LANES), F32)),
-        [vm, vm, vm, sm, sm, vm],
-        got, block, user_factors, tile_rows, tile_cols, errors,
+        (users_shape, users_shape, piece_shape, piece_shape),
+        [vm, vm, vm, sm, sm, vm, sm, vm],
+        got, block, user_factors, tile_rows, tile_cols, errors, theirs, their_errors,
         scratch=[
-            pltpu.VMEM((inners, LANES), F32),
+            pltpu.VMEM((group, LANES), F32),
             packed,
             pltpu.VMEM((inners, padded, LANES), F32),
+            pltpu.VMEM((group * ROWS, rank), BF16),
             users_f32,
         ],
     )
+    their_piece = swapped(their_piece)
+    rest = swapped(rest)
     state, sent = call(
         item_kernel,
         (state_shape, shape((strata, PAIR + 8 + padded, LANES), F32)),
-        [vm, vm, vm, vm, sm],
-        sums, item_factors, item_accum, gram_piece, neg_ids,
+        [vm, vm, vm, vm, vm, sm],
+        sums, item_factors, item_accum, gram_piece, their_piece, neg_ids,
     )
     met = exchanged(sent.astype(F16), "stratum").astype(F32)
     sent = call(
@@ -367,17 +428,17 @@
         met,
         scratch=[packed],
     ).astype(F16)
-    got = chunks_exchanged(sent, inners).astype(F32)
+    got = chunks_exchanged(sent, INNER).astype(F32)
     sums, mid, block, errors = call(
         functools.partial(second_kernel, total),
         (shape((inners * (PAIR + piece), LANES), F32), users_shape, block_shape, errors_shape),
-        [vm, vm, vm, vm, sm, sm, sm],
-        got, user_factors, mid, tile_values, tile_rows, tile_cols, tile_count,
+        [vm, vm, vm, vm, vm, sm, sm, sm],
+        got, user_factors, mid, rest, tile_values, tile_rows, tile_cols, tile_count,
         scratch=[packed, users_bf, pltpu.VMEM(block_shape.shape, F32)],
     )
     sums, state = lax.optimization_barrier((sums.astype(F16), state))
     state = lax.ppermute(state, "stratum", onward)
-    got = chunks_exchanged(sums, inners).astype(F32)
+    got = chunks_exchanged(sums, INNER).astype(F32)
     users = call(
         second_users_kernel, users_shape, [vm, vm, sm, sm, vm],
         block, mid, tile_rows, tile_cols, errors, scratch=[users_f32],
@@ -392,16 +453,21 @@
 
 
 def solution(mesh):
-    devices = P(("stratum", "inner"), None)
-    slots = P(None, ("stratum", "inner"))
+    strata, inners = mesh.devices.shape
+    fine = jax.sharding.Mesh(
+        mesh.devices.reshape(strata, inners // 4, 2, 2), ("stratum",) + INNER
+    )
+    every = ("stratum",) + INNER
+    devices = P(every, None)
+    slots = P(None, every)
     return jax.shard_map(
         shards,
-        mesh=mesh,
+        mesh=fine,
         in_specs=(
             devices,
             devices,
             devices,
-            P(None, ("stratum", "inner"), None, None),
+            P(None, every, None, None),
             slots,
             slots,
             slots,

time: 168 us -> 167 us (level)
  blocking collectives: 50.5 us -> 20.6 us
  starting transfers between devices: 39.6 us -> 67.7 us
  waiting for transfers between devices: 61.1 us -> 59.2 us
  other arithmetic: 2.01 us -> 3.85 us
    all_to_all x2 -> x1, blocking collectives: 50.5 us -> 20.6 us  [exchanged(): return lax.all_to_all(x, axis, 0, 0, tiled=True)]
    ppermute x0 -> x5, starting transfers between devices: none -> 14.2 us  [swapped(): return lax.ppermute(x, 'pair', [(0, 1), (1, 0)])]
    all_to_all x3 -> x4, starting transfers between devices: 31.7 us -> 45.7 us  [exchanged(): return lax.all_to_all(x, axis, 0, 0, tiled=True)]
    all_to_all x3 -> x4, waiting for transfers between devices: 56.4 us -> 46.5 us  [exchanged(): return lax.all_to_all(x, axis, 0, 0, tiled=True)]
    ppermute x0 -> x5, waiting for transfers between devices: none -> 8.1 us  [swapped(): return lax.ppermute(x, 'pair', [(0, 1), (1, 0)])]
  transfers between devices with their start and end apart: 5 -> 11, of which waited for: 4 -> 5; matrix products, arithmetic and copies ran while one was open for 0% -> 0% of each run, Pallas kernels for 2% -> 2%
where the time goes in v5:
time: 167 us; the launch traced here: 166 us
  starting transfers between devices  67.7 us (41%)
  waiting for transfers between devices  59.2 us (35%)
  blocking collectives  20.6 us (12%)
  Pallas kernels  11.1 us (7%)
  other arithmetic  3.85 us (2%)
  local copies, waits for them, and re-layouts  2.59 us (2%)
    all_to_all x4, waiting for transfers between devices, exchanged(): return lax.all_to_all(x, axis, 0, 0, tiled=True)  46.5 us
    all_to_all x4, starting transfers between devices, exchanged(): return lax.all_to_all(x, axis, 0, 0, tiled=True)  45.7 us
    all_to_all x1, blocking collectives, exchanged(): return lax.all_to_all(x, axis, 0, 0, tiled=True)  20.6 us
    ppermute x5, starting transfers between devices, swapped(): return lax.ppermute(x, 'pair', [(0, 1), (1, 0)])  14.2 us
    pallas_call x9, Pallas kernels, call(): pl.pallas_call(kernel, out_shape=out_shape, in_specs=specs, out_specs=jax...  11.1 us
    ppermute x5, waiting for transfers between devices, swapped(): return lax.ppermute(x, 'pair', [(0, 1), (1, 0)])  8.1 us
    ppermute x2, starting transfers between devices, shards(): state = lax.ppermute(state, 'stratum', onward)  7.86 us
    ppermute x2, waiting for transfers between devices, shards(): state = lax.ppermute(state, 'stratum', onward)  4.61 us
  transfers between devices with their start and end apart: 11, of which 5 were waited for; matrix products, arithmetic and copies ran while one was open for 0% of the time, Pallas kernels for 2%

profile of v5, /device:TPU:7, one launch (start us, length us, event | category | flops | bytes accessed | tf_op | source)
XLA Modules:
  0.0 166.1 jit_solution(14419396400178468416)
XLA Ops:
  0.6 0.0 copy-start
  0.7 0.0 copy-start.4
  0.7 1.0 slice_bitcast_fusion
  1.8 1.1 convert_element_type.31
  2.9 1.3 shard_map.103
  4.1 0.1 pad_add_fusion
  4.3 17.1 %all-to-all-start = ((bf16[24,17,2,128]{3,2,1,0:T(2,128)(2,1)}), bf16[24,17,2,128]{3,2,1,0:T(2,128)(2,1)S(1)}, u32[]{:S(2)}, u32[]{:S(2)}) async-start(bf16[24,17,2,128]{3,2,1,0:T(2,128)(2,1)} %bitcast.4), calls=%async_computation | async-start | bytes 417792 | tf_op jit(solution)/shard_map/all_to_all | solution.py:350
  21.4 3.2 %collective-permute-start = (bf16[512,256]{1,0:T(8,128)(2,1)S(1)}, bf16[512,256]{1,0:T(8,128)(2,1)S(1)}, u32[]{:S(2)}, u32[]{:S(2)}) collective-permute-start(bf16[512,256]{1,0:T(8,128)(2,1)S(1)} %convert_element_type.31), channel_id=1, source_target_pairs={{0,1},{1,0},{2,3},{3,2},{4,5},{5,4},{6,7},{7,6},{8,9},{9,8},{10,11... | collective-permute-start | bytes 786440 | tf_op jit(solution)/shard_map/ppermute | solution.py:359
  24.6 2.1 %collective-permute-start.1 = (bf16[8,128,128]{2,1,0:T(8,128)(2,1)S(1)}, bf16[8,128,128]{2,1,0:T(8,128)(2,1)S(1)}, u32[]{:S(2)}, u32[]{:S(2)}) collective-permute-start(bf16[8,128,128]{2,1,0:T(8,128)(2,1)S(1)} %slice_bitcast_fusion), channel_id=1, source_target_pairs={{0,1},{1,0},{2,3},{3,2},{4,5},{5,4},{6,7},{7,6},{8,9},{9,8},{10,11... | collective-permute-start | bytes 786440 | tf_op jit(solution)/shard_map/ppermute | solution.py:359
  26.7 3.2 %collective-permute-start.2 = (s32[17]{0:T(128)S(1)}, s32[17]{0:T(128)S(1)}, u32[]{:S(2)}, u32[]{:S(2)}) collective-permute-start(s32[17]{0:T(128)S(1)} %pad_add_fusion), channel_id=1, source_target_pairs={{0,1},{1,0},{2,3},{3,2},{4,5},{5,4},{6,7},{7,6},{8,9},{9,8},{10,11... | collective-permute-start | bytes 212 | tf_op jit(solution)/shard_map/ppermute | solution.py:359
  29.9 0.1 copy.11.count
  30.0 8.1 %collective-permute-done.2.theirs = s32[17]{0:T(128)S(1)} collective-permute-done((s32[17]{0:T(128)S(1)}, s32[17]{0:T(128)S(1)}, u32[]{:S(2)}, u32[]{:S(2)}) %collective-permute-start.2) | collective-permute-done | bytes 100 | tf_op jit(solution)/shard_map/ppermute | solution.py:359
  38.1 0.0 collective-permute-done.their_users
  38.1 0.0 collective-permute-done.1.their_values
  38.1 0.0 all-to-all-done
  38.1 1.8 %shard_map.104 = (f32[24,32,128]{2,1,0:T(8,128)S(1)}, bf16[768,256]{1,0:T(8,128)(2,1)S(1)}, bf16[8,128,128]{2,1,0:T(8,128)(2,1)S(1)}, bf16[8,128,128]{2,1,0:T(8,128)(2,1)S(1)}) custom-call(bf16[816,128]{1,0:T(8,128)(2,1)S(1)} %bitcast.16, f32[512,256]{1,0:T(8,128)S(1)} %copy-done, bf16[512,256]{1,0:T(8,128)(2,1)S(1)} %collective-permute-done.their_users, ...), custom_call_target="tpu_custom_call" | custom-call | tf_op jit(solution)/shard_map/pallas_call | solution.py:339
  39.9 0.7 convert_element_type.32
  40.6 10.5 %all-to-all-start.1 = ((f16[24,32,128]{2,1,0:T(8,128)(2,1)}), f16[24,32,128]{2,1,0:T(8,128)(2,1)S(1)}, u32[]{:S(2)}, u32[]{:S(2)}) async-start(f16[24,32,128]{2,1,0:T(8,128)(2,1)} %convert_element_type.32), calls=%async_computation.1 | async-start | bytes 393216 | tf_op jit(solution)/shard_map/all_to_all | solution.py:350
  51.2 0.0 copy-start.5
  51.2 1.4 shard_map.105
  52.6 0.0 copy-start.7
  52.6 0.8 copy-done.7
  53.4 2.7 %collective-permute-start.3 = (f32[8,128]{1,0:T(8,128)S(1)}, f32[8,128]{1,0:T(8,128)S(1)}, u32[]{:S(2)}, u32[]{:S(2)}) collective-permute-start(f32[8,128]{1,0:T(8,128)S(1)} %get-tuple-element.32), channel_id=1, source_target_pairs={{0,1},{1,0},{2,3},{3,2},{4,5},{5,4},{6,7},{7,6},{8,9},{9,8},{10,11... | collective-permute-start | bytes 12296 | tf_op jit(solution)/shard_map/ppermute | solution.py:359
  56.1 6.6 %all-to-all-done.1 = f16[24,32,128]{2,1,0:T(8,128)(2,1)S(1)} async-done(((f16[24,32,128]{2,1,0:T(8,128)(2,1)}), f16[24,32,128]{2,1,0:T(8,128)(2,1)S(1)}, u32[]{:S(2)}, u32[]{:S(2)}) %all-to-all-start.1) | async-done | bytes 196640 | tf_op jit(solution)/shard_map/all_to_all | solution.py:350
  62.7 0.0 collective-permute-done.3.their_piece
  62.8 0.6 shard_map.106
  63.4 20.6 %all_to_all.25 = f16[16,48,128]{2,1,0:T(8,128)(2,1)S(1)} all-to-all(f16[16,48,128]{2,1,0:T(8,128)(2,1)S(1)} %convert_element_type.34), channel_id=1, replica_groups=mesh['stratum'=16,'far'=12,'near'=2,'pair'=2] {'stratum'}, dimensions={0} | all-to-all | bytes 393216 | tf_op jit(solution)/shard_map/all_to_all | solution.py:350
  84.1 0.5 shard_map.107
  84.6 0.0 copy-start.8
  84.6 0.9 convert_element_type.36
  85.5 7.9 %all-to-all-start.3 = ((f16[48,22,2,128]{3,2,1,0:T(2,128)(2,1)}), f16[48,22,2,128]{3,2,1,0:T(2,128)(2,1)S(1)}, u32[]{:S(2)}, u32[]{:S(2)}) async-start(f16[48,22,2,128]{3,2,1,0:T(2,128)(2,1)} %bitcast.6), calls=%async_computation.3 | async-start | bytes 1081344 | tf_op jit(solution)/shard_map/all_to_all | solution.py:350
  93.4 3.0 %collective-permute-start.4 = (f32[512,256]{1,0:T(8,128)S(1)}, f32[512,256]{1,0:T(8,128)S(1)}, u32[]{:S(2)}, u32[]{:S(2)}) collective-permute-start(f32[512,256]{1,0:T(8,128)S(1)} %copy-done.8), channel_id=1, source_target_pairs={{0,1},{1,0},{2,3},{3,2},{4,5},{5,4},{6,7},{7,6},{8,9},{9,8},{10,11... | collective-permute-start | bytes 1572872 | tf_op jit(solution)/shard_map/ppermute | solution.py:359
  96.4 21.3 %all-to-all-done.3 = f16[48,22,2,128]{3,2,1,0:T(2,128)(2,1)S(1)} async-done(((f16[48,22,2,128]{3,2,1,0:T(2,128)(2,1)}), f16[48,22,2,128]{3,2,1,0:T(2,128)(2,1)S(1)}, u32[]{:S(2)}, u32[]{:S(2)}) %all-to-all-start.3) | async-done | bytes 540704 | tf_op jit(solution)/shard_map/all_to_all | solution.py:350
  117.8 0.1 convert.3.got
  117.8 0.0 collective-permute-done.4.rest
  117.9 3.1 %shard_map.108 = (f32[1824,128]{1,0:T(8,128)S(1)}, f32[512,256]{1,0:T(8,128)S(1)}, bf16[768,256]{1,0:T(8,128)(2,1)S(1)}, bf16[8,128,128]{2,1,0:T(8,128)(2,1)S(1)}) custom-call(f32[2112,128]{1,0:T(8,128)S(1)} %convert.3.got, f32[512,256]{1,0:T(8,128)S(1)} %copy-done, f32[512,256]{1,0:T(8,128)S(1)} %get-tuple-element.34.mid, ...), custom_call_target="tpu_custom_call" | custom-call | tf_op jit(solution)/shard_map/pallas_call | solution.py:339
  121.0 0.8 convert_element_type.39
  121.8 10.1 %all-to-all-start.4 = ((f16[48,19,2,128]{3,2,1,0:T(2,128)(2,1)}), f16[48,19,2,128]{3,2,1,0:T(2,128)(2,1)S(1)}, u32[]{:S(2)}, u32[]{:S(2)}) async-start(f16[48,19,2,128]{3,2,1,0:T(2,128)(2,1)} %bitcast.8), calls=%async_computation.4 | async-start | bytes 933888 | tf_op jit(solution)/shard_map/all_to_all | solution.py:350
  132.0 3.1 %collective-permute-start.5 = (f32[32,256]{1,0:T(8,128)S(1)}, f32[32,256]{1,0:T(8,128)S(1)}, u32[]{:S(2)}, u32[]{:S(2)}) collective-permute-start(f32[32,256]{1,0:T(8,128)S(1)} %get-tuple-element.42), channel_id=1, source_target_pairs={{48,0},{96,48},{144,96},{192,144},{240,192},{288,240},{336,288},{3... | collective-permute-start | bytes 98312 | tf_op jit(solution)/shard_map/ppermute | solution.py:440
  135.1 18.6 %all-to-all-done.4 = f16[48,19,2,128]{3,2,1,0:T(2,128)(2,1)S(1)} async-done(((f16[48,19,2,128]{3,2,1,0:T(2,128)(2,1)}), f16[48,19,2,128]{3,2,1,0:T(2,128)(2,1)S(1)}, u32[]{:S(2)}, u32[]{:S(2)}) %all-to-all-start.4) | async-done | bytes 466976 | tf_op jit(solution)/shard_map/all_to_all | solution.py:350
  153.7 0.1 convert.2.got
  153.7 0.0 collective-permute-done.5.state
  153.7 0.1 shard_map.111
  153.8 4.8 %collective-permute-start.6 = (f32[32,256]{1,0:T(8,128)S(1)}, f32[32,256]{1,0:T(8,128)S(1)}, u32[]{:S(2)}, u32[]{:S(2)}) collective-permute-start(f32[32,256]{1,0:T(8,128)S(1)} %shard_map.111), channel_id=1, source_target_pairs={{48,0},{96,48},{144,96},{192,144},{240,192},{288,240},{336,288},{3... | collective-permute-start | bytes 98312 | tf_op jit(solution)/shard_map/ppermute | solution.py:447
  158.6 0.9 shard_map.109.users
  159.6 1.3 shard_map.110
  160.8 4.6 %collective-permute-done.6 = f32[32,256]{1,0:T(8,128)S(1)} collective-permute-done((f32[32,256]{1,0:T(8,128)S(1)}, f32[32,256]{1,0:T(8,128)S(1)}, u32[]{:S(2)}, u32[]{:S(2)}) %collective-permute-start.6) | collective-permute-done | bytes 32800 | tf_op jit(solution)/shard_map/ppermute | solution.py:447
  165.5 0.6 fusion
  (18 shorter events, 0.1 us)
Async XLA Ops:
  0.6 37.5 %copy-start.1 = (bf16[2,8,128,128]{3,2,1,0:T(8,128)(2,1)S(1)}, bf16[2,8,128,128]{3,2,1,0:T(8,128)(2,1)}, u32[]{:S(2)}) copy-start(bf16[2,8,128,128]{3,2,1,0:T(8,128)(2,1)} %values.3) | copy-start | bytes 1572868
  0.6 37.5 %copy-start = (f32[512,256]{1,0:T(8,128)S(1)}, f32[512,256]{1,0:T(8,128)}, u32[]{:S(2)}) copy-start(f32[512,256]{1,0:T(8,128)} %users.5) | copy-start | bytes 1572868
  0.7 2.2 %copy-start.4 = (s32[2,8]{1,0:T(2,128)S(1)}, s32[2,8]{1,0:T(2,128)}, u32[]{:S(2)}) copy-start(s32[2,8]{1,0:T(2,128)} %cols.7) | copy-start | bytes 196
  0.7 2.2 %copy-start.3 = (s32[2,8]{1,0:T(2,128)S(1)}, s32[2,8]{1,0:T(2,128)}, u32[]{:S(2)}) copy-start(s32[2,8]{1,0:T(2,128)} %rows.7) | copy-start | bytes 196
  0.7 2.2 %copy-start.6 = (s32[2,4]{1,0:T(2,128)S(1)}, s32[2,4]{1,0:T(2,128)}, u32[]{:S(2)}) copy-start(s32[2,4]{1,0:T(2,128)} %ids.3) | copy-start | bytes 100
  0.7 2.2 %copy-start.2 = (f32[16,256]{1,0:T(8,128)S(1)}, f32[16,256]{1,0:T(8,128)}, u32[]{:S(2)}) copy-start(f32[16,256]{1,0:T(8,128)} %held.3) | copy-start | bytes 49156
  0.7 3.5 %copy-start.9 = (s32[2,1]{0,1:T(1,128)S(1)}, s32[2,1]{0,1:T(1,128)}, u32[]{:S(2)}) copy-start(s32[2,1]{0,1:T(1,128)} %param.14) | copy-start | bytes 28
  4.3 33.8 %all-to-all-start = ((bf16[24,17,2,128]{3,2,1,0:T(2,128)(2,1)}), bf16[24,17,2,128]{3,2,1,0:T(2,128)(2,1)S(1)}, u32[]{:S(2)}, u32[]{:S(2)}) async-start(bf16[24,17,2,128]{3,2,1,0:T(2,128)(2,1)} %bitcast.4), calls=%async_computation | async-start | bytes 417792 | tf_op jit(solution)/shard_map/all_to_all | solution.py:350
  21.4 16.7 %collective-permute-start = (bf16[512,256]{1,0:T(8,128)(2,1)S(1)}, bf16[512,256]{1,0:T(8,128)(2,1)S(1)}, u32[]{:S(2)}, u32[]{:S(2)}) collective-permute-start(bf16[512,256]{1,0:T(8,128)(2,1)S(1)} %convert_element_type.31), channel_id=1, source_target_pairs={{0,1},{1,0},{2,3},{3,2},{4,5},{5,4},{6,7},{7,6},{8,9},{9,8},{10,11... | collective-permute-start | bytes 786440 | tf_op jit(solution)/shard_map/ppermute | solution.py:359
  24.6 13.5 %collective-permute-start.1 = (bf16[8,128,128]{2,1,0:T(8,128)(2,1)S(1)}, bf16[8,128,128]{2,1,0:T(8,128)(2,1)S(1)}, u32[]{:S(2)}, u32[]{:S(2)}) collective-permute-start(bf16[8,128,128]{2,1,0:T(8,128)(2,1)S(1)} %slice_bitcast_fusion), channel_id=1, source_target_pairs={{0,1},{1,0},{2,3},{3,2},{4,5},{5,4},{6,7},{7,6},{8,9},{9,8},{10,11... | collective-permute-start | bytes 786440 | tf_op jit(solution)/shard_map/ppermute | solution.py:359
  26.7 11.4 %collective-permute-start.2 = (s32[17]{0:T(128)S(1)}, s32[17]{0:T(128)S(1)}, u32[]{:S(2)}, u32[]{:S(2)}) collective-permute-start(s32[17]{0:T(128)S(1)} %pad_add_fusion), channel_id=1, source_target_pairs={{0,1},{1,0},{2,3},{3,2},{4,5},{5,4},{6,7},{7,6},{8,9},{9,8},{10,11... | collective-permute-start | bytes 212 | tf_op jit(solution)/shard_map/ppermute | solution.py:359
  40.6 22.1 %all-to-all-start.1 = ((f16[24,32,128]{2,1,0:T(8,128)(2,1)}), f16[24,32,128]{2,1,0:T(8,128)(2,1)S(1)}, u32[]{:S(2)}, u32[]{:S(2)}) async-start(f16[24,32,128]{2,1,0:T(8,128)(2,1)} %convert_element_type.32), calls=%async_computation.1 | async-start | bytes 393216 | tf_op jit(solution)/shard_map/all_to_all | solution.py:350
  51.2 11.6 %copy-start.5 = (f32[16,256]{1,0:T(8,128)S(1)}, f32[16,256]{1,0:T(8,128)}, u32[]{:S(2)}) copy-start(f32[16,256]{1,0:T(8,128)} %accum.1) | copy-start | bytes 49156
  52.6 0.8 copy-start.7
  53.4 9.3 %collective-permute-start.3 = (f32[8,128]{1,0:T(8,128)S(1)}, f32[8,128]{1,0:T(8,128)S(1)}, u32[]{:S(2)}, u32[]{:S(2)}) collective-permute-start(f32[8,128]{1,0:T(8,128)S(1)} %get-tuple-element.32), channel_id=1, source_target_pairs={{0,1},{1,0},{2,3},{3,2},{4,5},{5,4},{6,7},{7,6},{8,9},{9,8},{10,11... | collective-permute-start | bytes 12296 | tf_op jit(solution)/shard_map/ppermute | solution.py:359
  84.6 8.8 %copy-start.8 = (f32[512,256]{1,0:T(8,128)S(1)}, f32[512,256]{1,0:T(8,128)}, u32[]{:S(2)}) copy-start(f32[512,256]{1,0:T(8,128)} %copy-done.7) | copy-start | bytes 1572868
  85.5 32.3 %all-to-all-start.3 = ((f16[48,22,2,128]{3,2,1,0:T(2,128)(2,1)}), f16[48,22,2,128]{3,2,1,0:T(2,128)(2,1)S(1)}, u32[]{:S(2)}, u32[]{:S(2)}) async-start(f16[48,22,2,128]{3,2,1,0:T(2,128)(2,1)} %bitcast.6), calls=%async_computation.3 | async-start | bytes 1081344 | tf_op jit(solution)/shard_map/all_to_all | solution.py:350
  93.4 24.5 %collective-permute-start.4 = (f32[512,256]{1,0:T(8,128)S(1)}, f32[512,256]{1,0:T(8,128)S(1)}, u32[]{:S(2)}, u32[]{:S(2)}) collective-permute-start(f32[512,256]{1,0:T(8,128)S(1)} %copy-done.8), channel_id=1, source_target_pairs={{0,1},{1,0},{2,3},{3,2},{4,5},{5,4},{6,7},{7,6},{8,9},{9,8},{10,11... | collective-permute-start | bytes 1572872 | tf_op jit(solution)/shard_map/ppermute | solution.py:359
  121.8 31.8 %all-to-all-start.4 = ((f16[48,19,2,128]{3,2,1,0:T(2,128)(2,1)}), f16[48,19,2,128]{3,2,1,0:T(2,128)(2,1)S(1)}, u32[]{:S(2)}, u32[]{:S(2)}) async-start(f16[48,19,2,128]{3,2,1,0:T(2,128)(2,1)} %bitcast.8), calls=%async_computation.4 | async-start | bytes 933888 | tf_op jit(solution)/shard_map/all_to_all | solution.py:350
  132.0 21.7 %collective-permute-start.5 = (f32[32,256]{1,0:T(8,128)S(1)}, f32[32,256]{1,0:T(8,128)S(1)}, u32[]{:S(2)}, u32[]{:S(2)}) collective-permute-start(f32[32,256]{1,0:T(8,128)S(1)} %get-tuple-element.42), channel_id=1, source_target_pairs={{48,0},{96,48},{144,96},{192,144},{240,192},{288,240},{336,288},{3... | collective-permute-start | bytes 98312 | tf_op jit(solution)/shard_map/ppermute | solution.py:440
  153.8 11.6 %collective-permute-start.6 = (f32[32,256]{1,0:T(8,128)S(1)}, f32[32,256]{1,0:T(8,128)S(1)}, u32[]{:S(2)}, u32[]{:S(2)}) collective-permute-start(f32[32,256]{1,0:T(8,128)S(1)} %shard_map.111), channel_id=1, source_target_pairs={{48,0},{96,48},{144,96},{192,144},{240,192},{288,240},{336,288},{3... | collective-permute-start | bytes 98312 | tf_op jit(solution)/shard_map/ppermute | solution.py:447

commit v6 on v5

--- a/solution.py
+++ b/solution.py
@@ -103,14 +103,48 @@
     return counts
 
 
-def start_kernel(held, ids, out):
+def lane_side():
+    lane = lax.broadcasted_iota(jnp.int32, (LANES, LANES), 1)
+    return lax.rem(lax.div(lane, ROWS), 2)
+
+
+def beside(x, side):
+    return jnp.where(side == 0, pltpu.roll(x, ROWS, 1), pltpu.roll(x, LANES - ROWS, 1))
+
+
+def start_kernel(held, ids, users, values, rows, cols, count, out, packet):
     stride = PAIR + 2
-    rows = halves(held[...].astype(BF16))
+    held_rows = halves(held[...].astype(BF16))
     counts = pick_row(ids, 0).astype(BF16)
     for chunk in range(out.shape[0] // stride):
         at = chunk * stride
-        out[at : at + PAIR, :] = rows
+        out[at : at + PAIR, :] = held_rows
         out[at + PAIR : at + stride, :] = counts
+    size = users.shape[0]
+    packet[0:size, :] = users[:, :LANES].astype(BF16)
+    packet[size : 2 * size, :] = users[:, LANES:].astype(BF16)
+    theirs = 1 - lax.axis_index("pair")
+    first = lane_side() == theirs
+    slots = values.shape[1]
+    for k in range(slots // 2):
+        other = beside(values[0, k + slots // 2].astype(F32), theirs)
+        at = 2 * size + k * LANES
+        packet[at : at + LANES, :] = jnp.where(first, values[0, k].astype(F32), other).astype(BF16)
+    lane = lax.broadcasted_iota(jnp.int32, (16, LANES), 1)
+    lists = jnp.where(lane == 2 * slots, count[0, 0], 0)
+    for k in range(slots):
+        lists = jnp.where(lane == k, rows[0, k], jnp.where(lane == slots + k, cols[0, k], lists))
+    at = 2 * size + slots // 2 * LANES
+    packet[at : at + 16, :] = lists.astype(F32).astype(BF16)
+
+
+def lists_of(packet, slots):
+    size = packet.shape[0]
+    line = packet[size - 16 : size, :].astype(F32)[0:1]
+    lane = lax.broadcasted_iota(jnp.int32, line.shape, 1)
+    return [
+        jnp.sum(jnp.where(lane == k, line, 0.0)).astype(jnp.int32) for k in range(2 * slots + 1)
+    ]
 
 
 def item_grads(users_bf, block, values, rows, cols, live, errors, owned, scale, add):
@@ -142,8 +176,8 @@
     return lambda k: ref[step, k]
 
 
-def from_list(ref, first):
-    return lambda k: ref[first + k]
+def from_list(scalars, first):
+    return lambda k: scalars[first + k]
 
 
 def pair_rows(chunk, side):
@@ -151,8 +185,8 @@
 
 
 def first_kernel(
-    got, users, their_users, values, their_values, rows, cols, count, theirs,
-    sums, block, errors, their_errors, users_bf, grads,
+    got, users, packet, values, rows, cols, count,
+    sums, block, errors, their_errors, users_bf, their_users, grads,
 ):
     stride = PAIR + 2
     chunks = got.shape[0] // stride
@@ -165,8 +199,16 @@
         block[pair_rows(chunk, side), LANES:] = got[at + ROWS : at + PAIR, :]
     users_bf[...] = users[...].astype(BF16)
     grads[...] = jnp.zeros_like(grads)
-    lane = lax.broadcasted_iota(jnp.int32, (tile_u, tile_i), 1)
-    owned = lax.rem(lax.div(lane, ROWS), 2) == side
+    owned = lane_side() == side
+    size = users.shape[0]
+    their_users[:, :LANES] = packet[0:size, :]
+    their_users[:, LANES:] = packet[size : 2 * size, :]
+    theirs = lists_of(packet, slots)
+
+    def their_values(k):
+        at = 2 * size + k % (slots // 2) * tile_u
+        shared = packet[at : at + tile_u, :].astype(F32)
+        return shared if k < slots // 2 else beside(shared, 1 - side)
 
     def add(col, part):
         at = pl.multiple_of(col * part.shape[0], part.shape[0])
@@ -177,7 +219,7 @@
         errors, owned, GRAD_SCALE, add,
     )
     item_grads(
-        their_users, block, lambda k: their_values[k], from_list(theirs, 0), from_list(theirs, slots),
+        their_users, block, their_values, from_list(theirs, 0), from_list(theirs, slots),
         theirs[2 * slots], their_errors, owned, GRAD_SCALE, add,
     )
     for chunk in range(chunks):
@@ -185,7 +227,7 @@
 
 
 def first_users_kernel(
-    got, block, users, rows, cols, errors, theirs, their_errors,
+    got, block, users, rows, cols, errors, packet, their_errors,
     users_out, their_grads, piece_out, their_piece, counts, packed, pieces, mine, grad_users,
 ):
     stride = PAIR + 2
@@ -216,6 +258,7 @@
     piece_out[...] = pieces[me]
     their_piece[...] = pieces[me + 1 - 2 * side]
     slots = errors.shape[0]
+    theirs = lists_of(packet, slots)
     user_grads(block, from_list(theirs, 0), from_list(theirs, slots), their_errors, their_grads)
     user_grads(block, at_step(rows, 0), at_step(cols, 0), errors, grad_users)
     users_out[...] = users[...] - LR_USER * grad_users[...]
@@ -382,28 +425,29 @@
     piece_shape = shape((padded, LANES), F32)
     packed = pltpu.VMEM((inners * piece, LANES), F32)
 
-    sent = call(start_kernel, shape((group * (PAIR + 2), LANES), BF16), [vm, sm], item_factors, neg_ids)
-    lists = jnp.concatenate([tile_rows[0], tile_cols[0], tile_count[0]])
-    sent, near_users, near_values, lists = lax.optimization_barrier(
-        (sent, user_factors.astype(BF16), tile_values[0], lists)
+    slots = tile_values.shape[1]
+    packet_rows = 2 * user_factors.shape[0] + slots // 2 * LANES + 16
+    sent, packet = call(
+        start_kernel,
+        (shape((group * (PAIR + 2), LANES), BF16), shape((packet_rows, LANES), BF16)),
+        [vm, sm, vm, vm, sm, sm, sm],
+        item_factors, neg_ids, user_factors, tile_values, tile_rows, tile_cols, tile_count,
     )
     got = chunks_exchanged(sent, GROUP)
-    theirs = swapped(lists)
-    their_users = swapped(near_users)
-    their_values = swapped(near_values)
+    packet = swapped(packet)
     sums, block, errors, their_errors = call(
         first_kernel,
         (shape((group, PAIR, LANES), F32), block_shape, errors_shape, errors_shape),
-        [vm, vm, vm, vm, vm, sm, sm, sm, sm],
-        got, user_factors, their_users, tile_values, their_values, tile_rows, tile_cols, tile_count, theirs,
-        scratch=[users_bf, pltpu.VMEM(block_shape.shape, F32)],
+        [vm, vm, vm, vm, sm, sm, sm],
+        got, user_factors, packet, tile_values, tile_rows, tile_cols, tile_count,
+        scratch=[users_bf, users_bf, pltpu.VMEM(block_shape.shape, F32)],
     )
     sums = exchanged(sums.astype(F16), GROUP).astype(F32)
     mid, rest, gram_piece, their_piece = call(
         first_users_kernel,
         (users_shape, users_shape, piece_shape, piece_shape),
-        [vm, vm, vm, sm, sm, vm, sm, vm],
-        got, block, user_factors, tile_rows, tile_cols, errors, theirs, their_errors,
+        [vm, vm, vm, sm, sm, vm, vm, vm],
+        got, block, user_factors, tile_rows, tile_cols, errors, packet, their_errors,
         scratch=[
             pltpu.VMEM((group, LANES), F32),
             packed,

time: 167 us -> 167 us (level)
  starting transfers between devices: 67.7 us -> 62.6 us
  local copies, waits for them, and re-layouts: 2.59 us -> 7.03 us
  waiting for transfers between devices: 59.2 us -> 61.8 us
    unnamed x21 -> x31, local copies, waits for them, and re-layouts: 0.93 us -> 6.41 us
    ppermute x5 -> x3, starting transfers between devices: 14.2 us -> 8.88 us  [swapped(): return lax.ppermute(x, 'pair', [(0, 1), (1, 0)])]
    ppermute x5 -> x3, waiting for transfers between devices: 8.1 us -> 10.7 us  [swapped(): return lax.ppermute(x, 'pair', [(0, 1), (1, 0)])]
  transfers between devices with their start and end apart: 11 -> 9, of which waited for: 5 -> 5; matrix products, arithmetic and copies ran while one was open for 0% -> 0% of each run, Pallas kernels for 2% -> 2%
where the time goes in v6:
time: 167 us
  starting transfers between devices  62.6 us (37%)
  waiting for transfers between devices  61.8 us (37%)
  blocking collectives  20.5 us (12%)
  Pallas kernels  11.2 us (7%)
  local copies, waits for them, and re-layouts  7.03 us (4%)
  other arithmetic  2.63 us (2%)
    all_to_all x4, waiting for transfers between devices, exchanged(): return lax.all_to_all(x, axis, 0, 0, tiled=True)  46.5 us
    all_to_all x4, starting transfers between devices, exchanged(): return lax.all_to_all(x, axis, 0, 0, tiled=True)  45.8 us
    all_to_all x1, blocking collectives, exchanged(): return lax.all_to_all(x, axis, 0, 0, tiled=True)  20.5 us
    pallas_call x9, Pallas kernels, call(): pl.pallas_call(kernel, out_shape=out_shape, in_specs=specs, out_specs=jax...  11.2 us
    ppermute x3, waiting for transfers between devices, swapped(): return lax.ppermute(x, 'pair', [(0, 1), (1, 0)])  10.7 us
    ppermute x3, starting transfers between devices, swapped(): return lax.ppermute(x, 'pair', [(0, 1), (1, 0)])  8.88 us
    ppermute x2, starting transfers between devices, shards(): state = lax.ppermute(state, 'stratum', onward)  7.86 us
    unnamed x31, local copies, waits for them, and re-layouts  6.41 us
  transfers between devices with their start and end apart: 9, of which 5 were waited for; matrix products, arithmetic and copies ran while one was open for 0% of the time, Pallas kernels for 2%

profile of v6, /device:TPU:7, one launch (start us, length us, event | category | flops | bytes accessed | tf_op | source)
XLA Modules:
  0.0 166.7 jit_solution(8753898264720830360)
XLA Ops:
  0.6 0.0 copy-start.7
  0.6 0.7 copy.11.count
  1.4 1.0 copy-done
  2.4 1.0 copy-done.2
  3.5 0.7 copy-done.4
  4.2 0.7 copy-done.6
  4.9 0.7 copy-done.8
  5.6 0.7 copy-done.11
  6.2 1.4 shard_map.103
  7.6 17.1 %all-to-all-start = ((bf16[24,17,2,128]{3,2,1,0:T(2,128)(2,1)}), bf16[24,17,2,128]{3,2,1,0:T(2,128)(2,1)S(1)}, u32[]{:S(2)}, u32[]{:S(2)}) async-start(bf16[24,17,2,128]{3,2,1,0:T(2,128)(2,1)} %bitcast), calls=%async_computation | async-start | bytes 417792 | tf_op jit(solution)/shard_map/all_to_all | solution.py:393
  24.7 3.2 %collective-permute-start = (bf16[1552,128]{1,0:T(8,128)(2,1)S(1)}, bf16[1552,128]{1,0:T(8,128)(2,1)S(1)}, u32[]{:S(2)}, u32[]{:S(2)}) collective-permute-start(bf16[1552,128]{1,0:T(8,128)(2,1)S(1)} %get-tuple-element.22), channel_id=1, source_target_pairs={{0,1},{1,0},{2,3},{3,2},{4,5},{5,4},{6,7},{7,6},{8,9},{9,8},{10,11... | collective-permute-start | bytes 1191944 | tf_op jit(solution)/shard_map/ppermute | solution.py:402
  28.0 10.7 %collective-permute-done.packet = bf16[1552,128]{1,0:T(8,128)(2,1)S(1)} collective-permute-done((bf16[1552,128]{1,0:T(8,128)(2,1)S(1)}, bf16[1552,128]{1,0:T(8,128)(2,1)S(1)}, u32[]{:S(2)}, u32[]{:S(2)}) %collective-permute-start) | collective-permute-done | bytes 397344 | tf_op jit(solution)/shard_map/ppermute | solution.py:402
  38.6 0.0 all-to-all-done
  38.7 1.8 %shard_map.104 = (f32[24,32,128]{2,1,0:T(8,128)S(1)}, bf16[768,256]{1,0:T(8,128)(2,1)S(1)}, bf16[8,128,128]{2,1,0:T(8,128)(2,1)S(1)}, bf16[8,128,128]{2,1,0:T(8,128)(2,1)S(1)}) custom-call(bf16[816,128]{1,0:T(8,128)(2,1)S(1)} %bitcast.8, f32[512,256]{1,0:T(8,128)S(1)} %copy-done.1, bf16[1552,128]{1,0:T(8,128)(2,1)S(1)} %collective-permute-done.packet, ...), custom_call_target="tpu_custom_call" | custom-call | tf_op jit(solution)/shard_map/pallas_call | solution.py:382
  40.5 0.7 convert_element_type.28
  41.2 10.6 %all-to-all-start.1 = ((f16[24,32,128]{2,1,0:T(8,128)(2,1)}), f16[24,32,128]{2,1,0:T(8,128)(2,1)S(1)}, u32[]{:S(2)}, u32[]{:S(2)}) async-start(f16[24,32,128]{2,1,0:T(8,128)(2,1)} %convert_element_type.28), calls=%async_computation.1 | async-start | bytes 393216 | tf_op jit(solution)/shard_map/all_to_all | solution.py:393
  51.8 0.0 copy-start.5
  51.8 0.0 copy-start.10
  51.8 0.0 copy-start.12
  51.9 1.5 shard_map.105
  53.3 0.0 copy-start.13
  53.3 0.8 copy-done.13
  54.1 2.6 %collective-permute-start.1 = (f32[8,128]{1,0:T(8,128)S(1)}, f32[8,128]{1,0:T(8,128)S(1)}, u32[]{:S(2)}, u32[]{:S(2)}) collective-permute-start(f32[8,128]{1,0:T(8,128)S(1)} %get-tuple-element.28), channel_id=1, source_target_pairs={{0,1},{1,0},{2,3},{3,2},{4,5},{5,4},{6,7},{7,6},{8,9},{9,8},{10,11... | collective-permute-start | bytes 12296 | tf_op jit(solution)/shard_map/ppermute | solution.py:402
  56.8 6.6 %all-to-all-done.1 = f16[24,32,128]{2,1,0:T(8,128)(2,1)S(1)} async-done(((f16[24,32,128]{2,1,0:T(8,128)(2,1)}), f16[24,32,128]{2,1,0:T(8,128)(2,1)S(1)}, u32[]{:S(2)}, u32[]{:S(2)}) %all-to-all-start.1) | async-done | bytes 196640 | tf_op jit(solution)/shard_map/all_to_all | solution.py:393
  63.4 0.0 collective-permute-done.1.their_piece
  63.4 0.6 shard_map.106
  64.1 20.5 %all_to_all.25 = f16[16,48,128]{2,1,0:T(8,128)(2,1)S(1)} all-to-all(f16[16,48,128]{2,1,0:T(8,128)(2,1)S(1)} %convert_element_type.30), channel_id=1, replica_groups=mesh['stratum'=16,'far'=12,'near'=2,'pair'=2] {'stratum'}, dimensions={0} | all-to-all | bytes 393216 | tf_op jit(solution)/shard_map/all_to_all | solution.py:393
  84.7 0.5 shard_map.107
  85.1 0.0 copy-start.14
  85.1 0.9 convert_element_type.32
  86.0 8.0 %all-to-all-start.3 = ((f16[48,22,2,128]{3,2,1,0:T(2,128)(2,1)}), f16[48,22,2,128]{3,2,1,0:T(2,128)(2,1)S(1)}, u32[]{:S(2)}, u32[]{:S(2)}) async-start(f16[48,22,2,128]{3,2,1,0:T(2,128)(2,1)} %bitcast.2), calls=%async_computation.3 | async-start | bytes 1081344 | tf_op jit(solution)/shard_map/all_to_all | solution.py:393
  94.0 3.0 %collective-permute-start.2 = (f32[512,256]{1,0:T(8,128)S(1)}, f32[512,256]{1,0:T(8,128)S(1)}, u32[]{:S(2)}, u32[]{:S(2)}) collective-permute-start(f32[512,256]{1,0:T(8,128)S(1)} %copy-done.14), channel_id=1, source_target_pairs={{0,1},{1,0},{2,3},{3,2},{4,5},{5,4},{6,7},{7,6},{8,9},{9,8},{10,11... | collective-permute-start | bytes 1572872 | tf_op jit(solution)/shard_map/ppermute | solution.py:402
  97.0 21.3 %all-to-all-done.3 = f16[48,22,2,128]{3,2,1,0:T(2,128)(2,1)S(1)} async-done(((f16[48,22,2,128]{3,2,1,0:T(2,128)(2,1)}), f16[48,22,2,128]{3,2,1,0:T(2,128)(2,1)S(1)}, u32[]{:S(2)}, u32[]{:S(2)}) %all-to-all-start.3) | async-done | bytes 540704 | tf_op jit(solution)/shard_map/all_to_all | solution.py:393
  118.4 0.1 convert.3.got
  118.5 0.0 collective-permute-done.2.rest
  118.5 3.2 %shard_map.108 = (f32[1824,128]{1,0:T(8,128)S(1)}, f32[512,256]{1,0:T(8,128)S(1)}, bf16[768,256]{1,0:T(8,128)(2,1)S(1)}, bf16[8,128,128]{2,1,0:T(8,128)(2,1)S(1)}) custom-call(f32[2112,128]{1,0:T(8,128)S(1)} %convert.3.got, f32[512,256]{1,0:T(8,128)S(1)} %copy-done.1, f32[512,256]{1,0:T(8,128)S(1)} %get-tuple-element.30.mid, ...), custom_call_target="tpu_custom_call" | custom-call | tf_op jit(solution)/shard_map/pallas_call | solution.py:382
  121.6 0.8 convert_element_type.35
  122.5 10.1 %all-to-all-start.4 = ((f16[48,19,2,128]{3,2,1,0:T(2,128)(2,1)}), f16[48,19,2,128]{3,2,1,0:T(2,128)(2,1)S(1)}, u32[]{:S(2)}, u32[]{:S(2)}) async-start(f16[48,19,2,128]{3,2,1,0:T(2,128)(2,1)} %bitcast.4), calls=%async_computation.4 | async-start | bytes 933888 | tf_op jit(solution)/shard_map/all_to_all | solution.py:393
  132.6 3.1 %collective-permute-start.3 = (f32[32,256]{1,0:T(8,128)S(1)}, f32[32,256]{1,0:T(8,128)S(1)}, u32[]{:S(2)}, u32[]{:S(2)}) collective-permute-start(f32[32,256]{1,0:T(8,128)S(1)} %get-tuple-element.38), channel_id=1, source_target_pairs={{48,0},{96,48},{144,96},{192,144},{240,192},{288,240},{336,288},{3... | collective-permute-start | bytes 98312 | tf_op jit(solution)/shard_map/ppermute | solution.py:484
  135.7 18.6 %all-to-all-done.4 = f16[48,19,2,128]{3,2,1,0:T(2,128)(2,1)S(1)} async-done(((f16[48,19,2,128]{3,2,1,0:T(2,128)(2,1)}), f16[48,19,2,128]{3,2,1,0:T(2,128)(2,1)S(1)}, u32[]{:S(2)}, u32[]{:S(2)}) %all-to-all-start.4) | async-done | bytes 466976 | tf_op jit(solution)/shard_map/all_to_all | solution.py:393
  154.3 0.1 convert.2.got
  154.3 0.0 collective-permute-done.3.state
  154.3 0.1 shard_map.111
  154.5 4.8 %collective-permute-start.4 = (f32[32,256]{1,0:T(8,128)S(1)}, f32[32,256]{1,0:T(8,128)S(1)}, u32[]{:S(2)}, u32[]{:S(2)}) collective-permute-start(f32[32,256]{1,0:T(8,128)S(1)} %shard_map.111), channel_id=1, source_target_pairs={{48,0},{96,48},{144,96},{192,144},{240,192},{288,240},{336,288},{3... | collective-permute-start | bytes 98312 | tf_op jit(solution)/shard_map/ppermute | solution.py:491
  159.2 0.9 shard_map.109.users
  160.2 1.3 shard_map.110
  161.5 4.6 %collective-permute-done.4 = f32[32,256]{1,0:T(8,128)S(1)} collective-permute-done((f32[32,256]{1,0:T(8,128)S(1)}, f32[32,256]{1,0:T(8,128)S(1)}, u32[]{:S(2)}, u32[]{:S(2)}) %collective-permute-start.4) | collective-permute-done | bytes 32800 | tf_op jit(solution)/shard_map/ppermute | solution.py:491
  166.1 0.6 fusion
  (20 shorter events, 0.1 us)
Async XLA Ops:
  0.6 38.0 %copy-start.7 = (s32[2,8]{1,0:T(2,128)S(1)}, s32[2,8]{1,0:T(2,128)}, u32[]{:S(2)}) copy-start(s32[2,8]{1,0:T(2,128)} %rows.9) | copy-start | bytes 196
  1.4 1.0 copy-start
  2.4 1.0 copy-start.2
  3.5 0.7 copy-start.4
  4.2 0.7 copy-start.6
  4.9 0.7 copy-start.8
  5.6 0.7 copy-start.11
  6.2 32.4 %copy-start.1 = (f32[512,256]{1,0:T(8,128)S(1)}, f32[512,256]{1,0:T(8,128)}, u32[]{:S(2)}) copy-start(f32[512,256]{1,0:T(8,128)} %users.7) | copy-start | bytes 1572868
  6.2 32.4 %copy-start.3 = (bf16[2,8,128,128]{3,2,1,0:T(8,128)(2,1)S(1)}, bf16[2,8,128,128]{3,2,1,0:T(8,128)(2,1)}, u32[]{:S(2)}) copy-start(bf16[2,8,128,128]{3,2,1,0:T(8,128)(2,1)} %values.5) | copy-start | bytes 1572868
  6.2 32.4 %copy-start.9 = (s32[2,8]{1,0:T(2,128)S(1)}, s32[2,8]{1,0:T(2,128)}, u32[]{:S(2)}) copy-start(s32[2,8]{1,0:T(2,128)} %cols.9) | copy-start | bytes 196
  7.6 31.0 %all-to-all-start = ((bf16[24,17,2,128]{3,2,1,0:T(2,128)(2,1)}), bf16[24,17,2,128]{3,2,1,0:T(2,128)(2,1)S(1)}, u32[]{:S(2)}, u32[]{:S(2)}) async-start(bf16[24,17,2,128]{3,2,1,0:T(2,128)(2,1)} %bitcast), calls=%async_computation | async-start | bytes 417792 | tf_op jit(solution)/shard_map/all_to_all | solution.py:393
  24.7 13.9 %collective-permute-start = (bf16[1552,128]{1,0:T(8,128)(2,1)S(1)}, bf16[1552,128]{1,0:T(8,128)(2,1)S(1)}, u32[]{:S(2)}, u32[]{:S(2)}) collective-permute-start(bf16[1552,128]{1,0:T(8,128)(2,1)S(1)} %get-tuple-element.22), channel_id=1, source_target_pairs={{0,1},{1,0},{2,3},{3,2},{4,5},{5,4},{6,7},{7,6},{8,9},{9,8},{10,11... | collective-permute-start | bytes 1191944 | tf_op jit(solution)/shard_map/ppermute | solution.py:402
  41.2 22.2 %all-to-all-start.1 = ((f16[24,32,128]{2,1,0:T(8,128)(2,1)}), f16[24,32,128]{2,1,0:T(8,128)(2,1)S(1)}, u32[]{:S(2)}, u32[]{:S(2)}) async-start(f16[24,32,128]{2,1,0:T(8,128)(2,1)} %convert_element_type.28), calls=%async_computation.1 | async-start | bytes 393216 | tf_op jit(solution)/shard_map/all_to_all | solution.py:393
  51.8 11.6 %copy-start.5 = (f32[16,256]{1,0:T(8,128)S(1)}, f32[16,256]{1,0:T(8,128)}, u32[]{:S(2)}) copy-start(f32[16,256]{1,0:T(8,128)} %held.3) | copy-start | bytes 49156
  51.8 11.6 %copy-start.10 = (f32[16,256]{1,0:T(8,128)S(1)}, f32[16,256]{1,0:T(8,128)}, u32[]{:S(2)}) copy-start(f32[16,256]{1,0:T(8,128)} %accum.1) | copy-start | bytes 49156
  51.8 11.6 %copy-start.12 = (s32[2,4]{1,0:T(2,128)S(1)}, s32[2,4]{1,0:T(2,128)}, u32[]{:S(2)}) copy-start(s32[2,4]{1,0:T(2,128)} %ids.3) | copy-start | bytes 100
  53.3 0.8 copy-start.13
  54.1 9.3 %collective-permute-start.1 = (f32[8,128]{1,0:T(8,128)S(1)}, f32[8,128]{1,0:T(8,128)S(1)}, u32[]{:S(2)}, u32[]{:S(2)}) collective-permute-start(f32[8,128]{1,0:T(8,128)S(1)} %get-tuple-element.28), channel_id=1, source_target_pairs={{0,1},{1,0},{2,3},{3,2},{4,5},{5,4},{6,7},{7,6},{8,9},{9,8},{10,11... | collective-permute-start | bytes 12296 | tf_op jit(solution)/shard_map/ppermute | solution.py:402
  85.1 8.9 %copy-start.14 = (f32[512,256]{1,0:T(8,128)S(1)}, f32[512,256]{1,0:T(8,128)}, u32[]{:S(2)}) copy-start(f32[512,256]{1,0:T(8,128)} %copy-done.13) | copy-start | bytes 1572868
  86.0 32.4 %all-to-all-start.3 = ((f16[48,22,2,128]{3,2,1,0:T(2,128)(2,1)}), f16[48,22,2,128]{3,2,1,0:T(2,128)(2,1)S(1)}, u32[]{:S(2)}, u32[]{:S(2)}) async-start(f16[48,22,2,128]{3,2,1,0:T(2,128)(2,1)} %bitcast.2), calls=%async_computation.3 | async-start | bytes 1081344 | tf_op jit(solution)/shard_map/all_to_all | solution.py:393
  94.0 24.5 %collective-permute-start.2 = (f32[512,256]{1,0:T(8,128)S(1)}, f32[512,256]{1,0:T(8,128)S(1)}, u32[]{:S(2)}, u32[]{:S(2)}) collective-permute-start(f32[512,256]{1,0:T(8,128)S(1)} %copy-done.14), channel_id=1, source_target_pairs={{0,1},{1,0},{2,3},{3,2},{4,5},{5,4},{6,7},{7,6},{8,9},{9,8},{10,11... | collective-permute-start | bytes 1572872 | tf_op jit(solution)/shard_map/ppermute | solution.py:402
  122.5 31.8 %all-to-all-start.4 = ((f16[48,19,2,128]{3,2,1,0:T(2,128)(2,1)}), f16[48,19,2,128]{3,2,1,0:T(2,128)(2,1)S(1)}, u32[]{:S(2)}, u32[]{:S(2)}) async-start(f16[48,19,2,128]{3,2,1,0:T(2,128)(2,1)} %bitcast.4), calls=%async_computation.4 | async-start | bytes 933888 | tf_op jit(solution)/shard_map/all_to_all | solution.py:393
  132.6 21.7 %collective-permute-start.3 = (f32[32,256]{1,0:T(8,128)S(1)}, f32[32,256]{1,0:T(8,128)S(1)}, u32[]{:S(2)}, u32[]{:S(2)}) collective-permute-start(f32[32,256]{1,0:T(8,128)S(1)} %get-tuple-element.38), channel_id=1, source_target_pairs={{48,0},{96,48},{144,96},{192,144},{240,192},{288,240},{336,288},{3... | collective-permute-start | bytes 98312 | tf_op jit(solution)/shard_map/ppermute | solution.py:484
  154.5 11.6 %collective-permute-start.4 = (f32[32,256]{1,0:T(8,128)S(1)}, f32[32,256]{1,0:T(8,128)S(1)}, u32[]{:S(2)}, u32[]{:S(2)}) collective-permute-start(f32[32,256]{1,0:T(8,128)S(1)} %shard_map.111), channel_id=1, source_target_pairs={{48,0},{96,48},{144,96},{192,144},{240,192},{288,240},{336,288},{3... | collective-permute-start | bytes 98312 | tf_op jit(solution)/shard_map/ppermute | solution.py:491

commit v7 on v6

--- a/solution.py
+++ b/solution.py
@@ -17,6 +17,7 @@
 F16 = jnp.float16
 
 GRAD_SCALE = 2.0**-7
+REST_SCALE = 2.0**-6
 ROOT_SCALE = 2.0**-9
 ITEM_SCALE = 2.0**12
 GRAM_SCALE = 2.0**12
@@ -112,7 +113,17 @@
     return jnp.where(side == 0, pltpu.roll(x, ROWS, 1), pltpu.roll(x, LANES - ROWS, 1))
 
 
-def start_kernel(held, ids, users, values, rows, cols, count, out, packet):
+def start_kernel(*refs):
+    given, (out, packet), taken, done = refs[:7], refs[7:9], refs[9:16], refs[16]
+    held, ids, users, values, rows, cols, count = taken
+    copies = []
+    for i, (source, target) in enumerate(zip(given, taken, strict=True)):
+        source = source.at[0] if target is values else source
+        copies.append(pltpu.make_async_copy(source, target, done.at[i]))
+    for copy in copies:
+        copy.start()
+    for copy in copies[:2]:
+        copy.wait()
     stride = PAIR + 2
     held_rows = halves(held[...].astype(BF16))
     counts = pick_row(ids, 0).astype(BF16)
@@ -120,16 +131,18 @@
         at = chunk * stride
         out[at : at + PAIR, :] = held_rows
         out[at + PAIR : at + stride, :] = counts
+    for copy in copies[2:]:
+        copy.wait()
     size = users.shape[0]
     packet[0:size, :] = users[:, :LANES].astype(BF16)
     packet[size : 2 * size, :] = users[:, LANES:].astype(BF16)
     theirs = 1 - lax.axis_index("pair")
     first = lane_side() == theirs
-    slots = values.shape[1]
+    slots = values.shape[0]
     for k in range(slots // 2):
-        other = beside(values[0, k + slots // 2].astype(F32), theirs)
+        other = beside(values[k + slots // 2].astype(F32), theirs)
         at = 2 * size + k * LANES
-        packet[at : at + LANES, :] = jnp.where(first, values[0, k].astype(F32), other).astype(BF16)
+        packet[at : at + LANES, :] = jnp.where(first, values[k].astype(F32), other).astype(BF16)
     lane = lax.broadcasted_iota(jnp.int32, (16, LANES), 1)
     lists = jnp.where(lane == 2 * slots, count[0, 0], 0)
     for k in range(slots):
@@ -330,7 +343,7 @@
         packed[chunk * piece : (chunk + 1) * piece, :] = got[at + PAIR : at + PAIR + piece, :]
         full = full + got[at + PAIR + piece : at + stride, :]
     gram = whole_gram(packed, 1.0 / GRAM_SCALE)
-    part = mid[...] - LR_USER * rest[...]
+    part = mid[...] - (LR_USER / REST_SCALE) * rest[...]
     now = part - (LR_USER * LAMBDA) * times_gram(users[...], gram)
     mid_out[...] = now
     users_bf[...] = now.astype(BF16)
@@ -378,14 +391,14 @@
     out[...] = users[...] - (LR_USER * LAMBDA) * times_gram(mid[...], gram)
 
 
-def call(kernel, out_shape, specs, *args, scratch=()):
+def call(kernel, out_shape, specs, *args, scratch=(), vmem=44):
     return pl.pallas_call(
         kernel,
         out_shape=out_shape,
         in_specs=specs,
         out_specs=jax.tree.map(lambda _: pl.BlockSpec(memory_space=VMEM), out_shape),
         scratch_shapes=scratch,
-        compiler_params=pltpu.CompilerParams(vmem_limit_bytes=44 * 2**20),
+        compiler_params=pltpu.CompilerParams(vmem_limit_bytes=vmem * 2**20),
     )(*args)
 
 
@@ -430,8 +443,19 @@
     sent, packet = call(
         start_kernel,
         (shape((group * (PAIR + 2), LANES), BF16), shape((packet_rows, LANES), BF16)),
-        [vm, sm, vm, vm, sm, sm, sm],
+        [pl.BlockSpec(memory_space=pltpu.HBM)] * 7,
         item_factors, neg_ids, user_factors, tile_values, tile_rows, tile_cols, tile_count,
+        scratch=[
+            pltpu.VMEM(item_factors.shape, F32),
+            pltpu.SMEM(neg_ids.shape, jnp.int32),
+            users_f32,
+            pltpu.VMEM(tile_values.shape[1:], BF16),
+            pltpu.SMEM(tile_rows.shape, jnp.int32),
+            pltpu.SMEM(tile_cols.shape, jnp.int32),
+            pltpu.SMEM(tile_count.shape, jnp.int32),
+            pltpu.SemaphoreType.DMA((7,)),
+        ],
+        vmem=62,
     )
     got = chunks_exchanged(sent, GROUP)
     packet = swapped(packet)
@@ -457,14 +481,16 @@
         ],
     )
     their_piece = swapped(their_piece)
-    rest = swapped(rest)
+    rest = swapped((rest * REST_SCALE).astype(F16))
     state, sent = call(
         item_kernel,
         (state_shape, shape((strata, PAIR + 8 + padded, LANES), F32)),
         [vm, vm, vm, vm, vm, sm],
         sums, item_factors, item_accum, gram_piece, their_piece, neg_ids,
     )
-    met = exchanged(sent.astype(F16), "stratum").astype(F32)
+    met = exchanged(sent.astype(F16), "stratum")
+    met, rest = lax.optimization_barrier((met, rest))
+    met, rest = met.astype(F32), rest.astype(F32)
     sent = call(
         functools.partial(gather_kernel, total),
         shape((inners * (PAIR + 2 * piece), LANES), F32),

time: 167 us -> 163 us (0.976)
  blocking collectives: 20.5 us -> 0 us
  waiting for transfers between devices: 61.8 us -> 72.4 us
  starting transfers between devices: 62.6 us -> 68.7 us
  local copies, waits for them, and re-layouts: 7.03 us -> 2.99 us
  other arithmetic: 2.63 us -> 4.41 us
    all_to_all x1 -> x0, blocking collectives: 20.5 us -> none  [exchanged(): return lax.all_to_all(x, axis, 0, 0, tiled=True)]
    ppermute x3, waiting for transfers between devices: 10.7 us -> 19.6 us  [swapped(): return lax.ppermute(x, 'pair', [(0, 1), (1, 0)])]
    all_to_all x4 -> x5, starting transfers between devices: 45.8 us -> 52.4 us  [exchanged(): return lax.all_to_all(x, axis, 0, 0, tiled=True)]
    unnamed x31 -> x21, local copies, waits for them, and re-layouts: 6.41 us -> 2.38 us
    all_to_all x4 -> x5, waiting for transfers between devices: 46.5 us -> 48.4 us  [exchanged(): return lax.all_to_all(x, axis, 0, 0, tiled=True)]
  transfers between devices with their start and end apart: 9 -> 10, of which waited for: 5 -> 6; matrix products, arithmetic and copies ran while one was open for 0% -> 1% of each run, Pallas kernels for 2% -> 2%
where the time goes in v7:
time: 163 us; the launch traced here: 161 us
  waiting for transfers between devices  72.4 us (44%)
  starting transfers between devices  68.7 us (42%)
  Pallas kernels  12 us (7%)
  other arithmetic  4.41 us (3%)
  local copies, waits for them, and re-layouts  2.99 us (2%)
    all_to_all x5, starting transfers between devices, exchanged(): return lax.all_to_all(x, axis, 0, 0, tiled=True)  52.4 us
    all_to_all x5, waiting for transfers between devices, exchanged(): return lax.all_to_all(x, axis, 0, 0, tiled=True)  48.4 us
    ppermute x3, waiting for transfers between devices, swapped(): return lax.ppermute(x, 'pair', [(0, 1), (1, 0)])  19.6 us
    pallas_call x9, Pallas kernels, call(): pl.pallas_call(kernel, out_shape=out_shape, in_specs=specs, out_specs=jax...  12 us
    ppermute x2, starting transfers between devices, shards(): state = lax.ppermute(state, 'stratum', onward)  8.21 us
    ppermute x3, starting transfers between devices, swapped(): return lax.ppermute(x, 'pair', [(0, 1), (1, 0)])  8.04 us
    ppermute x2, waiting for transfers between devices, shards(): state = lax.ppermute(state, 'stratum', onward)  4.41 us
  transfers between devices with their start and end apart: 10, of which 6 were waited for; matrix products, arithmetic and copies ran while one was open for 1% of the time, Pallas kernels for 2%

profile of v7, /device:TPU:7, one launch (start us, length us, event | category | flops | bytes accessed | tf_op | source)
XLA Modules:
  0.0 161.4 jit_solution(10737462958179492137)
XLA Ops:
  0.6 0.0 copy-start.6
  0.6 0.0 copy-start.5
  0.7 0.0 copy-start
  0.7 0.0 copy-start.1
  0.7 1.4 copy.11.refs_6_.count
  2.1 2.1 %shard_map.103 = (bf16[816,128]{1,0:T(8,128)(2,1)}, bf16[1552,128]{1,0:T(8,128)(2,1)}) custom-call(f32[16,256]{1,0:T(8,128)} %held.1, s32[2,4]{1,0:T(2,128)} %ids.1, f32[512,256]{1,0:T(8,128)} %users.5, bf16[2,8,128,128]{3,2,1,0:T(8,128)(2,1)} %values.3, s32[2,8]{1,0:T(2,128)} %rows.7, s32[2,8]{1,0:T(2,128)} %cols.7, s32[2,1]{1,0:T(2,128)} %copy.11.refs_6_.count), custom_call_target="tpu_custom_call" | custom-call | tf_op jit(solution)/shard_map/pallas_call | solution.py:395
  4.2 17.1 %all-to-all-start = ((bf16[24,17,2,128]{3,2,1,0:T(2,128)(2,1)}), bf16[24,17,2,128]{3,2,1,0:T(2,128)(2,1)S(1)}, u32[]{:S(2)}, u32[]{:S(2)}) async-start(bf16[24,17,2,128]{3,2,1,0:T(2,128)(2,1)} %bitcast.12), calls=%async_computation | async-start | bytes 417792 | tf_op jit(solution)/shard_map/all_to_all | solution.py:406
  21.3 3.2 %collective-permute-start = (bf16[1552,128]{1,0:T(8,128)(2,1)}, bf16[1552,128]{1,0:T(8,128)(2,1)S(1)}, u32[]{:S(2)}, u32[]{:S(2)}) collective-permute-start(bf16[1552,128]{1,0:T(8,128)(2,1)} %get-tuple-element.24), channel_id=1, source_target_pairs={{0,1},{1,0},{2,3},{3,2},{4,5},{5,4},{6,7},{7,6},{8,9},{9,8},{10,11... | collective-permute-start | bytes 1191944 | tf_op jit(solution)/shard_map/ppermute | solution.py:415
  24.5 10.8 %collective-permute-done.packet = bf16[1552,128]{1,0:T(8,128)(2,1)S(1)} collective-permute-done((bf16[1552,128]{1,0:T(8,128)(2,1)}, bf16[1552,128]{1,0:T(8,128)(2,1)S(1)}, u32[]{:S(2)}, u32[]{:S(2)}) %collective-permute-start) | collective-permute-done | bytes 397344 | tf_op jit(solution)/shard_map/ppermute | solution.py:415
  35.3 0.0 all-to-all-done
  35.3 0.0 copy-done.5
  35.3 0.0 copy-done
  35.4 1.8 %shard_map.104 = (f32[24,32,128]{2,1,0:T(8,128)S(1)}, bf16[768,256]{1,0:T(8,128)(2,1)S(1)}, bf16[8,128,128]{2,1,0:T(8,128)(2,1)S(1)}, bf16[8,128,128]{2,1,0:T(8,128)(2,1)S(1)}) custom-call(bf16[816,128]{1,0:T(8,128)(2,1)S(1)} %bitcast.8, f32[512,256]{1,0:T(8,128)S(1)} %copy-done, bf16[1552,128]{1,0:T(8,128)(2,1)S(1)} %collective-permute-done.packet, ...), custom_call_target="tpu_custom_call" | custom-call | tf_op jit(solution)/shard_map/pallas_call | solution.py:395
  37.2 0.0 copy-start.2
  37.2 0.8 convert_element_type.34
  38.0 10.7 %all-to-all-start.1 = ((f16[24,32,128]{2,1,0:T(8,128)(2,1)}), f16[24,32,128]{2,1,0:T(8,128)(2,1)}, u32[]{:S(2)}, u32[]{:S(2)}) async-start(f16[24,32,128]{2,1,0:T(8,128)(2,1)} %convert_element_type.34), calls=%async_computation.1 | async-start | bytes 393216 | tf_op jit(solution)/shard_map/all_to_all | solution.py:406
  48.7 0.0 copy-start.3
  48.7 0.9 copy-done.3
  49.6 1.5 shard_map.105
  51.1 2.8 %collective-permute-start.1 = (f32[8,128]{1,0:T(8,128)S(1)}, f32[8,128]{1,0:T(8,128)S(1)}, u32[]{:S(2)}, u32[]{:S(2)}) collective-permute-start(f32[8,128]{1,0:T(8,128)S(1)} %get-tuple-element.30), channel_id=1, source_target_pairs={{0,1},{1,0},{2,3},{3,2},{4,5},{5,4},{6,7},{7,6},{8,9},{9,8},{10,11... | collective-permute-start | bytes 12296 | tf_op jit(solution)/shard_map/ppermute | solution.py:415
  53.9 6.3 %all-to-all-done.1 = f16[24,32,128]{2,1,0:T(8,128)(2,1)} async-done(((f16[24,32,128]{2,1,0:T(8,128)(2,1)}), f16[24,32,128]{2,1,0:T(8,128)(2,1)}, u32[]{:S(2)}, u32[]{:S(2)}) %all-to-all-start.1) | async-done | bytes 196640 | tf_op jit(solution)/shard_map/all_to_all | solution.py:406
  60.2 1.0 convert_element_type.35.got
  61.2 0.0 collective-permute-done.1.their_piece
  61.2 0.6 shard_map.106
  61.8 0.7 convert_element_type.36
  62.5 11.5 %all-to-all-start.2 = ((f16[16,48,128]{2,1,0:T(8,128)(2,1)}), f16[16,48,128]{2,1,0:T(8,128)(2,1)S(1)}, u32[]{:S(2)}, u32[]{:S(2)}) async-start(f16[16,48,128]{2,1,0:T(8,128)(2,1)} %convert_element_type.36), calls=%async_computation.2 | async-start | bytes 393216 | tf_op jit(solution)/shard_map/all_to_all | solution.py:406
  74.0 0.1 multiply_convert_fusion
  74.1 2.1 %collective-permute-start.2 = (f16[512,256]{1,0:T(8,128)(2,1)S(1)}, f16[512,256]{1,0:T(8,128)(2,1)S(1)}, u32[]{:S(2)}, u32[]{:S(2)}) collective-permute-start(f16[512,256]{1,0:T(8,128)(2,1)S(1)} %multiply_convert_fusion), channel_id=1, source_target_pairs={{0,1},{1,0},{2,3},{3,2},{4,5},{5,4},{6,7},{7,6},{8,9},{9,8},{10,11... | collective-permute-start | bytes 786440 | tf_op jit(solution)/shard_map/ppermute | solution.py:415
  76.2 8.8 %collective-permute-done.2 = f16[512,256]{1,0:T(8,128)(2,1)S(1)} collective-permute-done((f16[512,256]{1,0:T(8,128)(2,1)S(1)}, f16[512,256]{1,0:T(8,128)(2,1)S(1)}, u32[]{:S(2)}, u32[]{:S(2)}) %collective-permute-start.2) | collective-permute-done | bytes 262176 | tf_op jit(solution)/shard_map/ppermute | solution.py:415
  85.0 0.0 all-to-all-done.2
  85.0 0.5 shard_map.107
  85.5 0.9 convert_element_type.39
  86.4 6.4 %all-to-all-start.3 = ((f16[48,22,2,128]{3,2,1,0:T(2,128)(2,1)}), f16[48,22,2,128]{3,2,1,0:T(2,128)(2,1)S(1)}, u32[]{:S(2)}, u32[]{:S(2)}) async-start(f16[48,22,2,128]{3,2,1,0:T(2,128)(2,1)} %bitcast.2), calls=%async_computation.3 | async-start | bytes 1081344 | tf_op jit(solution)/shard_map/all_to_all | solution.py:406
  92.8 23.9 %all-to-all-done.3 = f16[48,22,2,128]{3,2,1,0:T(2,128)(2,1)S(1)} async-done(((f16[48,22,2,128]{3,2,1,0:T(2,128)(2,1)}), f16[48,22,2,128]{3,2,1,0:T(2,128)(2,1)S(1)}, u32[]{:S(2)}, u32[]{:S(2)}) %all-to-all-start.3) | async-done | bytes 540704 | tf_op jit(solution)/shard_map/all_to_all | solution.py:406
  116.8 0.1 convert.3.got
  116.8 3.1 %shard_map.108 = (f32[1824,128]{1,0:T(8,128)S(1)}, f32[512,256]{1,0:T(8,128)S(1)}, bf16[768,256]{1,0:T(8,128)(2,1)S(1)}, bf16[8,128,128]{2,1,0:T(8,128)(2,1)S(1)}) custom-call(f32[2112,128]{1,0:T(8,128)S(1)} %convert.3.got, f32[512,256]{1,0:T(8,128)S(1)} %copy-done, f32[512,256]{1,0:T(8,128)S(1)} %get-tuple-element.34.mid, ...), custom_call_target="tpu_custom_call" | custom-call | tf_op jit(solution)/shard_map/pallas_call | solution.py:395
  120.0 0.8 convert_element_type.43
  120.8 6.7 %all-to-all-start.4 = ((f16[48,19,2,128]{3,2,1,0:T(2,128)(2,1)}), f16[48,19,2,128]{3,2,1,0:T(2,128)(2,1)S(1)}, u32[]{:S(2)}, u32[]{:S(2)}) async-start(f16[48,19,2,128]{3,2,1,0:T(2,128)(2,1)} %bitcast.4), calls=%async_computation.4 | async-start | bytes 933888 | tf_op jit(solution)/shard_map/all_to_all | solution.py:406
  127.6 3.6 %collective-permute-start.3 = (f32[32,256]{1,0:T(8,128)S(1)}, f32[32,256]{1,0:T(8,128)S(1)}, u32[]{:S(2)}, u32[]{:S(2)}) collective-permute-start(f32[32,256]{1,0:T(8,128)S(1)} %get-tuple-element.42), channel_id=1, source_target_pairs={{48,0},{96,48},{144,96},{192,144},{240,192},{288,240},{336,288},{3... | collective-permute-start | bytes 98312 | tf_op jit(solution)/shard_map/ppermute | solution.py:510
  131.2 18.1 %all-to-all-done.4 = f16[48,19,2,128]{3,2,1,0:T(2,128)(2,1)S(1)} async-done(((f16[48,19,2,128]{3,2,1,0:T(2,128)(2,1)}), f16[48,19,2,128]{3,2,1,0:T(2,128)(2,1)S(1)}, u32[]{:S(2)}, u32[]{:S(2)}) %all-to-all-start.4) | async-done | bytes 466976 | tf_op jit(solution)/shard_map/all_to_all | solution.py:406
  149.3 0.1 convert.2.got
  149.4 0.0 collective-permute-done.3.state
  149.4 0.1 shard_map.111
  149.5 4.6 %collective-permute-start.4 = (f32[32,256]{1,0:T(8,128)S(1)}, f32[32,256]{1,0:T(8,128)S(1)}, u32[]{:S(2)}, u32[]{:S(2)}) collective-permute-start(f32[32,256]{1,0:T(8,128)S(1)} %shard_map.111), channel_id=1, source_target_pairs={{48,0},{96,48},{144,96},{192,144},{240,192},{288,240},{336,288},{3... | collective-permute-start | bytes 98312 | tf_op jit(solution)/shard_map/ppermute | solution.py:517
  154.1 0.9 shard_map.109.users
  155.0 1.3 shard_map.110
  156.3 4.4 %collective-permute-done.4 = f32[32,256]{1,0:T(8,128)S(1)} collective-permute-done((f32[32,256]{1,0:T(8,128)S(1)}, f32[32,256]{1,0:T(8,128)S(1)}, u32[]{:S(2)}, u32[]{:S(2)}) %collective-permute-start.4) | collective-permute-done | bytes 32800 | tf_op jit(solution)/shard_map/ppermute | solution.py:517
  160.7 0.6 fusion
  (13 shorter events, 0.1 us)
Async XLA Ops:
  0.6 34.7 %copy-start.6 = (s32[2,8]{1,0:T(2,128)S(1)}, s32[2,8]{1,0:T(2,128)}, u32[]{:S(2)}) copy-start(s32[2,8]{1,0:T(2,128)} %cols.7) | copy-start | bytes 196
  0.6 34.7 %copy-start.5 = (s32[2,8]{1,0:T(2,128)S(1)}, s32[2,8]{1,0:T(2,128)}, u32[]{:S(2)}) copy-start(s32[2,8]{1,0:T(2,128)} %rows.7) | copy-start | bytes 196
  0.7 34.7 %copy-start = (f32[512,256]{1,0:T(8,128)S(1)}, f32[512,256]{1,0:T(8,128)}, u32[]{:S(2)}) copy-start(f32[512,256]{1,0:T(8,128)} %users.5) | copy-start | bytes 1572868
  0.7 34.7 %copy-start.1 = (bf16[2,8,128,128]{3,2,1,0:T(8,128)(2,1)S(1)}, bf16[2,8,128,128]{3,2,1,0:T(8,128)(2,1)}, u32[]{:S(2)}) copy-start(bf16[2,8,128,128]{3,2,1,0:T(8,128)(2,1)} %values.3) | copy-start | bytes 1572868
  2.1 33.3 %copy-start.8 = (s32[2,1]{1,0:T(2,128)S(1)}, s32[2,1]{1,0:T(2,128)}, u32[]{:S(2)}) copy-start(s32[2,1]{1,0:T(2,128)} %copy.11.refs_6_.count) | copy-start | bytes 28
  4.2 31.1 %all-to-all-start = ((bf16[24,17,2,128]{3,2,1,0:T(2,128)(2,1)}), bf16[24,17,2,128]{3,2,1,0:T(2,128)(2,1)S(1)}, u32[]{:S(2)}, u32[]{:S(2)}) async-start(bf16[24,17,2,128]{3,2,1,0:T(2,128)(2,1)} %bitcast.12), calls=%async_computation | async-start | bytes 417792 | tf_op jit(solution)/shard_map/all_to_all | solution.py:406
  21.3 14.0 %collective-permute-start = (bf16[1552,128]{1,0:T(8,128)(2,1)}, bf16[1552,128]{1,0:T(8,128)(2,1)S(1)}, u32[]{:S(2)}, u32[]{:S(2)}) collective-permute-start(bf16[1552,128]{1,0:T(8,128)(2,1)} %get-tuple-element.24), channel_id=1, source_target_pairs={{0,1},{1,0},{2,3},{3,2},{4,5},{5,4},{6,7},{7,6},{8,9},{9,8},{10,11... | collective-permute-start | bytes 1191944 | tf_op jit(solution)/shard_map/ppermute | solution.py:415
  37.2 11.4 %copy-start.2 = (bf16[8,128,128]{2,1,0:T(8,128)(2,1)}, bf16[8,128,128]{2,1,0:T(8,128)(2,1)S(1)}, u32[]{:S(2)}) copy-start(bf16[8,128,128]{2,1,0:T(8,128)(2,1)S(1)} %get-tuple-element.28.their_errors) | copy-start | bytes 786436
  38.0 22.2 %all-to-all-start.1 = ((f16[24,32,128]{2,1,0:T(8,128)(2,1)}), f16[24,32,128]{2,1,0:T(8,128)(2,1)}, u32[]{:S(2)}, u32[]{:S(2)}) async-start(f16[24,32,128]{2,1,0:T(8,128)(2,1)} %convert_element_type.34), calls=%async_computation.1 | async-start | bytes 393216 | tf_op jit(solution)/shard_map/all_to_all | solution.py:406
  48.7 1.0 copy-start.3
  49.6 11.6 %copy-start.4 = (f32[16,256]{1,0:T(8,128)S(1)}, f32[16,256]{1,0:T(8,128)}, u32[]{:S(2)}) copy-start(f32[16,256]{1,0:T(8,128)} %held.1) | copy-start | bytes 49156
  49.6 11.6 %copy-start.7 = (f32[16,256]{1,0:T(8,128)S(1)}, f32[16,256]{1,0:T(8,128)}, u32[]{:S(2)}) copy-start(f32[16,256]{1,0:T(8,128)} %accum.1) | copy-start | bytes 49156
  49.6 11.6 %copy-start.9 = (s32[2,4]{1,0:T(2,128)S(1)}, s32[2,4]{1,0:T(2,128)}, u32[]{:S(2)}) copy-start(s32[2,4]{1,0:T(2,128)} %ids.1) | copy-start | bytes 100
  51.1 10.1 %collective-permute-start.1 = (f32[8,128]{1,0:T(8,128)S(1)}, f32[8,128]{1,0:T(8,128)S(1)}, u32[]{:S(2)}, u32[]{:S(2)}) collective-permute-start(f32[8,128]{1,0:T(8,128)S(1)} %get-tuple-element.30), channel_id=1, source_target_pairs={{0,1},{1,0},{2,3},{3,2},{4,5},{5,4},{6,7},{7,6},{8,9},{9,8},{10,11... | collective-permute-start | bytes 12296 | tf_op jit(solution)/shard_map/ppermute | solution.py:415
  62.5 22.5 %all-to-all-start.2 = ((f16[16,48,128]{2,1,0:T(8,128)(2,1)}), f16[16,48,128]{2,1,0:T(8,128)(2,1)S(1)}, u32[]{:S(2)}, u32[]{:S(2)}) async-start(f16[16,48,128]{2,1,0:T(8,128)(2,1)} %convert_element_type.36), calls=%async_computation.2 | async-start | bytes 393216 | tf_op jit(solution)/shard_map/all_to_all | solution.py:406
  74.1 10.9 %collective-permute-start.2 = (f16[512,256]{1,0:T(8,128)(2,1)S(1)}, f16[512,256]{1,0:T(8,128)(2,1)S(1)}, u32[]{:S(2)}, u32[]{:S(2)}) collective-permute-start(f16[512,256]{1,0:T(8,128)(2,1)S(1)} %multiply_convert_fusion), channel_id=1, source_target_pairs={{0,1},{1,0},{2,3},{3,2},{4,5},{5,4},{6,7},{7,6},{8,9},{9,8},{10,11... | collective-permute-start | bytes 786440 | tf_op jit(solution)/shard_map/ppermute | solution.py:415
  86.4 30.4 %all-to-all-start.3 = ((f16[48,22,2,128]{3,2,1,0:T(2,128)(2,1)}), f16[48,22,2,128]{3,2,1,0:T(2,128)(2,1)S(1)}, u32[]{:S(2)}, u32[]{:S(2)}) async-start(f16[48,22,2,128]{3,2,1,0:T(2,128)(2,1)} %bitcast.2), calls=%async_computation.3 | async-start | bytes 1081344 | tf_op jit(solution)/shard_map/all_to_all | solution.py:406
  120.8 28.5 %all-to-all-start.4 = ((f16[48,19,2,128]{3,2,1,0:T(2,128)(2,1)}), f16[48,19,2,128]{3,2,1,0:T(2,128)(2,1)S(1)}, u32[]{:S(2)}, u32[]{:S(2)}) async-start(f16[48,19,2,128]{3,2,1,0:T(2,128)(2,1)} %bitcast.4), calls=%async_computation.4 | async-start | bytes 933888 | tf_op jit(solution)/shard_map/all_to_all | solution.py:406
  127.6 21.8 %collective-permute-start.3 = (f32[32,256]{1,0:T(8,128)S(1)}, f32[32,256]{1,0:T(8,128)S(1)}, u32[]{:S(2)}, u32[]{:S(2)}) collective-permute-start(f32[32,256]{1,0:T(8,128)S(1)} %get-tuple-element.42), channel_id=1, source_target_pairs={{48,0},{96,48},{144,96},{192,144},{240,192},{288,240},{336,288},{3... | collective-permute-start | bytes 98312 | tf_op jit(solution)/shard_map/ppermute | solution.py:510
  149.5 11.3 %collective-permute-start.4 = (f32[32,256]{1,0:T(8,128)S(1)}, f32[32,256]{1,0:T(8,128)S(1)}, u32[]{:S(2)}, u32[]{:S(2)}) collective-permute-start(f32[32,256]{1,0:T(8,128)S(1)} %shard_map.111), channel_id=1, source_target_pairs={{48,0},{96,48},{144,96},{192,144},{240,192},{288,240},{336,288},{3... | collective-permute-start | bytes 98312 | tf_op jit(solution)/shard_map/ppermute | solution.py:517

commit v8 on v7

--- a/solution.py
+++ b/solution.py
@@ -114,7 +114,7 @@
 
 
 def start_kernel(*refs):
-    given, (out, packet), taken, done = refs[:7], refs[7:9], refs[9:16], refs[16]
+    given, (out, *packets), taken, done = refs[:7], refs[7:10], refs[10:17], refs[17]
     held, ids, users, values, rows, cols, count = taken
     copies = []
     for i, (source, target) in enumerate(zip(given, taken, strict=True)):
@@ -134,21 +134,21 @@
     for copy in copies[2:]:
         copy.wait()
     size = users.shape[0]
-    packet[0:size, :] = users[:, :LANES].astype(BF16)
-    packet[size : 2 * size, :] = users[:, LANES:].astype(BF16)
+    packets[0][0:size, :] = users[:, :LANES].astype(BF16)
+    packets[1][0:size, :] = users[:, LANES:].astype(BF16)
     theirs = 1 - lax.axis_index("pair")
     first = lane_side() == theirs
     slots = values.shape[0]
     for k in range(slots // 2):
         other = beside(values[k + slots // 2].astype(F32), theirs)
-        at = 2 * size + k * LANES
-        packet[at : at + LANES, :] = jnp.where(first, values[k].astype(F32), other).astype(BF16)
+        at = size + k // 2 * LANES
+        packets[k % 2][at : at + LANES, :] = jnp.where(first, values[k].astype(F32), other).astype(BF16)
     lane = lax.broadcasted_iota(jnp.int32, (16, LANES), 1)
     lists = jnp.where(lane == 2 * slots, count[0, 0], 0)
     for k in range(slots):
         lists = jnp.where(lane == k, rows[0, k], jnp.where(lane == slots + k, cols[0, k], lists))
-    at = 2 * size + slots // 2 * LANES
-    packet[at : at + 16, :] = lists.astype(F32).astype(BF16)
+    at = size + slots // 4 * LANES
+    packets[0][at : at + 16, :] = lists.astype(F32).astype(BF16)
 
 
 def lists_of(packet, slots):
@@ -198,7 +198,7 @@
 
 
 def first_kernel(
-    got, users, packet, values, rows, cols, count,
+    got, users, packet, packet_too, values, rows, cols, count,
     sums, block, errors, their_errors, users_bf, their_users, grads,
 ):
     stride = PAIR + 2
@@ -215,12 +215,12 @@
     owned = lane_side() == side
     size = users.shape[0]
     their_users[:, :LANES] = packet[0:size, :]
-    their_users[:, LANES:] = packet[size : 2 * size, :]
+    their_users[:, LANES:] = packet_too[0:size, :]
     theirs = lists_of(packet, slots)
 
     def their_values(k):
-        at = 2 * size + k % (slots // 2) * tile_u
-        shared = packet[at : at + tile_u, :].astype(F32)
+        at = size + k % (slots // 2) // 2 * tile_u
+        shared = (packet, packet_too)[k % 2][at : at + tile_u, :].astype(F32)
         return shared if k < slots // 2 else beside(shared, 1 - side)
 
     def add(col, part):
@@ -439,10 +439,14 @@
     packed = pltpu.VMEM((inners * piece, LANES), F32)
 
     slots = tile_values.shape[1]
-    packet_rows = 2 * user_factors.shape[0] + slots // 2 * LANES + 16
-    sent, packet = call(
+    packet_rows = user_factors.shape[0] + slots // 4 * LANES
+    sent, packet, packet_too = call(
         start_kernel,
-        (shape((group * (PAIR + 2), LANES), BF16), shape((packet_rows, LANES), BF16)),
+        (
+            shape((group * (PAIR + 2), LANES), BF16),
+            shape((packet_rows + 16, LANES), BF16),
+            shape((packet_rows, LANES), BF16),
+        ),
         [pl.BlockSpec(memory_space=pltpu.HBM)] * 7,
         item_factors, neg_ids, user_factors, tile_values, tile_rows, tile_cols, tile_count,
         scratch=[
@@ -458,12 +462,12 @@
         vmem=62,
     )
     got = chunks_exchanged(sent, GROUP)
-    packet = swapped(packet)
+    packet, packet_too = swapped(packet), swapped(packet_too)
     sums, block, errors, their_errors = call(
         first_kernel,
         (shape((group, PAIR, LANES), F32), block_shape, errors_shape, errors_shape),
-        [vm, vm, vm, vm, sm, sm, sm],
-        got, user_factors, packet, tile_values, tile_rows, tile_cols, tile_count,
+        [vm, vm, vm, vm, vm, sm, sm, sm],
+        got, user_factors, packet, packet_too, tile_values, tile_rows, tile_cols, tile_count,
         scratch=[users_bf, users_bf, pltpu.VMEM(block_shape.shape, F32)],
     )
     sums = exchanged(sums.astype(F16), GROUP).astype(F32)
@@ -489,8 +493,7 @@
         sums, item_factors, item_accum, gram_piece, their_piece, neg_ids,
     )
     met = exchanged(sent.astype(F16), "stratum")
-    met, rest = lax.optimization_barrier((met, rest))
-    met, rest = met.astype(F32), rest.astype(F32)
+    met = met.astype(F32)
     sent = call(
         functools.partial(gather_kernel, total),
         shape((inners * (PAIR + 2 * piece), LANES), F32),
@@ -503,7 +506,7 @@
         functools.partial(second_kernel, total),
         (shape((inners * (PAIR + piece), LANES), F32), users_shape, block_shape, errors_shape),
         [vm, vm, vm, vm, vm, sm, sm, sm],
-        got, user_factors, mid, rest, tile_values, tile_rows, tile_cols, tile_count,
+        got, user_factors, mid, rest.astype(F32), tile_values, tile_rows, tile_cols, tile_count,
         scratch=[packed, users_bf, pltpu.VMEM(block_shape.shape, F32)],
     )
     sums, state = lax.optimization_barrier((sums.astype(F16), state))

time: 163 us -> 163 us (level)
  blocking collectives: 0 us -> 20.8 us
  waiting for transfers between devices: 72.4 us -> 59.5 us
  starting transfers between devices: 68.7 us -> 61.4 us
    all_to_all x0 -> x1, blocking collectives: none -> 20.8 us  [exchanged(): return lax.all_to_all(x, axis, 0, 0, tiled=True)]
    all_to_all x5 -> x4, waiting for transfers between devices: 48.4 us -> 37.4 us  [exchanged(): return lax.all_to_all(x, axis, 0, 0, tiled=True)]
    all_to_all x5 -> x4, starting transfers between devices: 52.4 us -> 42.4 us  [exchanged(): return lax.all_to_all(x, axis, 0, 0, tiled=True)]
    ppermute x3 -> x4, starting transfers between devices: 8.04 us -> 11 us  [swapped(): return lax.ppermute(x, 'pair', [(0, 1), (1, 0)])]
    ppermute x3 -> x4, waiting for transfers between devices: 19.6 us -> 17.4 us  [swapped(): return lax.ppermute(x, 'pair', [(0, 1), (1, 0)])]
  transfers between devices with their start and end apart: 10 -> 10, of which waited for: 6 -> 6; matrix products, arithmetic and copies ran while one was open for 1% -> 0% of each run, Pallas kernels for 2% -> 2%
where the time goes in v8:
time: 163 us; the launch traced here: 162 us
  starting transfers between devices  61.4 us (38%)
  waiting for transfers between devices  59.5 us (37%)
  blocking collectives  20.8 us (13%)
  Pallas kernels  12 us (7%)
  other arithmetic  3.81 us (2%)
  local copies, waits for them, and re-layouts  3.68 us (2%)
    all_to_all x4, starting transfers between devices, exchanged(): return lax.all_to_all(x, axis, 0, 0, tiled=True)  42.4 us
    all_to_all x4, waiting for transfers between devices, exchanged(): return lax.all_to_all(x, axis, 0, 0, tiled=True)  37.4 us
    all_to_all x1, blocking collectives, exchanged(): return lax.all_to_all(x, axis, 0, 0, tiled=True)  20.8 us
    ppermute x4, waiting for transfers between devices, swapped(): return lax.ppermute(x, 'pair', [(0, 1), (1, 0)])  17.4 us
    pallas_call x9, Pallas kernels, call(): pl.pallas_call(kernel, out_shape=out_shape, in_specs=specs, out_specs=jax...  12 us
    ppermute x4, starting transfers between devices, swapped(): return lax.ppermute(x, 'pair', [(0, 1), (1, 0)])  11 us
    ppermute x2, starting transfers between devices, shards(): state = lax.ppermute(state, 'stratum', onward)  7.93 us
    ppermute x2, waiting for transfers between devices, shards(): state = lax.ppermute(state, 'stratum', onward)  4.66 us
  transfers between devices with their start and end apart: 10, of which 6 were waited for; matrix products, arithmetic and copies ran while one was open for 0% of the time, Pallas kernels for 2%

profile of v8, /device:TPU:7, one launch (start us, length us, event | category | flops | bytes accessed | tf_op | source)
XLA Modules:
  0.0 162.0 jit_solution(15829156486157964617)
XLA Ops:
  0.6 0.0 copy-start.6
  0.6 0.0 copy-start.5
  0.7 0.0 copy-start
  0.7 0.0 copy-start.1
  0.7 1.4 copy.11.refs_6_.count
  2.1 2.1 %shard_map.103 = (bf16[816,128]{1,0:T(8,128)(2,1)}, bf16[784,128]{1,0:T(8,128)(2,1)}, bf16[768,128]{1,0:T(8,128)(2,1)}) custom-call(f32[16,256]{1,0:T(8,128)} %held.1, s32[2,4]{1,0:T(2,128)} %ids.1, f32[512,256]{1,0:T(8,128)} %users.5, bf16[2,8,128,128]{3,2,1,0:T(8,128)(2,1)} %values.3, s32[2,8]{1,0:T(2,128)} %rows.7, s32[2,8]{1,0:T(2,128)} %cols.7, ...), custom_call_target="tpu_custom_call" | custom-call | tf_op jit(solution)/shard_map/pallas_call | solution.py:395
  4.2 17.1 %all-to-all-start = ((bf16[24,17,2,128]{3,2,1,0:T(2,128)(2,1)}), bf16[24,17,2,128]{3,2,1,0:T(2,128)(2,1)S(1)}, u32[]{:S(2)}, u32[]{:S(2)}) async-start(bf16[24,17,2,128]{3,2,1,0:T(2,128)(2,1)} %bitcast.11), calls=%async_computation | async-start | bytes 417792 | tf_op jit(solution)/shard_map/all_to_all | solution.py:406
  21.3 3.2 %collective-permute-start = (bf16[784,128]{1,0:T(8,128)(2,1)}, bf16[784,128]{1,0:T(8,128)(2,1)S(1)}, u32[]{:S(2)}, u32[]{:S(2)}) collective-permute-start(bf16[784,128]{1,0:T(8,128)(2,1)} %get-tuple-element.23), channel_id=1, source_target_pairs={{0,1},{1,0},{2,3},{3,2},{4,5},{5,4},{6,7},{7,6},{8,9},{9,8},{10,11... | collective-permute-start | bytes 602120 | tf_op jit(solution)/shard_map/ppermute | solution.py:415
  24.5 2.1 %collective-permute-start.1 = (bf16[768,128]{1,0:T(8,128)(2,1)}, bf16[768,128]{1,0:T(8,128)(2,1)S(1)}, u32[]{:S(2)}, u32[]{:S(2)}) collective-permute-start(bf16[768,128]{1,0:T(8,128)(2,1)} %get-tuple-element.24), channel_id=1, source_target_pairs={{0,1},{1,0},{2,3},{3,2},{4,5},{5,4},{6,7},{7,6},{8,9},{9,8},{10,11... | collective-permute-start | bytes 589832 | tf_op jit(solution)/shard_map/ppermute | solution.py:415
  26.6 8.7 %collective-permute-done.1.packet_too = bf16[768,128]{1,0:T(8,128)(2,1)S(1)} collective-permute-done((bf16[768,128]{1,0:T(8,128)(2,1)}, bf16[768,128]{1,0:T(8,128)(2,1)S(1)}, u32[]{:S(2)}, u32[]{:S(2)}) %collective-permute-start.1) | collective-permute-done | bytes 196640 | tf_op jit(solution)/shard_map/ppermute | solution.py:415
  35.3 0.0 collective-permute-done.packet
  35.3 0.0 all-to-all-done
  35.3 0.0 copy-done.6
  35.3 0.0 copy-done.5
  35.4 1.8 %shard_map.104 = (f32[24,32,128]{2,1,0:T(8,128)S(1)}, bf16[768,256]{1,0:T(8,128)(2,1)S(1)}, bf16[8,128,128]{2,1,0:T(8,128)(2,1)S(1)}, bf16[8,128,128]{2,1,0:T(8,128)(2,1)S(1)}) custom-call(bf16[816,128]{1,0:T(8,128)(2,1)S(1)} %bitcast.8, f32[512,256]{1,0:T(8,128)S(1)} %copy-done, bf16[784,128]{1,0:T(8,128)(2,1)S(1)} %collective-permute-done.packet, ...), custom_call_target="tpu_custom_call" | custom-call | tf_op jit(solution)/shard_map/pallas_call | solution.py:395
  37.2 0.0 copy-start.2
  37.2 0.7 copy-done.2
  37.9 0.7 convert_element_type.34
  38.6 10.6 %all-to-all-start.1 = ((f16[24,32,128]{2,1,0:T(8,128)(2,1)}), f16[24,32,128]{2,1,0:T(8,128)(2,1)S(1)}, u32[]{:S(2)}, u32[]{:S(2)}) async-start(f16[24,32,128]{2,1,0:T(8,128)(2,1)} %convert_element_type.34), calls=%async_computation.1 | async-start | bytes 393216 | tf_op jit(solution)/shard_map/all_to_all | solution.py:406
  49.2 0.0 copy-start.3
  49.2 0.9 copy-done.3
  50.2 1.4 shard_map.105
  51.6 2.8 %collective-permute-start.2 = (f32[8,128]{1,0:T(8,128)S(1)}, f32[8,128]{1,0:T(8,128)S(1)}, u32[]{:S(2)}, u32[]{:S(2)}) collective-permute-start(f32[8,128]{1,0:T(8,128)S(1)} %get-tuple-element.30), channel_id=1, source_target_pairs={{0,1},{1,0},{2,3},{3,2},{4,5},{5,4},{6,7},{7,6},{8,9},{9,8},{10,11... | collective-permute-start | bytes 12296 | tf_op jit(solution)/shard_map/ppermute | solution.py:415
  54.4 6.3 %all-to-all-done.1 = f16[24,32,128]{2,1,0:T(8,128)(2,1)S(1)} async-done(((f16[24,32,128]{2,1,0:T(8,128)(2,1)}), f16[24,32,128]{2,1,0:T(8,128)(2,1)S(1)}, u32[]{:S(2)}, u32[]{:S(2)}) %all-to-all-start.1) | async-done | bytes 196640 | tf_op jit(solution)/shard_map/all_to_all | solution.py:406
  60.8 0.0 collective-permute-done.2.their_piece
  60.8 0.6 shard_map.106
  61.5 20.8 %all_to_all.25 = f16[16,48,128]{2,1,0:T(8,128)(2,1)S(1)} all-to-all(f16[16,48,128]{2,1,0:T(8,128)(2,1)S(1)} %convert_element_type.36), channel_id=1, replica_groups=mesh['stratum'=16,'far'=12,'near'=2,'pair'=2] {'stratum'}, dimensions={0} | all-to-all | bytes 393216 | tf_op jit(solution)/shard_map/all_to_all | solution.py:406
  82.4 0.5 shard_map.107
  82.8 0.9 convert_element_type.38
  83.7 8.1 %all-to-all-start.3 = ((f16[48,22,2,128]{3,2,1,0:T(2,128)(2,1)}), f16[48,22,2,128]{3,2,1,0:T(2,128)(2,1)}, u32[]{:S(2)}, u32[]{:S(2)}) async-start(f16[48,22,2,128]{3,2,1,0:T(2,128)(2,1)} %bitcast.2), calls=%async_computation.3 | async-start | bytes 1081344 | tf_op jit(solution)/shard_map/all_to_all | solution.py:406
  91.8 0.1 multiply_convert_fusion
  91.9 3.0 %collective-permute-start.3 = (f16[512,256]{1,0:T(8,128)(2,1)S(1)}, f16[512,256]{1,0:T(8,128)(2,1)S(1)}, u32[]{:S(2)}, u32[]{:S(2)}) collective-permute-start(f16[512,256]{1,0:T(8,128)(2,1)S(1)} %multiply_convert_fusion), channel_id=1, source_target_pairs={{0,1},{1,0},{2,3},{3,2},{4,5},{5,4},{6,7},{7,6},{8,9},{9,8},{10,11... | collective-permute-start | bytes 786440 | tf_op jit(solution)/shard_map/ppermute | solution.py:415
  94.9 8.7 %collective-permute-done.3 = f16[512,256]{1,0:T(8,128)(2,1)S(1)} collective-permute-done((f16[512,256]{1,0:T(8,128)(2,1)S(1)}, f16[512,256]{1,0:T(8,128)(2,1)S(1)}, u32[]{:S(2)}, u32[]{:S(2)}) %collective-permute-start.3) | collective-permute-done | bytes 262176 | tf_op jit(solution)/shard_map/ppermute | solution.py:415
  103.6 12.6 %all-to-all-done.3 = f16[48,22,2,128]{3,2,1,0:T(2,128)(2,1)} async-done(((f16[48,22,2,128]{3,2,1,0:T(2,128)(2,1)}), f16[48,22,2,128]{3,2,1,0:T(2,128)(2,1)}, u32[]{:S(2)}, u32[]{:S(2)}) %all-to-all-start.3) | async-done | bytes 540704 | tf_op jit(solution)/shard_map/all_to_all | solution.py:406
  116.2 1.1 convert.3.got
  117.3 3.1 %shard_map.108 = (f32[1824,128]{1,0:T(8,128)S(1)}, f32[512,256]{1,0:T(8,128)S(1)}, bf16[768,256]{1,0:T(8,128)(2,1)S(1)}, bf16[8,128,128]{2,1,0:T(8,128)(2,1)S(1)}) custom-call(f32[2112,128]{1,0:T(8,128)S(1)} %convert.3.got, f32[512,256]{1,0:T(8,128)S(1)} %copy-done, f32[512,256]{1,0:T(8,128)S(1)} %get-tuple-element.32.mid, ...), custom_call_target="tpu_custom_call" | custom-call | tf_op jit(solution)/shard_map/pallas_call | solution.py:395
  120.4 0.8 convert_element_type.43
  121.3 6.6 %all-to-all-start.4 = ((f16[48,19,2,128]{3,2,1,0:T(2,128)(2,1)}), f16[48,19,2,128]{3,2,1,0:T(2,128)(2,1)S(1)}, u32[]{:S(2)}, u32[]{:S(2)}) async-start(f16[48,19,2,128]{3,2,1,0:T(2,128)(2,1)} %bitcast.4), calls=%async_computation.4 | async-start | bytes 933888 | tf_op jit(solution)/shard_map/all_to_all | solution.py:406
  127.9 3.2 %collective-permute-start.4 = (f32[32,256]{1,0:T(8,128)S(1)}, f32[32,256]{1,0:T(8,128)S(1)}, u32[]{:S(2)}, u32[]{:S(2)}) collective-permute-start(f32[32,256]{1,0:T(8,128)S(1)} %get-tuple-element.40), channel_id=1, source_target_pairs={{48,0},{96,48},{144,96},{192,144},{240,192},{288,240},{336,288},{3... | collective-permute-start | bytes 98312 | tf_op jit(solution)/shard_map/ppermute | solution.py:513
  131.1 18.5 %all-to-all-done.4 = f16[48,19,2,128]{3,2,1,0:T(2,128)(2,1)S(1)} async-done(((f16[48,19,2,128]{3,2,1,0:T(2,128)(2,1)}), f16[48,19,2,128]{3,2,1,0:T(2,128)(2,1)S(1)}, u32[]{:S(2)}, u32[]{:S(2)}) %all-to-all-start.4) | async-done | bytes 466976 | tf_op jit(solution)/shard_map/all_to_all | solution.py:406
  149.6 0.1 convert.2.got
  149.7 0.0 collective-permute-done.4.state
  149.7 0.1 shard_map.111
  149.8 4.7 %collective-permute-start.5 = (f32[32,256]{1,0:T(8,128)S(1)}, f32[32,256]{1,0:T(8,128)S(1)}, u32[]{:S(2)}, u32[]{:S(2)}) collective-permute-start(f32[32,256]{1,0:T(8,128)S(1)} %shard_map.111), channel_id=1, source_target_pairs={{48,0},{96,48},{144,96},{192,144},{240,192},{288,240},{336,288},{3... | collective-permute-start | bytes 98312 | tf_op jit(solution)/shard_map/ppermute | solution.py:520
  154.5 0.9 shard_map.109.users
  155.5 1.3 shard_map.110
  156.8 4.7 %collective-permute-done.5 = f32[32,256]{1,0:T(8,128)S(1)} collective-permute-done((f32[32,256]{1,0:T(8,128)S(1)}, f32[32,256]{1,0:T(8,128)S(1)}, u32[]{:S(2)}, u32[]{:S(2)}) %collective-permute-start.5) | collective-permute-done | bytes 32800 | tf_op jit(solution)/shard_map/ppermute | solution.py:520
  161.4 0.6 fusion
  (14 shorter events, 0.1 us)
Async XLA Ops:
  0.6 34.7 %copy-start.6 = (s32[2,8]{1,0:T(2,128)S(1)}, s32[2,8]{1,0:T(2,128)}, u32[]{:S(2)}) copy-start(s32[2,8]{1,0:T(2,128)} %cols.7) | copy-start | bytes 196
  0.6 34.7 %copy-start.5 = (s32[2,8]{1,0:T(2,128)S(1)}, s32[2,8]{1,0:T(2,128)}, u32[]{:S(2)}) copy-start(s32[2,8]{1,0:T(2,128)} %rows.7) | copy-start | bytes 196
  0.7 34.7 %copy-start = (f32[512,256]{1,0:T(8,128)S(1)}, f32[512,256]{1,0:T(8,128)}, u32[]{:S(2)}) copy-start(f32[512,256]{1,0:T(8,128)} %users.5) | copy-start | bytes 1572868
  0.7 34.7 %copy-start.1 = (bf16[2,8,128,128]{3,2,1,0:T(8,128)(2,1)S(1)}, bf16[2,8,128,128]{3,2,1,0:T(8,128)(2,1)}, u32[]{:S(2)}) copy-start(bf16[2,8,128,128]{3,2,1,0:T(8,128)(2,1)} %values.3) | copy-start | bytes 1572868
  2.1 33.3 %copy-start.8 = (s32[2,1]{1,0:T(2,128)S(1)}, s32[2,1]{1,0:T(2,128)}, u32[]{:S(2)}) copy-start(s32[2,1]{1,0:T(2,128)} %copy.11.refs_6_.count) | copy-start | bytes 28
  4.2 31.2 %all-to-all-start = ((bf16[24,17,2,128]{3,2,1,0:T(2,128)(2,1)}), bf16[24,17,2,128]{3,2,1,0:T(2,128)(2,1)S(1)}, u32[]{:S(2)}, u32[]{:S(2)}) async-start(bf16[24,17,2,128]{3,2,1,0:T(2,128)(2,1)} %bitcast.11), calls=%async_computation | async-start | bytes 417792 | tf_op jit(solution)/shard_map/all_to_all | solution.py:406
  21.3 14.0 %collective-permute-start = (bf16[784,128]{1,0:T(8,128)(2,1)}, bf16[784,128]{1,0:T(8,128)(2,1)S(1)}, u32[]{:S(2)}, u32[]{:S(2)}) collective-permute-start(bf16[784,128]{1,0:T(8,128)(2,1)} %get-tuple-element.23), channel_id=1, source_target_pairs={{0,1},{1,0},{2,3},{3,2},{4,5},{5,4},{6,7},{7,6},{8,9},{9,8},{10,11... | collective-permute-start | bytes 602120 | tf_op jit(solution)/shard_map/ppermute | solution.py:415
  24.5 10.8 %collective-permute-start.1 = (bf16[768,128]{1,0:T(8,128)(2,1)}, bf16[768,128]{1,0:T(8,128)(2,1)S(1)}, u32[]{:S(2)}, u32[]{:S(2)}) collective-permute-start(bf16[768,128]{1,0:T(8,128)(2,1)} %get-tuple-element.24), channel_id=1, source_target_pairs={{0,1},{1,0},{2,3},{3,2},{4,5},{5,4},{6,7},{7,6},{8,9},{9,8},{10,11... | collective-permute-start | bytes 589832 | tf_op jit(solution)/shard_map/ppermute | solution.py:415
  37.2 0.7 copy-start.2
  38.6 22.1 %all-to-all-start.1 = ((f16[24,32,128]{2,1,0:T(8,128)(2,1)}), f16[24,32,128]{2,1,0:T(8,128)(2,1)S(1)}, u32[]{:S(2)}, u32[]{:S(2)}) async-start(f16[24,32,128]{2,1,0:T(8,128)(2,1)} %convert_element_type.34), calls=%async_computation.1 | async-start | bytes 393216 | tf_op jit(solution)/shard_map/all_to_all | solution.py:406
  49.2 1.0 copy-start.3
  50.2 10.6 %copy-start.4 = (f32[16,256]{1,0:T(8,128)S(1)}, f32[16,256]{1,0:T(8,128)}, u32[]{:S(2)}) copy-start(f32[16,256]{1,0:T(8,128)} %held.1) | copy-start | bytes 49156
  50.2 10.6 %copy-start.7 = (f32[16,256]{1,0:T(8,128)S(1)}, f32[16,256]{1,0:T(8,128)}, u32[]{:S(2)}) copy-start(f32[16,256]{1,0:T(8,128)} %accum.1) | copy-start | bytes 49156
  50.2 10.6 %copy-start.9 = (s32[2,4]{1,0:T(2,128)S(1)}, s32[2,4]{1,0:T(2,128)}, u32[]{:S(2)}) copy-start(s32[2,4]{1,0:T(2,128)} %ids.1) | copy-start | bytes 100
  51.6 9.2 %collective-permute-start.2 = (f32[8,128]{1,0:T(8,128)S(1)}, f32[8,128]{1,0:T(8,128)S(1)}, u32[]{:S(2)}, u32[]{:S(2)}) collective-permute-start(f32[8,128]{1,0:T(8,128)S(1)} %get-tuple-element.30), channel_id=1, source_target_pairs={{0,1},{1,0},{2,3},{3,2},{4,5},{5,4},{6,7},{7,6},{8,9},{9,8},{10,11... | collective-permute-start | bytes 12296 | tf_op jit(solution)/shard_map/ppermute | solution.py:415
  83.7 32.4 %all-to-all-start.3 = ((f16[48,22,2,128]{3,2,1,0:T(2,128)(2,1)}), f16[48,22,2,128]{3,2,1,0:T(2,128)(2,1)}, u32[]{:S(2)}, u32[]{:S(2)}) async-start(f16[48,22,2,128]{3,2,1,0:T(2,128)(2,1)} %bitcast.2), calls=%async_computation.3 | async-start | bytes 1081344 | tf_op jit(solution)/shard_map/all_to_all | solution.py:406
  91.9 11.7 %collective-permute-start.3 = (f16[512,256]{1,0:T(8,128)(2,1)S(1)}, f16[512,256]{1,0:T(8,128)(2,1)S(1)}, u32[]{:S(2)}, u32[]{:S(2)}) collective-permute-start(f16[512,256]{1,0:T(8,128)(2,1)S(1)} %multiply_convert_fusion), channel_id=1, source_target_pairs={{0,1},{1,0},{2,3},{3,2},{4,5},{5,4},{6,7},{7,6},{8,9},{9,8},{10,11... | collective-permute-start | bytes 786440 | tf_op jit(solution)/shard_map/ppermute | solution.py:415
  121.3 28.4 %all-to-all-start.4 = ((f16[48,19,2,128]{3,2,1,0:T(2,128)(2,1)}), f16[48,19,2,128]{3,2,1,0:T(2,128)(2,1)S(1)}, u32[]{:S(2)}, u32[]{:S(2)}) async-start(f16[48,19,2,128]{3,2,1,0:T(2,128)(2,1)} %bitcast.4), calls=%async_computation.4 | async-start | bytes 933888 | tf_op jit(solution)/shard_map/all_to_all | solution.py:406
  127.9 21.8 %collective-permute-start.4 = (f32[32,256]{1,0:T(8,128)S(1)}, f32[32,256]{1,0:T(8,128)S(1)}, u32[]{:S(2)}, u32[]{:S(2)}) collective-permute-start(f32[32,256]{1,0:T(8,128)S(1)} %get-tuple-element.40), channel_id=1, source_target_pairs={{48,0},{96,48},{144,96},{192,144},{240,192},{288,240},{336,288},{3... | collective-permute-start | bytes 98312 | tf_op jit(solution)/shard_map/ppermute | solution.py:513
  149.8 11.6 %collective-permute-start.5 = (f32[32,256]{1,0:T(8,128)S(1)}, f32[32,256]{1,0:T(8,128)S(1)}, u32[]{:S(2)}, u32[]{:S(2)}) collective-permute-start(f32[32,256]{1,0:T(8,128)S(1)} %shard_map.111), channel_id=1, source_target_pairs={{48,0},{96,48},{144,96},{192,144},{240,192},{288,240},{336,288},{3... | collective-permute-start | bytes 98312 | tf_op jit(solution)/shard_map/ppermute | solution.py:520

commit v9 on v8

--- a/solution.py
+++ b/solution.py
@@ -144,7 +144,7 @@
         at = size + k // 2 * LANES
         packets[k % 2][at : at + LANES, :] = jnp.where(first, values[k].astype(F32), other).astype(BF16)
     lane = lax.broadcasted_iota(jnp.int32, (16, LANES), 1)
-    lists = jnp.where(lane == 2 * slots, count[0, 0], 0)
+    lists = jnp.where(lane == 2 * slots, count[0], 0)
     for k in range(slots):
         lists = jnp.where(lane == k, rows[0, k], jnp.where(lane == slots + k, cols[0, k], lists))
     at = size + slots // 4 * LANES
@@ -228,7 +228,7 @@
         grads[pl.ds(at, part.shape[0]), :] += part
 
     item_grads(
-        users_bf, block, lambda k: values[0, k], at_step(rows, 0), at_step(cols, 0), count[0, 0],
+        users_bf, block, lambda k: values[0, k], at_step(rows, 0), at_step(cols, 0), count[0],
         errors, owned, GRAD_SCALE, add,
     )
     item_grads(
@@ -354,7 +354,7 @@
         grads[pl.ds(at, part.shape[0]), :] += part
 
     item_grads(
-        users_bf, block, lambda k: values[1, k], at_step(rows, 1), at_step(cols, 1), count[1, 0],
+        users_bf, block, lambda k: values[1, k], at_step(rows, 1), at_step(cols, 1), count[1],
         errors, None, None, add,
     )
     full = full * (GRAM_SCALE / GRAM_INNER_SCALE / total)
@@ -439,6 +439,7 @@
     packed = pltpu.VMEM((inners * piece, LANES), F32)
 
     slots = tile_values.shape[1]
+    tile_count = tile_count.reshape(-1)
     packet_rows = user_factors.shape[0] + slots // 4 * LANES
     sent, packet, packet_too = call(
         start_kernel,
@@ -501,7 +502,10 @@
         met,
         scratch=[packed],
     ).astype(F16)
-    got = chunks_exchanged(sent, INNER).astype(F32)
+    got = chunks_exchanged(sent, INNER)
+    state = lax.ppermute(state, "stratum", onward)
+    got, rest, state = lax.optimization_barrier((got, rest, state))
+    got = got.astype(F32)
     sums, mid, block, errors = call(
         functools.partial(second_kernel, total),
         (shape((inners * (PAIR + piece), LANES), F32), users_shape, block_shape, errors_shape),
@@ -509,9 +513,7 @@
         got, user_factors, mid, rest.astype(F32), tile_values, tile_rows, tile_cols, tile_count,
         scratch=[packed, users_bf, pltpu.VMEM(block_shape.shape, F32)],
     )
-    sums, state = lax.optimization_barrier((sums.astype(F16), state))
-    state = lax.ppermute(state, "stratum", onward)
-    got = chunks_exchanged(sums, INNER).astype(F32)
+    got = chunks_exchanged(sums.astype(F16), INNER).astype(F32)
     users = call(
         second_users_kernel, users_shape, [vm, vm, sm, sm, vm],
         block, mid, tile_rows, tile_cols, errors, scratch=[users_f32],

time: 163 us -> 158 us (0.969)
  blocking collectives: 20.8 us -> 49.4 us
  waiting for transfers between devices: 59.5 us -> 37.8 us
  starting transfers between devices: 61.4 us -> 53.6 us
  local copies, waits for them, and re-layouts: 3.68 us -> 0.65 us
    all_to_all x1 -> x2, blocking collectives: 20.8 us -> 49.4 us  [exchanged(): return lax.all_to_all(x, axis, 0, 0, tiled=True)]
    all_to_all x4 -> x3, waiting for transfers between devices: 37.4 us -> 15 us  [exchanged(): return lax.all_to_all(x, axis, 0, 0, tiled=True)]
    all_to_all x4 -> x3, starting transfers between devices: 42.4 us -> 34.6 us  [exchanged(): return lax.all_to_all(x, axis, 0, 0, tiled=True)]
    ppermute x2, waiting for transfers between devices: 4.66 us -> 8.71 us  [shards(): state = lax.ppermute(state, 'stratum', onward)]
    ppermute x4, waiting for transfers between devices: 17.4 us -> 14.1 us  [swapped(): return lax.ppermute(x, 'pair', [(0, 1), (1, 0)])]
    unnamed x21 -> x16, local copies, waits for them, and re-layouts: 3.07 us -> 0.04 us
    convert_element_type x3, other arithmetic: 2.01 us -> 0.2 us  [the longest x2 0.13 us: shards(): got = chunks_exchanged(sums.astype(F16), INNER).astype(F32)]
  transfers between devices with their start and end apart: 10 -> 9, of which waited for: 6 -> 6; matrix products, arithmetic and copies ran while one was open for 0% -> 1% of each run, Pallas kernels for 2% -> 2%
where the time goes in v9:
time: 158 us; the launch traced here: 157 us
  starting transfers between devices  53.6 us (34%)
  blocking collectives  49.4 us (31%)
  waiting for transfers between devices  37.8 us (24%)
  Pallas kernels  12.1 us (8%)
  other arithmetic  2.9 us (2%)
    all_to_all x2, blocking collectives, exchanged(): return lax.all_to_all(x, axis, 0, 0, tiled=True)  49.4 us
    all_to_all x3, starting transfers between devices, exchanged(): return lax.all_to_all(x, axis, 0, 0, tiled=True)  34.6 us
    all_to_all x3, waiting for transfers between devices, exchanged(): return lax.all_to_all(x, axis, 0, 0, tiled=True)  15 us
    ppermute x4, waiting for transfers between devices, swapped(): return lax.ppermute(x, 'pair', [(0, 1), (1, 0)])  14.1 us
    pallas_call x9, Pallas kernels, call(): pl.pallas_call(kernel, out_shape=out_shape, in_specs=specs, out_specs=jax...  12.1 us
    ppermute x4, starting transfers between devices, swapped(): return lax.ppermute(x, 'pair', [(0, 1), (1, 0)])  11.1 us
    ppermute x2, waiting for transfers between devices, shards(): state = lax.ppermute(state, 'stratum', onward)  8.71 us
    ppermute x2, starting transfers between devices, shards(): state = lax.ppermute(state, 'stratum', onward)  7.9 us
  transfers between devices with their start and end apart: 9, of which 6 were waited for; matrix products, arithmetic and copies ran while one was open for 1% of the time, Pallas kernels for 2%

profile of v9, /device:TPU:7, one launch (start us, length us, event | category | flops | bytes accessed | tf_op | source)
XLA Modules:
  0.0 157.4 jit_solution(7712828312831657554)
XLA Ops:
  0.6 0.0 copy-start.4
  0.6 0.0 copy-start.3
  0.7 0.0 copy-start
  0.7 0.0 copy-start.1
  0.7 0.0 copy-start.6
  0.7 2.2 %shard_map.103 = (bf16[816,128]{1,0:T(8,128)(2,1)}, bf16[784,128]{1,0:T(8,128)(2,1)}, bf16[768,128]{1,0:T(8,128)(2,1)}) custom-call(f32[16,256]{1,0:T(8,128)} %held.1, s32[2,4]{1,0:T(2,128)} %ids.1, f32[512,256]{1,0:T(8,128)} %users.5, bf16[2,8,128,128]{3,2,1,0:T(8,128)(2,1)} %values.3, s32[2,8]{1,0:T(2,128)} %rows.7, s32[2,8]{1,0:T(2,128)} %cols.7, s32[2]{0:T(128)} %bitcast.10), custom_call_target="tpu_custom_call" | custom-call | tf_op jit(solution)/shard_map/pallas_call | solution.py:395
  2.9 17.1 %all-to-all-start = ((bf16[24,17,2,128]{3,2,1,0:T(2,128)(2,1)}), bf16[24,17,2,128]{3,2,1,0:T(2,128)(2,1)S(1)}, u32[]{:S(2)}, u32[]{:S(2)}) async-start(bf16[24,17,2,128]{3,2,1,0:T(2,128)(2,1)} %bitcast.17), calls=%async_computation | async-start | bytes 417792 | tf_op jit(solution)/shard_map/all_to_all | solution.py:406
  20.0 3.2 %collective-permute-start = (bf16[784,128]{1,0:T(8,128)(2,1)}, bf16[784,128]{1,0:T(8,128)(2,1)S(1)}, u32[]{:S(2)}, u32[]{:S(2)}) collective-permute-start(bf16[784,128]{1,0:T(8,128)(2,1)} %get-tuple-element.24), channel_id=1, source_target_pairs={{0,1},{1,0},{2,3},{3,2},{4,5},{5,4},{6,7},{7,6},{8,9},{9,8},{10,11... | collective-permute-start | bytes 602120 | tf_op jit(solution)/shard_map/ppermute | solution.py:415
  23.2 2.1 %collective-permute-start.1 = (bf16[768,128]{1,0:T(8,128)(2,1)}, bf16[768,128]{1,0:T(8,128)(2,1)S(1)}, u32[]{:S(2)}, u32[]{:S(2)}) collective-permute-start(bf16[768,128]{1,0:T(8,128)(2,1)} %get-tuple-element.25), channel_id=1, source_target_pairs={{0,1},{1,0},{2,3},{3,2},{4,5},{5,4},{6,7},{7,6},{8,9},{9,8},{10,11... | collective-permute-start | bytes 589832 | tf_op jit(solution)/shard_map/ppermute | solution.py:415
  25.3 8.7 %collective-permute-done.1.packet_too = bf16[768,128]{1,0:T(8,128)(2,1)S(1)} collective-permute-done((bf16[768,128]{1,0:T(8,128)(2,1)}, bf16[768,128]{1,0:T(8,128)(2,1)S(1)}, u32[]{:S(2)}, u32[]{:S(2)}) %collective-permute-start.1) | collective-permute-done | bytes 196640 | tf_op jit(solution)/shard_map/ppermute | solution.py:415
  34.0 0.0 collective-permute-done.packet
  34.0 0.0 all-to-all-done
  34.0 0.0 copy-done.3
  34.0 0.0 copy-done
  34.0 0.0 copy-done.1
  34.1 1.8 %shard_map.104 = (f32[24,32,128]{2,1,0:T(8,128)S(1)}, bf16[768,256]{1,0:T(8,128)(2,1)S(1)}, bf16[8,128,128]{2,1,0:T(8,128)(2,1)S(1)}, bf16[8,128,128]{2,1,0:T(8,128)(2,1)S(1)}) custom-call(bf16[816,128]{1,0:T(8,128)(2,1)S(1)} %bitcast.8, f32[512,256]{1,0:T(8,128)S(1)} %copy-done, bf16[784,128]{1,0:T(8,128)(2,1)S(1)} %collective-permute-done.packet, ...), custom_call_target="tpu_custom_call" | custom-call | tf_op jit(solution)/shard_map/pallas_call | solution.py:395
  35.9 0.7 convert_element_type.32
  36.6 10.7 %all-to-all-start.1 = ((f16[24,32,128]{2,1,0:T(8,128)(2,1)}), f16[24,32,128]{2,1,0:T(8,128)(2,1)}, u32[]{:S(2)}, u32[]{:S(2)}) async-start(f16[24,32,128]{2,1,0:T(8,128)(2,1)} %convert_element_type.32), calls=%async_computation.1 | async-start | bytes 393216 | tf_op jit(solution)/shard_map/all_to_all | solution.py:406
  47.3 0.0 copy-start.2
  47.3 0.0 copy-start.5
  47.3 0.0 copy-start.7
  47.3 1.5 shard_map.105
  48.8 2.8 %collective-permute-start.2 = (f32[8,128]{1,0:T(8,128)S(1)}, f32[8,128]{1,0:T(8,128)S(1)}, u32[]{:S(2)}, u32[]{:S(2)}) collective-permute-start(f32[8,128]{1,0:T(8,128)S(1)} %get-tuple-element.31), channel_id=1, source_target_pairs={{0,1},{1,0},{2,3},{3,2},{4,5},{5,4},{6,7},{7,6},{8,9},{9,8},{10,11... | collective-permute-start | bytes 12296 | tf_op jit(solution)/shard_map/ppermute | solution.py:415
  51.6 7.2 %all-to-all-done.1 = f16[24,32,128]{2,1,0:T(8,128)(2,1)} async-done(((f16[24,32,128]{2,1,0:T(8,128)(2,1)}), f16[24,32,128]{2,1,0:T(8,128)(2,1)}, u32[]{:S(2)}, u32[]{:S(2)}) %all-to-all-start.1) | async-done | bytes 196640 | tf_op jit(solution)/shard_map/all_to_all | solution.py:406
  58.8 1.0 convert_element_type.33.got
  59.8 0.0 collective-permute-done.2.their_piece
  59.8 0.6 shard_map.106
  60.5 20.8 %all_to_all.25 = f16[16,48,128]{2,1,0:T(8,128)(2,1)S(1)} all-to-all(f16[16,48,128]{2,1,0:T(8,128)(2,1)S(1)} %convert_element_type.34), channel_id=1, replica_groups=mesh['stratum'=16,'far'=12,'near'=2,'pair'=2] {'stratum'}, dimensions={0} | all-to-all | bytes 393216 | tf_op jit(solution)/shard_map/all_to_all | solution.py:406
  81.4 0.5 shard_map.107
  81.8 0.9 convert_element_type.36
  82.7 6.8 %all-to-all-start.3 = ((f16[48,22,2,128]{3,2,1,0:T(2,128)(2,1)}), f16[48,22,2,128]{3,2,1,0:T(2,128)(2,1)S(1)}, u32[]{:S(2)}, u32[]{:S(2)}) async-start(f16[48,22,2,128]{3,2,1,0:T(2,128)(2,1)} %bitcast.14), calls=%async_computation.3 | async-start | bytes 1081344 | tf_op jit(solution)/shard_map/all_to_all | solution.py:406
  89.6 0.1 multiply_convert_fusion
  89.6 3.0 %collective-permute-start.3 = (f16[512,256]{1,0:T(8,128)(2,1)S(1)}, f16[512,256]{1,0:T(8,128)(2,1)S(1)}, u32[]{:S(2)}, u32[]{:S(2)}) collective-permute-start(f16[512,256]{1,0:T(8,128)(2,1)S(1)} %multiply_convert_fusion), channel_id=1, source_target_pairs={{0,1},{1,0},{2,3},{3,2},{4,5},{5,4},{6,7},{7,6},{8,9},{9,8},{10,11... | collective-permute-start | bytes 786440 | tf_op jit(solution)/shard_map/ppermute | solution.py:415
  92.7 3.1 %collective-permute-start.4 = (f32[32,256]{1,0:T(8,128)S(1)}, f32[32,256]{1,0:T(8,128)S(1)}, u32[]{:S(2)}, u32[]{:S(2)}) collective-permute-start(f32[32,256]{1,0:T(8,128)S(1)} %get-tuple-element.34), channel_id=1, source_target_pairs={{48,0},{96,48},{144,96},{192,144},{240,192},{288,240},{336,288},{3... | collective-permute-start | bytes 98312 | tf_op jit(solution)/shard_map/ppermute | solution.py:506
  95.8 5.4 %collective-permute-done.3 = f16[512,256]{1,0:T(8,128)(2,1)S(1)} collective-permute-done((f16[512,256]{1,0:T(8,128)(2,1)S(1)}, f16[512,256]{1,0:T(8,128)(2,1)S(1)}, u32[]{:S(2)}, u32[]{:S(2)}) %collective-permute-start.3) | collective-permute-done | bytes 262176 | tf_op jit(solution)/shard_map/ppermute | solution.py:415
  101.2 4.5 %collective-permute-done.4.state = f32[32,256]{1,0:T(8,128)S(1)} collective-permute-done((f32[32,256]{1,0:T(8,128)S(1)}, f32[32,256]{1,0:T(8,128)S(1)}, u32[]{:S(2)}, u32[]{:S(2)}) %collective-permute-start.4) | collective-permute-done | bytes 32800 | tf_op jit(solution)/shard_map/ppermute | solution.py:506
  105.7 7.7 %all-to-all-done.3 = f16[48,22,2,128]{3,2,1,0:T(2,128)(2,1)S(1)} async-done(((f16[48,22,2,128]{3,2,1,0:T(2,128)(2,1)}), f16[48,22,2,128]{3,2,1,0:T(2,128)(2,1)S(1)}, u32[]{:S(2)}, u32[]{:S(2)}) %all-to-all-start.3) | async-done | bytes 540704 | tf_op jit(solution)/shard_map/all_to_all | solution.py:406
  113.5 0.1 convert_element_type.38.got
  113.5 3.1 %shard_map.108 = (f32[1824,128]{1,0:T(8,128)S(1)}, f32[512,256]{1,0:T(8,128)S(1)}, bf16[768,256]{1,0:T(8,128)(2,1)S(1)}, bf16[8,128,128]{2,1,0:T(8,128)(2,1)S(1)}) custom-call(f32[2112,128]{1,0:T(8,128)S(1)} %convert_element_type.38.got, f32[512,256]{1,0:T(8,128)S(1)} %copy-done, f32[512,256]{1,0:T(8,128)S(1)} %get-tuple-element.36.mid, ...), custom_call_target="tpu_custom_call" | custom-call | tf_op jit(solution)/shard_map/pallas_call | solution.py:395
  116.7 0.1 convert_element_type.40
  116.8 28.6 %all_to_all.26 = f16[48,19,2,128]{3,2,1,0:T(2,128)(2,1)S(1)} all-to-all(f16[48,19,2,128]{3,2,1,0:T(2,128)(2,1)S(1)} %bitcast.15), channel_id=1, replica_groups=mesh['stratum'=16,'far'=12,'near'=2,'pair'=2] {'far','near','pair'}, dimensions={0} | all-to-all | bytes 933888 | tf_op jit(solution)/shard_map/all_to_all | solution.py:406
  145.3 0.1 convert.1.got
  145.4 0.1 shard_map.111
  145.5 4.8 %collective-permute-start.5 = (f32[32,256]{1,0:T(8,128)S(1)}, f32[32,256]{1,0:T(8,128)S(1)}, u32[]{:S(2)}, u32[]{:S(2)}) collective-permute-start(f32[32,256]{1,0:T(8,128)S(1)} %shard_map.111), channel_id=1, source_target_pairs={{48,0},{96,48},{144,96},{192,144},{240,192},{288,240},{336,288},{3... | collective-permute-start | bytes 98312 | tf_op jit(solution)/shard_map/ppermute | solution.py:522
  150.3 0.9 shard_map.109.users
  151.2 1.3 shard_map.110
  152.5 4.3 %collective-permute-done.5 = f32[32,256]{1,0:T(8,128)S(1)} collective-permute-done((f32[32,256]{1,0:T(8,128)S(1)}, f32[32,256]{1,0:T(8,128)S(1)}, u32[]{:S(2)}, u32[]{:S(2)}) %collective-permute-start.5) | collective-permute-done | bytes 32800 | tf_op jit(solution)/shard_map/ppermute | solution.py:522
  156.8 0.6 fusion
  (8 shorter events, 0.1 us)
Async XLA Ops:
  0.6 33.4 %copy-start.4 = (s32[2,8]{1,0:T(2,128)S(1)}, s32[2,8]{1,0:T(2,128)}, u32[]{:S(2)}) copy-start(s32[2,8]{1,0:T(2,128)} %cols.7) | copy-start | bytes 196
  0.6 33.4 %copy-start.3 = (s32[2,8]{1,0:T(2,128)S(1)}, s32[2,8]{1,0:T(2,128)}, u32[]{:S(2)}) copy-start(s32[2,8]{1,0:T(2,128)} %rows.7) | copy-start | bytes 196
  0.7 33.4 %copy-start = (f32[512,256]{1,0:T(8,128)S(1)}, f32[512,256]{1,0:T(8,128)}, u32[]{:S(2)}) copy-start(f32[512,256]{1,0:T(8,128)} %users.5) | copy-start | bytes 1572868
  0.7 33.4 %copy-start.1 = (bf16[2,8,128,128]{3,2,1,0:T(8,128)(2,1)S(1)}, bf16[2,8,128,128]{3,2,1,0:T(8,128)(2,1)}, u32[]{:S(2)}) copy-start(bf16[2,8,128,128]{3,2,1,0:T(8,128)(2,1)} %values.3) | copy-start | bytes 1572868
  0.7 33.4 %copy-start.6 = (s32[2,1]{0,1:T(1,128)S(1)}, s32[2,1]{0,1:T(1,128)}, u32[]{:S(2)}) copy-start(s32[2,1]{0,1:T(1,128)} %param.14) | copy-start | bytes 28
  2.9 31.2 %all-to-all-start = ((bf16[24,17,2,128]{3,2,1,0:T(2,128)(2,1)}), bf16[24,17,2,128]{3,2,1,0:T(2,128)(2,1)S(1)}, u32[]{:S(2)}, u32[]{:S(2)}) async-start(bf16[24,17,2,128]{3,2,1,0:T(2,128)(2,1)} %bitcast.17), calls=%async_computation | async-start | bytes 417792 | tf_op jit(solution)/shard_map/all_to_all | solution.py:406
  20.0 14.0 %collective-permute-start = (bf16[784,128]{1,0:T(8,128)(2,1)}, bf16[784,128]{1,0:T(8,128)(2,1)S(1)}, u32[]{:S(2)}, u32[]{:S(2)}) collective-permute-start(bf16[784,128]{1,0:T(8,128)(2,1)} %get-tuple-element.24), channel_id=1, source_target_pairs={{0,1},{1,0},{2,3},{3,2},{4,5},{5,4},{6,7},{7,6},{8,9},{9,8},{10,11... | collective-permute-start | bytes 602120 | tf_op jit(solution)/shard_map/ppermute | solution.py:415
  23.2 10.8 %collective-permute-start.1 = (bf16[768,128]{1,0:T(8,128)(2,1)}, bf16[768,128]{1,0:T(8,128)(2,1)S(1)}, u32[]{:S(2)}, u32[]{:S(2)}) collective-permute-start(bf16[768,128]{1,0:T(8,128)(2,1)} %get-tuple-element.25), channel_id=1, source_target_pairs={{0,1},{1,0},{2,3},{3,2},{4,5},{5,4},{6,7},{7,6},{8,9},{9,8},{10,11... | collective-permute-start | bytes 589832 | tf_op jit(solution)/shard_map/ppermute | solution.py:415
  36.6 22.2 %all-to-all-start.1 = ((f16[24,32,128]{2,1,0:T(8,128)(2,1)}), f16[24,32,128]{2,1,0:T(8,128)(2,1)}, u32[]{:S(2)}, u32[]{:S(2)}) async-start(f16[24,32,128]{2,1,0:T(8,128)(2,1)} %convert_element_type.32), calls=%async_computation.1 | async-start | bytes 393216 | tf_op jit(solution)/shard_map/all_to_all | solution.py:406
  47.3 12.5 %copy-start.2 = (f32[16,256]{1,0:T(8,128)S(1)}, f32[16,256]{1,0:T(8,128)}, u32[]{:S(2)}) copy-start(f32[16,256]{1,0:T(8,128)} %held.1) | copy-start | bytes 49156
  47.3 12.5 %copy-start.5 = (f32[16,256]{1,0:T(8,128)S(1)}, f32[16,256]{1,0:T(8,128)}, u32[]{:S(2)}) copy-start(f32[16,256]{1,0:T(8,128)} %accum.1) | copy-start | bytes 49156
  47.3 12.5 %copy-start.7 = (s32[2,4]{1,0:T(2,128)S(1)}, s32[2,4]{1,0:T(2,128)}, u32[]{:S(2)}) copy-start(s32[2,4]{1,0:T(2,128)} %ids.1) | copy-start | bytes 100
  48.8 11.0 %collective-permute-start.2 = (f32[8,128]{1,0:T(8,128)S(1)}, f32[8,128]{1,0:T(8,128)S(1)}, u32[]{:S(2)}, u32[]{:S(2)}) collective-permute-start(f32[8,128]{1,0:T(8,128)S(1)} %get-tuple-element.31), channel_id=1, source_target_pairs={{0,1},{1,0},{2,3},{3,2},{4,5},{5,4},{6,7},{7,6},{8,9},{9,8},{10,11... | collective-permute-start | bytes 12296 | tf_op jit(solution)/shard_map/ppermute | solution.py:415
  82.7 30.7 %all-to-all-start.3 = ((f16[48,22,2,128]{3,2,1,0:T(2,128)(2,1)}), f16[48,22,2,128]{3,2,1,0:T(2,128)(2,1)S(1)}, u32[]{:S(2)}, u32[]{:S(2)}) async-start(f16[48,22,2,128]{3,2,1,0:T(2,128)(2,1)} %bitcast.14), calls=%async_computation.3 | async-start | bytes 1081344 | tf_op jit(solution)/shard_map/all_to_all | solution.py:406
  89.6 11.6 %collective-permute-start.3 = (f16[512,256]{1,0:T(8,128)(2,1)S(1)}, f16[512,256]{1,0:T(8,128)(2,1)S(1)}, u32[]{:S(2)}, u32[]{:S(2)}) collective-permute-start(f16[512,256]{1,0:T(8,128)(2,1)S(1)} %multiply_convert_fusion), channel_id=1, source_target_pairs={{0,1},{1,0},{2,3},{3,2},{4,5},{5,4},{6,7},{7,6},{8,9},{9,8},{10,11... | collective-permute-start | bytes 786440 | tf_op jit(solution)/shard_map/ppermute | solution.py:415
  92.7 13.0 %collective-permute-start.4 = (f32[32,256]{1,0:T(8,128)S(1)}, f32[32,256]{1,0:T(8,128)S(1)}, u32[]{:S(2)}, u32[]{:S(2)}) collective-permute-start(f32[32,256]{1,0:T(8,128)S(1)} %get-tuple-element.34), channel_id=1, source_target_pairs={{48,0},{96,48},{144,96},{192,144},{240,192},{288,240},{336,288},{3... | collective-permute-start | bytes 98312 | tf_op jit(solution)/shard_map/ppermute | solution.py:506
  145.5 11.3 %collective-permute-start.5 = (f32[32,256]{1,0:T(8,128)S(1)}, f32[32,256]{1,0:T(8,128)S(1)}, u32[]{:S(2)}, u32[]{:S(2)}) collective-permute-start(f32[32,256]{1,0:T(8,128)S(1)} %shard_map.111), channel_id=1, source_target_pairs={{48,0},{96,48},{144,96},{192,144},{240,192},{288,240},{336,288},{3... | collective-permute-start | bytes 98312 | tf_op jit(solution)/shard_map/ppermute | solution.py:522

commit v10 on v9

--- a/solution.py
+++ b/solution.py
@@ -293,23 +293,28 @@
 
 
 def item_kernel(got, held, accum, gram_piece, their_piece, ids, state, out):
+    side = lax.axis_index("pair")
     strata = out.shape[0]
     gradient = widths(jnp.sum(got[...], axis=0) * (1.0 / GRAD_SCALE))
     new, state[ROWS:, :] = update(held[...], accum[...], gradient)
     state[0:ROWS, :] = new
     items = halves(new.astype(BF16).astype(F32)) * ITEM_SCALE
-    sent = jnp.concatenate([items, pick_counts(ids, 1), gram_piece[...] + their_piece[...]], axis=0)
-    out[...] = jnp.broadcast_to(sent[None], (strata,) + sent.shape)
-
-
-def gather_kernel(total, met, out, packed):
-    strata = met.shape[0]
+    counts = pick_counts(ids, 1)
+    for to in range(2):
+        piece = jnp.where(side == to, gram_piece[...], their_piece[...])
+        sent = jnp.concatenate([items, counts, piece], axis=0)
+        out[:, to] = jnp.broadcast_to(sent[None], (strata,) + sent.shape)
+
+
+def gather_kernel(total, all_met, out, packed):
+    strata = all_met.shape[0]
+    met = all_met.at[:, lax.axis_index("pair")]
     chunks = lax.axis_size(INNER)
     piece = packed.shape[0] // chunks
     stride = PAIR + 2 * piece
     after = lax.rem(lax.axis_index("stratum") + 1, strata)
     items = met[pl.ds(after, 1), 0:PAIR, :][0]
-    full = jnp.sum(met[:, 40:, :], axis=0)[0:piece] * (GRAM_SCALE / GRAM_STRATUM_SCALE / total)
+    full = jnp.sum(all_met[:, 0, 40:, :] + all_met[:, 1, 40:, :], axis=0)[0:piece] * (GRAM_SCALE / GRAM_STRATUM_SCALE / total)
     counts = jnp.concatenate([met[-1:, 32:40, :], met[:-1, 32:40, :]], axis=0)
     counts = jnp.concatenate([counts[:, :, 0:1], counts[:, :, 64:65]], axis=1)
     rows = [met[:, 0:ROWS, :] * (1.0 / ITEM_SCALE), met[:, ROWS:PAIR, :] * (1.0 / ITEM_SCALE)]
@@ -471,7 +476,6 @@
         got, user_factors, packet, packet_too, tile_values, tile_rows, tile_cols, tile_count,
         scratch=[users_bf, users_bf, pltpu.VMEM(block_shape.shape, F32)],
     )
-    sums = exchanged(sums.astype(F16), GROUP).astype(F32)
     mid, rest, gram_piece, their_piece = call(
         first_users_kernel,
         (users_shape, users_shape, piece_shape, piece_shape),
@@ -485,16 +489,19 @@
             users_f32,
         ],
     )
-    their_piece = swapped(their_piece)
+    sums, mid, rest, gram_piece, their_piece = lax.optimization_barrier(
+        (sums.astype(F16), mid, rest, gram_piece, their_piece)
+    )
+    sums = exchanged(sums, GROUP).astype(F32)
     rest = swapped((rest * REST_SCALE).astype(F16))
     state, sent = call(
         item_kernel,
-        (state_shape, shape((strata, PAIR + 8 + padded, LANES), F32)),
+        (state_shape, shape((strata, 2, PAIR + 8 + padded, LANES), F32)),
         [vm, vm, vm, vm, vm, sm],
         sums, item_factors, item_accum, gram_piece, their_piece, neg_ids,
     )
-    met = exchanged(sent.astype(F16), "stratum")
-    met = met.astype(F32)
+    met = exchanged(sent.astype(F16).reshape(2 * strata, -1, LANES), ("stratum", "pair"))
+    met = met.reshape(sent.shape).astype(F32)
     sent = call(
         functools.partial(gather_kernel, total),
         shape((inners * (PAIR + 2 * piece), LANES), F32),

time: 158 us -> 161 us (1.019)
  blocking collectives: 49.4 us -> 76 us
  starting transfers between devices: 53.6 us -> 39 us
  waiting for transfers between devices: 37.8 us -> 30.6 us
    all_to_all x2 -> x3, blocking collectives: 49.4 us -> 76 us  [exchanged(): return lax.all_to_all(x, axis, 0, 0, tiled=True)]
    all_to_all x3 -> x2, starting transfers between devices: 34.6 us -> 22.8 us  [exchanged(): return lax.all_to_all(x, axis, 0, 0, tiled=True)]
    all_to_all x3 -> x2, waiting for transfers between devices: 15 us -> 7.25 us  [exchanged(): return lax.all_to_all(x, axis, 0, 0, tiled=True)]
    ppermute x4 -> x3, starting transfers between devices: 11.1 us -> 8.31 us  [swapped(): return lax.ppermute(x, 'pair', [(0, 1), (1, 0)])]
    ppermute x4 -> x3, waiting for transfers between devices: 14.1 us -> 14.1 us  [swapped(): return lax.ppermute(x, 'pair', [(0, 1), (1, 0)])]
  transfers between devices with their start and end apart: 9 -> 7, of which waited for: 6 -> 5; matrix products, arithmetic and copies ran while one was open for 1% -> 0% of each run, Pallas kernels for 2% -> 1%
where the time goes in v10:
time: 161 us
  blocking collectives  76 us (47%)
  starting transfers between devices  39 us (24%)
  waiting for transfers between devices  30.6 us (19%)
  Pallas kernels  12 us (7%)
    all_to_all x3, blocking collectives, exchanged(): return lax.all_to_all(x, axis, 0, 0, tiled=True)  76 us
    all_to_all x2, starting transfers between devices, exchanged(): return lax.all_to_all(x, axis, 0, 0, tiled=True)  22.8 us
    ppermute x3, waiting for transfers between devices, swapped(): return lax.ppermute(x, 'pair', [(0, 1), (1, 0)])  14.1 us
    pallas_call x9, Pallas kernels, call(): pl.pallas_call(kernel, out_shape=out_shape, in_specs=specs, out_specs=jax...  12 us
    ppermute x2, waiting for transfers between devices, shards(): state = lax.ppermute(state, 'stratum', onward)  9.18 us
    ppermute x3, starting transfers between devices, swapped(): return lax.ppermute(x, 'pair', [(0, 1), (1, 0)])  8.31 us
    ppermute x2, starting transfers between devices, shards(): state = lax.ppermute(state, 'stratum', onward)  7.86 us
    all_to_all x2, waiting for transfers between devices, exchanged(): return lax.all_to_all(x, axis, 0, 0, tiled=True)  7.25 us
  transfers between devices with their start and end apart: 7, of which 5 were waited for; matrix products, arithmetic and copies ran while one was open for 0% of the time, Pallas kernels for 1%

profile of v10, /device:TPU:7, one launch (start us, length us, event | category | flops | bytes accessed | tf_op | source)
XLA Modules:
  0.0 160.6 jit_solution(7051786558212988775)
XLA Ops:
  0.6 0.0 copy-start.4
  0.6 0.0 copy-start.3
  0.7 0.0 copy-start
  0.7 0.0 copy-start.1
  0.7 0.0 copy-start.6
  0.7 2.2 %shard_map.103 = (bf16[816,128]{1,0:T(8,128)(2,1)}, bf16[784,128]{1,0:T(8,128)(2,1)}, bf16[768,128]{1,0:T(8,128)(2,1)}) custom-call(f32[16,256]{1,0:T(8,128)} %held.1, s32[2,4]{1,0:T(2,128)} %ids.1, f32[512,256]{1,0:T(8,128)} %users.5, bf16[2,8,128,128]{3,2,1,0:T(8,128)(2,1)} %values.3, s32[2,8]{1,0:T(2,128)} %rows.7, s32[2,8]{1,0:T(2,128)} %cols.7, s32[2]{0:T(128)} %bitcast.13), custom_call_target="tpu_custom_call" | custom-call | tf_op jit(solution)/shard_map/pallas_call | solution.py:400
  2.9 17.1 %all-to-all-start = ((bf16[24,17,2,128]{3,2,1,0:T(2,128)(2,1)}), bf16[24,17,2,128]{3,2,1,0:T(2,128)(2,1)S(1)}, u32[]{:S(2)}, u32[]{:S(2)}) async-start(bf16[24,17,2,128]{3,2,1,0:T(2,128)(2,1)} %bitcast.22), calls=%async_computation | async-start | bytes 417792 | tf_op jit(solution)/shard_map/all_to_all | solution.py:411
  20.0 3.2 %collective-permute-start = (bf16[784,128]{1,0:T(8,128)(2,1)}, bf16[784,128]{1,0:T(8,128)(2,1)S(1)}, u32[]{:S(2)}, u32[]{:S(2)}) collective-permute-start(bf16[784,128]{1,0:T(8,128)(2,1)} %get-tuple-element.29), channel_id=1, source_target_pairs={{0,1},{1,0},{2,3},{3,2},{4,5},{5,4},{6,7},{7,6},{8,9},{9,8},{10,11... | collective-permute-start | bytes 602120 | tf_op jit(solution)/shard_map/ppermute | solution.py:420
  23.2 2.1 %collective-permute-start.1 = (bf16[768,128]{1,0:T(8,128)(2,1)}, bf16[768,128]{1,0:T(8,128)(2,1)S(1)}, u32[]{:S(2)}, u32[]{:S(2)}) collective-permute-start(bf16[768,128]{1,0:T(8,128)(2,1)} %get-tuple-element.30), channel_id=1, source_target_pairs={{0,1},{1,0},{2,3},{3,2},{4,5},{5,4},{6,7},{7,6},{8,9},{9,8},{10,11... | collective-permute-start | bytes 589832 | tf_op jit(solution)/shard_map/ppermute | solution.py:420
  25.3 8.7 %collective-permute-done.1.packet_too = bf16[768,128]{1,0:T(8,128)(2,1)S(1)} collective-permute-done((bf16[768,128]{1,0:T(8,128)(2,1)}, bf16[768,128]{1,0:T(8,128)(2,1)S(1)}, u32[]{:S(2)}, u32[]{:S(2)}) %collective-permute-start.1) | collective-permute-done | bytes 196640 | tf_op jit(solution)/shard_map/ppermute | solution.py:420
  34.0 0.0 collective-permute-done.packet
  34.0 0.0 all-to-all-done
  34.0 0.0 copy-done.4
  34.0 0.0 copy-done.3
  34.0 0.0 copy-done
  34.0 0.0 copy-done.1
  34.1 0.0 copy-done.6
  34.1 1.8 %shard_map.104 = (f32[24,32,128]{2,1,0:T(8,128)S(1)}, bf16[768,256]{1,0:T(8,128)(2,1)S(1)}, bf16[8,128,128]{2,1,0:T(8,128)(2,1)S(1)}, bf16[8,128,128]{2,1,0:T(8,128)(2,1)S(1)}) custom-call(bf16[816,128]{1,0:T(8,128)(2,1)S(1)} %bitcast.11, f32[512,256]{1,0:T(8,128)S(1)} %copy-done, bf16[784,128]{1,0:T(8,128)(2,1)S(1)} %collective-permute-done.packet, ...), custom_call_target="tpu_custom_call" | custom-call | tf_op jit(solution)/shard_map/pallas_call | solution.py:400
  35.9 0.0 copy-start.2
  35.9 0.0 copy-start.5
  36.0 0.0 copy-start.7
  36.0 1.5 shard_map.105
  37.4 21.9 %all_to_all.25 = f16[24,32,128]{2,1,0:T(8,128)(2,1)S(1)} all-to-all(f16[24,32,128]{2,1,0:T(8,128)(2,1)S(1)} %convert_element_type.34), channel_id=1, replica_groups=mesh['stratum'=16,'far'=12,'near'=2,'pair'=2] {'far','near'}, dimensions={0} | all-to-all | bytes 393216 | tf_op jit(solution)/shard_map/all_to_all | solution.py:411
  59.4 0.0 copy-done.2
  59.4 0.6 shard_map.106
  60.1 0.1 convert_element_type.36
  60.1 25.5 %all_to_all.26 = f16[32,48,128]{2,1,0:T(8,128)(2,1)S(1)} all-to-all(f16[32,48,128]{2,1,0:T(8,128)(2,1)S(1)} %bitcast.20), channel_id=1, replica_groups=mesh['stratum'=16,'far'=12,'near'=2,'pair'=2] {'stratum','pair'}, dimensions={0} | all-to-all | bytes 786432 | tf_op jit(solution)/shard_map/all_to_all | solution.py:411
  85.6 0.1 convert.3.all_met
  85.7 0.5 shard_map.107
  86.1 0.9 convert_element_type.39
  87.0 5.7 %all-to-all-start.3 = ((f16[48,22,2,128]{3,2,1,0:T(2,128)(2,1)}), f16[48,22,2,128]{3,2,1,0:T(2,128)(2,1)S(1)}, u32[]{:S(2)}, u32[]{:S(2)}) async-start(f16[48,22,2,128]{3,2,1,0:T(2,128)(2,1)} %bitcast.17), calls=%async_computation.3 | async-start | bytes 1081344 | tf_op jit(solution)/shard_map/all_to_all | solution.py:411
  92.7 0.1 multiply_convert_fusion
  92.8 3.0 %collective-permute-start.2 = (f16[512,256]{1,0:T(8,128)(2,1)S(1)}, f16[512,256]{1,0:T(8,128)(2,1)S(1)}, u32[]{:S(2)}, u32[]{:S(2)}) collective-permute-start(f16[512,256]{1,0:T(8,128)(2,1)S(1)} %multiply_convert_fusion), channel_id=1, source_target_pairs={{0,1},{1,0},{2,3},{3,2},{4,5},{5,4},{6,7},{7,6},{8,9},{9,8},{10,11... | collective-permute-start | bytes 786440 | tf_op jit(solution)/shard_map/ppermute | solution.py:420
  95.8 3.1 %collective-permute-start.3 = (f32[32,256]{1,0:T(8,128)S(1)}, f32[32,256]{1,0:T(8,128)S(1)}, u32[]{:S(2)}, u32[]{:S(2)}) collective-permute-start(f32[32,256]{1,0:T(8,128)S(1)} %get-tuple-element.44), channel_id=1, source_target_pairs={{48,0},{96,48},{144,96},{192,144},{240,192},{288,240},{336,288},{3... | collective-permute-start | bytes 98312 | tf_op jit(solution)/shard_map/ppermute | solution.py:513
  99.0 5.4 %collective-permute-done.2 = f16[512,256]{1,0:T(8,128)(2,1)S(1)} collective-permute-done((f16[512,256]{1,0:T(8,128)(2,1)S(1)}, f16[512,256]{1,0:T(8,128)(2,1)S(1)}, u32[]{:S(2)}, u32[]{:S(2)}) %collective-permute-start.2) | collective-permute-done | bytes 262176 | tf_op jit(solution)/shard_map/ppermute | solution.py:420
  104.4 4.9 %collective-permute-done.3.state = f32[32,256]{1,0:T(8,128)S(1)} collective-permute-done((f32[32,256]{1,0:T(8,128)S(1)}, f32[32,256]{1,0:T(8,128)S(1)}, u32[]{:S(2)}, u32[]{:S(2)}) %collective-permute-start.3) | collective-permute-done | bytes 32800 | tf_op jit(solution)/shard_map/ppermute | solution.py:513
  109.3 7.2 %all-to-all-done.3 = f16[48,22,2,128]{3,2,1,0:T(2,128)(2,1)S(1)} async-done(((f16[48,22,2,128]{3,2,1,0:T(2,128)(2,1)}), f16[48,22,2,128]{3,2,1,0:T(2,128)(2,1)S(1)}, u32[]{:S(2)}, u32[]{:S(2)}) %all-to-all-start.3) | async-done | bytes 540704 | tf_op jit(solution)/shard_map/all_to_all | solution.py:411
  116.6 0.1 convert_element_type.41.got
  116.7 3.1 %shard_map.108 = (f32[1824,128]{1,0:T(8,128)S(1)}, f32[512,256]{1,0:T(8,128)S(1)}, bf16[768,256]{1,0:T(8,128)(2,1)S(1)}, bf16[8,128,128]{2,1,0:T(8,128)(2,1)S(1)}) custom-call(f32[2112,128]{1,0:T(8,128)S(1)} %convert_element_type.41.got, f32[512,256]{1,0:T(8,128)S(1)} %copy-done, f32[512,256]{1,0:T(8,128)S(1)} %get-tuple-element.46.mid, ...), custom_call_target="tpu_custom_call" | custom-call | tf_op jit(solution)/shard_map/pallas_call | solution.py:400
  119.8 0.1 convert_element_type.43
  119.9 28.6 %all_to_all.27 = f16[48,19,2,128]{3,2,1,0:T(2,128)(2,1)S(1)} all-to-all(f16[48,19,2,128]{3,2,1,0:T(2,128)(2,1)S(1)} %bitcast.18), channel_id=1, replica_groups=mesh['stratum'=16,'far'=12,'near'=2,'pair'=2] {'far','near','pair'}, dimensions={0} | all-to-all | bytes 933888 | tf_op jit(solution)/shard_map/all_to_all | solution.py:411
  148.5 0.1 convert.2.got
  148.6 0.1 shard_map.111
  148.7 4.8 %collective-permute-start.4 = (f32[32,256]{1,0:T(8,128)S(1)}, f32[32,256]{1,0:T(8,128)S(1)}, u32[]{:S(2)}, u32[]{:S(2)}) collective-permute-start(f32[32,256]{1,0:T(8,128)S(1)} %shard_map.111), channel_id=1, source_target_pairs={{48,0},{96,48},{144,96},{192,144},{240,192},{288,240},{336,288},{3... | collective-permute-start | bytes 98312 | tf_op jit(solution)/shard_map/ppermute | solution.py:529
  153.5 0.9 shard_map.109.users
  154.4 1.3 shard_map.110
  155.7 4.3 %collective-permute-done.4 = f32[32,256]{1,0:T(8,128)S(1)} collective-permute-done((f32[32,256]{1,0:T(8,128)S(1)}, f32[32,256]{1,0:T(8,128)S(1)}, u32[]{:S(2)}, u32[]{:S(2)}) %collective-permute-start.4) | collective-permute-done | bytes 32800 | tf_op jit(solution)/shard_map/ppermute | solution.py:529
  160.0 0.6 fusion
  (5 shorter events, 0.1 us)
Async XLA Ops:
  0.6 33.4 %copy-start.4 = (s32[2,8]{1,0:T(2,128)S(1)}, s32[2,8]{1,0:T(2,128)}, u32[]{:S(2)}) copy-start(s32[2,8]{1,0:T(2,128)} %cols.7) | copy-start | bytes 196
  0.6 33.4 %copy-start.3 = (s32[2,8]{1,0:T(2,128)S(1)}, s32[2,8]{1,0:T(2,128)}, u32[]{:S(2)}) copy-start(s32[2,8]{1,0:T(2,128)} %rows.7) | copy-start | bytes 196
  0.7 33.4 %copy-start = (f32[512,256]{1,0:T(8,128)S(1)}, f32[512,256]{1,0:T(8,128)}, u32[]{:S(2)}) copy-start(f32[512,256]{1,0:T(8,128)} %users.5) | copy-start | bytes 1572868
  0.7 33.4 %copy-start.1 = (bf16[2,8,128,128]{3,2,1,0:T(8,128)(2,1)S(1)}, bf16[2,8,128,128]{3,2,1,0:T(8,128)(2,1)}, u32[]{:S(2)}) copy-start(bf16[2,8,128,128]{3,2,1,0:T(8,128)(2,1)} %values.3) | copy-start | bytes 1572868
  0.7 33.4 %copy-start.6 = (s32[2,1]{0,1:T(1,128)S(1)}, s32[2,1]{0,1:T(1,128)}, u32[]{:S(2)}) copy-start(s32[2,1]{0,1:T(1,128)} %param.14) | copy-start | bytes 28
  2.9 31.2 %all-to-all-start = ((bf16[24,17,2,128]{3,2,1,0:T(2,128)(2,1)}), bf16[24,17,2,128]{3,2,1,0:T(2,128)(2,1)S(1)}, u32[]{:S(2)}, u32[]{:S(2)}) async-start(bf16[24,17,2,128]{3,2,1,0:T(2,128)(2,1)} %bitcast.22), calls=%async_computation | async-start | bytes 417792 | tf_op jit(solution)/shard_map/all_to_all | solution.py:411
  20.0 14.0 %collective-permute-start = (bf16[784,128]{1,0:T(8,128)(2,1)}, bf16[784,128]{1,0:T(8,128)(2,1)S(1)}, u32[]{:S(2)}, u32[]{:S(2)}) collective-permute-start(bf16[784,128]{1,0:T(8,128)(2,1)} %get-tuple-element.29), channel_id=1, source_target_pairs={{0,1},{1,0},{2,3},{3,2},{4,5},{5,4},{6,7},{7,6},{8,9},{9,8},{10,11... | collective-permute-start | bytes 602120 | tf_op jit(solution)/shard_map/ppermute | solution.py:420
  23.2 10.8 %collective-permute-start.1 = (bf16[768,128]{1,0:T(8,128)(2,1)}, bf16[768,128]{1,0:T(8,128)(2,1)S(1)}, u32[]{:S(2)}, u32[]{:S(2)}) collective-permute-start(bf16[768,128]{1,0:T(8,128)(2,1)} %get-tuple-element.30), channel_id=1, source_target_pairs={{0,1},{1,0},{2,3},{3,2},{4,5},{5,4},{6,7},{7,6},{8,9},{9,8},{10,11... | collective-permute-start | bytes 589832 | tf_op jit(solution)/shard_map/ppermute | solution.py:420
  35.9 23.4 %copy-start.2 = (f32[16,256]{1,0:T(8,128)S(1)}, f32[16,256]{1,0:T(8,128)}, u32[]{:S(2)}) copy-start(f32[16,256]{1,0:T(8,128)} %held.1) | copy-start | bytes 49156
  35.9 23.4 %copy-start.5 = (f32[16,256]{1,0:T(8,128)S(1)}, f32[16,256]{1,0:T(8,128)}, u32[]{:S(2)}) copy-start(f32[16,256]{1,0:T(8,128)} %accum.1) | copy-start | bytes 49156
  36.0 23.4 %copy-start.7 = (s32[2,4]{1,0:T(2,128)S(1)}, s32[2,4]{1,0:T(2,128)}, u32[]{:S(2)}) copy-start(s32[2,4]{1,0:T(2,128)} %ids.1) | copy-start | bytes 100
  87.0 29.5 %all-to-all-start.3 = ((f16[48,22,2,128]{3,2,1,0:T(2,128)(2,1)}), f16[48,22,2,128]{3,2,1,0:T(2,128)(2,1)S(1)}, u32[]{:S(2)}, u32[]{:S(2)}) async-start(f16[48,22,2,128]{3,2,1,0:T(2,128)(2,1)} %bitcast.17), calls=%async_computation.3 | async-start | bytes 1081344 | tf_op jit(solution)/shard_map/all_to_all | solution.py:411
  92.8 11.6 %collective-permute-start.2 = (f16[512,256]{1,0:T(8,128)(2,1)S(1)}, f16[512,256]{1,0:T(8,128)(2,1)S(1)}, u32[]{:S(2)}, u32[]{:S(2)}) collective-permute-start(f16[512,256]{1,0:T(8,128)(2,1)S(1)} %multiply_convert_fusion), channel_id=1, source_target_pairs={{0,1},{1,0},{2,3},{3,2},{4,5},{5,4},{6,7},{7,6},{8,9},{9,8},{10,11... | collective-permute-start | bytes 786440 | tf_op jit(solution)/shard_map/ppermute | solution.py:420
  95.8 13.4 %collective-permute-start.3 = (f32[32,256]{1,0:T(8,128)S(1)}, f32[32,256]{1,0:T(8,128)S(1)}, u32[]{:S(2)}, u32[]{:S(2)}) collective-permute-start(f32[32,256]{1,0:T(8,128)S(1)} %get-tuple-element.44), channel_id=1, source_target_pairs={{48,0},{96,48},{144,96},{192,144},{240,192},{288,240},{336,288},{3... | collective-permute-start | bytes 98312 | tf_op jit(solution)/shard_map/ppermute | solution.py:513
  148.7 11.3 %collective-permute-start.4 = (f32[32,256]{1,0:T(8,128)S(1)}, f32[32,256]{1,0:T(8,128)S(1)}, u32[]{:S(2)}, u32[]{:S(2)}) collective-permute-start(f32[32,256]{1,0:T(8,128)S(1)} %shard_map.111), channel_id=1, source_target_pairs={{48,0},{96,48},{144,96},{192,144},{240,192},{288,240},{336,288},{3... | collective-permute-start | bytes 98312 | tf_op jit(solution)/shard_map/ppermute | solution.py:529

commit v11 on v9

--- a/solution.py
+++ b/solution.py
@@ -114,7 +114,7 @@
 
 
 def start_kernel(*refs):
-    given, (out, *packets), taken, done = refs[:7], refs[7:10], refs[10:17], refs[17]
+    given, (out, *packets), taken, done = refs[:7], refs[7:11], refs[11:18], refs[18]
     held, ids, users, values, rows, cols, count = taken
     copies = []
     for i, (source, target) in enumerate(zip(given, taken, strict=True)):
@@ -141,14 +141,12 @@
     slots = values.shape[0]
     for k in range(slots // 2):
         other = beside(values[k + slots // 2].astype(F32), theirs)
-        at = size + k // 2 * LANES
-        packets[k % 2][at : at + LANES, :] = jnp.where(first, values[k].astype(F32), other).astype(BF16)
+        packets[2][k * LANES : (k + 1) * LANES, :] = jnp.where(first, values[k].astype(F32), other).astype(BF16)
     lane = lax.broadcasted_iota(jnp.int32, (16, LANES), 1)
     lists = jnp.where(lane == 2 * slots, count[0], 0)
     for k in range(slots):
         lists = jnp.where(lane == k, rows[0, k], jnp.where(lane == slots + k, cols[0, k], lists))
-    at = size + slots // 4 * LANES
-    packets[0][at : at + 16, :] = lists.astype(F32).astype(BF16)
+    packets[0][size : size + 16, :] = lists.astype(F32).astype(BF16)
 
 
 def lists_of(packet, slots):
@@ -198,7 +196,7 @@
 
 
 def first_kernel(
-    got, users, packet, packet_too, values, rows, cols, count,
+    got, users, packet, packet_too, packet_three, values, rows, cols, count,
     sums, block, errors, their_errors, users_bf, their_users, grads,
 ):
     stride = PAIR + 2
@@ -219,8 +217,8 @@
     theirs = lists_of(packet, slots)
 
     def their_values(k):
-        at = size + k % (slots // 2) // 2 * tile_u
-        shared = (packet, packet_too)[k % 2][at : at + tile_u, :].astype(F32)
+        at = k % (slots // 2) * tile_u
+        shared = packet_three[at : at + tile_u, :].astype(F32)
         return shared if k < slots // 2 else beside(shared, 1 - side)
 
     def add(col, part):
@@ -294,7 +292,7 @@
 
 def item_kernel(got, held, accum, gram_piece, their_piece, ids, state, out):
     strata = out.shape[0]
-    gradient = widths(jnp.sum(got[...], axis=0) * (1.0 / GRAD_SCALE))
+    gradient = widths(got[...] * (1.0 / GRAD_SCALE))
     new, state[ROWS:, :] = update(held[...], accum[...], gradient)
     state[0:ROWS, :] = new
     items = halves(new.astype(BF16).astype(F32)) * ITEM_SCALE
@@ -440,13 +438,14 @@
 
     slots = tile_values.shape[1]
     tile_count = tile_count.reshape(-1)
-    packet_rows = user_factors.shape[0] + slots // 4 * LANES
-    sent, packet, packet_too = call(
+    packet_rows = user_factors.shape[0]
+    sent, packet, packet_too, packet_three = call(
         start_kernel,
         (
             shape((group * (PAIR + 2), LANES), BF16),
             shape((packet_rows + 16, LANES), BF16),
             shape((packet_rows, LANES), BF16),
+            shape((slots // 2 * LANES, LANES), BF16),
         ),
         [pl.BlockSpec(memory_space=pltpu.HBM)] * 7,
         item_factors, neg_ids, user_factors, tile_values, tile_rows, tile_cols, tile_count,
@@ -463,15 +462,15 @@
         vmem=62,
     )
     got = chunks_exchanged(sent, GROUP)
-    packet, packet_too = swapped(packet), swapped(packet_too)
+    packet, packet_too, packet_three = swapped(packet), swapped(packet_too), swapped(packet_three)
     sums, block, errors, their_errors = call(
         first_kernel,
         (shape((group, PAIR, LANES), F32), block_shape, errors_shape, errors_shape),
-        [vm, vm, vm, vm, vm, sm, sm, sm],
-        got, user_factors, packet, packet_too, tile_values, tile_rows, tile_cols, tile_count,
+        [vm, vm, vm, vm, vm, vm, sm, sm, sm],
+        got, user_factors, packet, packet_too, packet_three, tile_values, tile_rows, tile_cols, tile_count,
         scratch=[users_bf, users_bf, pltpu.VMEM(block_shape.shape, F32)],
     )
-    sums = exchanged(sums.astype(F16), GROUP).astype(F32)
+    sums = jnp.sum(exchanged(sums.astype(F16), GROUP).astype(F32), axis=0)
     mid, rest, gram_piece, their_piece = call(
         first_users_kernel,
         (users_shape, users_shape, piece_shape, piece_shape),

time: 158 us -> 158 us (level)
  starting transfers between devices: 53.6 us -> 56.7 us
  waiting for transfers between devices: 37.8 us -> 35.5 us
    ppermute x4 -> x5, waiting for transfers between devices: 14.1 us -> 11.2 us  [swapped(): return lax.ppermute(x, 'pair', [(0, 1), (1, 0)])]
    ppermute x4 -> x5, starting transfers between devices: 11.1 us -> 13.7 us  [swapped(): return lax.ppermute(x, 'pair', [(0, 1), (1, 0)])]
  transfers between devices with their start and end apart: 9 -> 10, of which waited for: 6 -> 7; matrix products, arithmetic and copies ran while one was open for 1% -> 1% of each run, Pallas kernels for 2% -> 2%
where the time goes in v11:
time: 158 us; the launch traced here: 157 us
  starting transfers between devices  56.7 us (36%)
  blocking collectives  48.7 us (31%)
  waiting for transfers between devices  35.5 us (22%)
  Pallas kernels  12 us (8%)
  other arithmetic  2.91 us (2%)
    all_to_all x2, blocking collectives, exchanged(): return lax.all_to_all(x, axis, 0, 0, tiled=True)  48.7 us
    all_to_all x3, starting transfers between devices, exchanged(): return lax.all_to_all(x, axis, 0, 0, tiled=True)  35.1 us
    all_to_all x3, waiting for transfers between devices, exchanged(): return lax.all_to_all(x, axis, 0, 0, tiled=True)  15.7 us
    ppermute x5, starting transfers between devices, swapped(): return lax.ppermute(x, 'pair', [(0, 1), (1, 0)])  13.7 us
    pallas_call x9, Pallas kernels, call(): pl.pallas_call(kernel, out_shape=out_shape, in_specs=specs, out_specs=jax...  12 us
    ppermute x5, waiting for transfers between devices, swapped(): return lax.ppermute(x, 'pair', [(0, 1), (1, 0)])  11.2 us
    ppermute x2, waiting for transfers between devices, shards(): state = lax.ppermute(state, 'stratum', onward)  8.72 us
    ppermute x2, starting transfers between devices, shards(): state = lax.ppermute(state, 'stratum', onward)  7.9 us
  transfers between devices with their start and end apart: 10, of which 7 were waited for; matrix products, arithmetic and copies ran while one was open for 1% of the time, Pallas kernels for 2%

profile of v11, /device:TPU:7, one launch (start us, length us, event | category | flops | bytes accessed | tf_op | source)
XLA Modules:
  0.0 157.4 jit_solution(7555426697824259178)
XLA Ops:
  0.6 0.0 copy-start.4
  0.6 0.0 copy-start.3
  0.7 0.0 copy-start
  0.7 0.0 copy-start.1
  0.7 0.0 copy-start.6
  0.7 2.2 %shard_map.103 = (bf16[816,128]{1,0:T(8,128)(2,1)}, bf16[528,128]{1,0:T(8,128)(2,1)}, bf16[512,128]{1,0:T(8,128)(2,1)}, bf16[512,128]{1,0:T(8,128)(2,1)}) custom-call(f32[16,256]{1,0:T(8,128)} %held.1, s32[2,4]{1,0:T(2,128)} %ids.1, f32[512,256]{1,0:T(8,128)} %users.5, bf16[2,8,128,128]{3,2,1,0:T(8,128)(2,1)} %values.3, s32[2,8]{1,0:T(2,128)} %rows.7, ...), custom_call_target="tpu_custom_call" | custom-call | tf_op jit(solution)/shard_map/pallas_call | solution.py:393
  2.9 17.1 %all-to-all-start = ((bf16[24,17,2,128]{3,2,1,0:T(2,128)(2,1)}), bf16[24,17,2,128]{3,2,1,0:T(2,128)(2,1)S(1)}, u32[]{:S(2)}, u32[]{:S(2)}) async-start(bf16[24,17,2,128]{3,2,1,0:T(2,128)(2,1)} %bitcast.16), calls=%async_computation | async-start | bytes 417792 | tf_op jit(solution)/shard_map/all_to_all | solution.py:404
  20.0 3.2 %collective-permute-start = (bf16[528,128]{1,0:T(8,128)(2,1)}, bf16[528,128]{1,0:T(8,128)(2,1)S(1)}, u32[]{:S(2)}, u32[]{:S(2)}) collective-permute-start(bf16[528,128]{1,0:T(8,128)(2,1)} %get-tuple-element.25), channel_id=1, source_target_pairs={{0,1},{1,0},{2,3},{3,2},{4,5},{5,4},{6,7},{7,6},{8,9},{9,8},{10,11... | collective-permute-start | bytes 405512 | tf_op jit(solution)/shard_map/ppermute | solution.py:413
  23.2 2.1 %collective-permute-start.1 = (bf16[512,128]{1,0:T(8,128)(2,1)}, bf16[512,128]{1,0:T(8,128)(2,1)S(1)}, u32[]{:S(2)}, u32[]{:S(2)}) collective-permute-start(bf16[512,128]{1,0:T(8,128)(2,1)} %get-tuple-element.26), channel_id=1, source_target_pairs={{0,1},{1,0},{2,3},{3,2},{4,5},{5,4},{6,7},{7,6},{8,9},{9,8},{10,11... | collective-permute-start | bytes 393224 | tf_op jit(solution)/shard_map/ppermute | solution.py:413
  25.3 3.2 %collective-permute-start.2 = (bf16[512,128]{1,0:T(8,128)(2,1)}, bf16[512,128]{1,0:T(8,128)(2,1)S(1)}, u32[]{:S(2)}, u32[]{:S(2)}) collective-permute-start(bf16[512,128]{1,0:T(8,128)(2,1)} %get-tuple-element.27), channel_id=1, source_target_pairs={{0,1},{1,0},{2,3},{3,2},{4,5},{5,4},{6,7},{7,6},{8,9},{9,8},{10,11... | collective-permute-start | bytes 393224 | tf_op jit(solution)/shard_map/ppermute | solution.py:413
  28.5 2.3 %collective-permute-done.1.packet_too = bf16[512,128]{1,0:T(8,128)(2,1)S(1)} collective-permute-done((bf16[512,128]{1,0:T(8,128)(2,1)}, bf16[512,128]{1,0:T(8,128)(2,1)S(1)}, u32[]{:S(2)}, u32[]{:S(2)}) %collective-permute-start.1) | collective-permute-done | bytes 131104 | tf_op jit(solution)/shard_map/ppermute | solution.py:413
  30.8 3.5 %collective-permute-done.2.packet_three = bf16[512,128]{1,0:T(8,128)(2,1)S(1)} collective-permute-done((bf16[512,128]{1,0:T(8,128)(2,1)}, bf16[512,128]{1,0:T(8,128)(2,1)S(1)}, u32[]{:S(2)}, u32[]{:S(2)}) %collective-permute-start.2) | collective-permute-done | bytes 131104 | tf_op jit(solution)/shard_map/ppermute | solution.py:413
  34.2 0.0 collective-permute-done.packet
  34.2 0.0 all-to-all-done
  34.3 1.8 %shard_map.104 = (f32[24,32,128]{2,1,0:T(8,128)S(1)}, bf16[768,256]{1,0:T(8,128)(2,1)S(1)}, bf16[8,128,128]{2,1,0:T(8,128)(2,1)S(1)}, bf16[8,128,128]{2,1,0:T(8,128)(2,1)S(1)}) custom-call(bf16[816,128]{1,0:T(8,128)(2,1)S(1)} %bitcast.8, f32[512,256]{1,0:T(8,128)S(1)} %copy-done, bf16[528,128]{1,0:T(8,128)(2,1)S(1)} %collective-permute-done.packet, ...), custom_call_target="tpu_custom_call" | custom-call | tf_op jit(solution)/shard_map/pallas_call | solution.py:393
  36.1 0.7 convert_element_type.32
  36.9 11.1 %all-to-all-start.1 = ((f16[24,32,128]{2,1,0:T(8,128)(2,1)}), f16[24,32,128]{2,1,0:T(8,128)(2,1)}, u32[]{:S(2)}, u32[]{:S(2)}) async-start(f16[24,32,128]{2,1,0:T(8,128)(2,1)} %convert_element_type.32), calls=%async_computation.1 | async-start | bytes 393216 | tf_op jit(solution)/shard_map/all_to_all | solution.py:404
  47.9 0.0 copy-start.2
  47.9 0.0 copy-start.5
  47.9 0.0 copy-start.7
  48.0 1.5 shard_map.105
  49.4 2.1 %collective-permute-start.3 = (f32[8,128]{1,0:T(8,128)S(1)}, f32[8,128]{1,0:T(8,128)S(1)}, u32[]{:S(2)}, u32[]{:S(2)}) collective-permute-start(f32[8,128]{1,0:T(8,128)S(1)} %get-tuple-element.33), channel_id=1, source_target_pairs={{0,1},{1,0},{2,3},{3,2},{4,5},{5,4},{6,7},{7,6},{8,9},{9,8},{10,11... | collective-permute-start | bytes 12296 | tf_op jit(solution)/shard_map/ppermute | solution.py:413
  51.6 7.9 %all-to-all-done.1 = f16[24,32,128]{2,1,0:T(8,128)(2,1)} async-done(((f16[24,32,128]{2,1,0:T(8,128)(2,1)}), f16[24,32,128]{2,1,0:T(8,128)(2,1)}, u32[]{:S(2)}, u32[]{:S(2)}) %all-to-all-start.1) | async-done | bytes 196640 | tf_op jit(solution)/shard_map/all_to_all | solution.py:404
  59.5 1.0 convert_reduce_fusion.got
  60.5 0.0 collective-permute-done.3.their_piece
  60.5 0.0 copy-done.2
  60.5 0.6 shard_map.106
  61.1 20.2 %all_to_all.25 = f16[16,48,128]{2,1,0:T(8,128)(2,1)S(1)} all-to-all(f16[16,48,128]{2,1,0:T(8,128)(2,1)S(1)} %convert_element_type.34), channel_id=1, replica_groups=mesh['stratum'=16,'far'=12,'near'=2,'pair'=2] {'stratum'}, dimensions={0} | all-to-all | bytes 393216 | tf_op jit(solution)/shard_map/all_to_all | solution.py:404
  81.3 0.5 shard_map.107
  81.8 0.9 convert_element_type.36
  82.7 6.9 %all-to-all-start.3 = ((f16[48,22,2,128]{3,2,1,0:T(2,128)(2,1)}), f16[48,22,2,128]{3,2,1,0:T(2,128)(2,1)S(1)}, u32[]{:S(2)}, u32[]{:S(2)}) async-start(f16[48,22,2,128]{3,2,1,0:T(2,128)(2,1)} %bitcast.3), calls=%async_computation.3 | async-start | bytes 1081344 | tf_op jit(solution)/shard_map/all_to_all | solution.py:404
  89.6 0.1 multiply_convert_fusion
  89.7 3.0 %collective-permute-start.4 = (f16[512,256]{1,0:T(8,128)(2,1)S(1)}, f16[512,256]{1,0:T(8,128)(2,1)S(1)}, u32[]{:S(2)}, u32[]{:S(2)}) collective-permute-start(f16[512,256]{1,0:T(8,128)(2,1)S(1)} %multiply_convert_fusion), channel_id=1, source_target_pairs={{0,1},{1,0},{2,3},{3,2},{4,5},{5,4},{6,7},{7,6},{8,9},{9,8},{10,11... | collective-permute-start | bytes 786440 | tf_op jit(solution)/shard_map/ppermute | solution.py:413
  92.7 3.1 %collective-permute-start.5 = (f32[32,256]{1,0:T(8,128)S(1)}, f32[32,256]{1,0:T(8,128)S(1)}, u32[]{:S(2)}, u32[]{:S(2)}) collective-permute-start(f32[32,256]{1,0:T(8,128)S(1)} %get-tuple-element.36), channel_id=1, source_target_pairs={{48,0},{96,48},{144,96},{192,144},{240,192},{288,240},{336,288},{3... | collective-permute-start | bytes 98312 | tf_op jit(solution)/shard_map/ppermute | solution.py:505
  95.8 5.4 %collective-permute-done.4 = f16[512,256]{1,0:T(8,128)(2,1)S(1)} collective-permute-done((f16[512,256]{1,0:T(8,128)(2,1)S(1)}, f16[512,256]{1,0:T(8,128)(2,1)S(1)}, u32[]{:S(2)}, u32[]{:S(2)}) %collective-permute-start.4) | collective-permute-done | bytes 262176 | tf_op jit(solution)/shard_map/ppermute | solution.py:413
  101.3 4.5 %collective-permute-done.5.state = f32[32,256]{1,0:T(8,128)S(1)} collective-permute-done((f32[32,256]{1,0:T(8,128)S(1)}, f32[32,256]{1,0:T(8,128)S(1)}, u32[]{:S(2)}, u32[]{:S(2)}) %collective-permute-start.5) | collective-permute-done | bytes 32800 | tf_op jit(solution)/shard_map/ppermute | solution.py:505
  105.7 7.7 %all-to-all-done.3 = f16[48,22,2,128]{3,2,1,0:T(2,128)(2,1)S(1)} async-done(((f16[48,22,2,128]{3,2,1,0:T(2,128)(2,1)}), f16[48,22,2,128]{3,2,1,0:T(2,128)(2,1)S(1)}, u32[]{:S(2)}, u32[]{:S(2)}) %all-to-all-start.3) | async-done | bytes 540704 | tf_op jit(solution)/shard_map/all_to_all | solution.py:404
  113.5 0.1 convert_element_type.38.got
  113.6 3.1 %shard_map.108 = (f32[1824,128]{1,0:T(8,128)S(1)}, f32[512,256]{1,0:T(8,128)S(1)}, bf16[768,256]{1,0:T(8,128)(2,1)S(1)}, bf16[8,128,128]{2,1,0:T(8,128)(2,1)S(1)}) custom-call(f32[2112,128]{1,0:T(8,128)S(1)} %convert_element_type.38.got, f32[512,256]{1,0:T(8,128)S(1)} %copy-done, f32[512,256]{1,0:T(8,128)S(1)} %get-tuple-element.38.mid, ...), custom_call_target="tpu_custom_call" | custom-call | tf_op jit(solution)/shard_map/pallas_call | solution.py:393
  116.7 0.1 convert_element_type.40
  116.8 28.6 %all_to_all.26 = f16[48,19,2,128]{3,2,1,0:T(2,128)(2,1)S(1)} all-to-all(f16[48,19,2,128]{3,2,1,0:T(2,128)(2,1)S(1)} %bitcast.14), channel_id=1, replica_groups=mesh['stratum'=16,'far'=12,'near'=2,'pair'=2] {'far','near','pair'}, dimensions={0} | all-to-all | bytes 933888 | tf_op jit(solution)/shard_map/all_to_all | solution.py:404
  145.4 0.1 convert.1.got
  145.4 0.1 shard_map.111
  145.5 4.8 %collective-permute-start.6 = (f32[32,256]{1,0:T(8,128)S(1)}, f32[32,256]{1,0:T(8,128)S(1)}, u32[]{:S(2)}, u32[]{:S(2)}) collective-permute-start(f32[32,256]{1,0:T(8,128)S(1)} %shard_map.111), channel_id=1, source_target_pairs={{48,0},{96,48},{144,96},{192,144},{240,192},{288,240},{336,288},{3... | collective-permute-start | bytes 98312 | tf_op jit(solution)/shard_map/ppermute | solution.py:521
  150.3 0.9 shard_map.109.users
  151.2 1.3 shard_map.110
  152.5 4.3 %collective-permute-done.6 = f32[32,256]{1,0:T(8,128)S(1)} collective-permute-done((f32[32,256]{1,0:T(8,128)S(1)}, f32[32,256]{1,0:T(8,128)S(1)}, u32[]{:S(2)}, u32[]{:S(2)}) %collective-permute-start.6) | collective-permute-done | bytes 32800 | tf_op jit(solution)/shard_map/ppermute | solution.py:521
  156.8 0.6 fusion
  (10 shorter events, 0.1 us)
Async XLA Ops:
  0.6 33.6 %copy-start.4 = (s32[2,8]{1,0:T(2,128)S(1)}, s32[2,8]{1,0:T(2,128)}, u32[]{:S(2)}) copy-start(s32[2,8]{1,0:T(2,128)} %cols.7) | copy-start | bytes 196
  0.6 33.6 %copy-start.3 = (s32[2,8]{1,0:T(2,128)S(1)}, s32[2,8]{1,0:T(2,128)}, u32[]{:S(2)}) copy-start(s32[2,8]{1,0:T(2,128)} %rows.7) | copy-start | bytes 196
  0.7 33.6 %copy-start = (f32[512,256]{1,0:T(8,128)S(1)}, f32[512,256]{1,0:T(8,128)}, u32[]{:S(2)}) copy-start(f32[512,256]{1,0:T(8,128)} %users.5) | copy-start | bytes 1572868
  0.7 33.6 %copy-start.1 = (bf16[2,8,128,128]{3,2,1,0:T(8,128)(2,1)S(1)}, bf16[2,8,128,128]{3,2,1,0:T(8,128)(2,1)}, u32[]{:S(2)}) copy-start(bf16[2,8,128,128]{3,2,1,0:T(8,128)(2,1)} %values.3) | copy-start | bytes 1572868
  0.7 33.6 %copy-start.6 = (s32[2,1]{0,1:T(1,128)S(1)}, s32[2,1]{0,1:T(1,128)}, u32[]{:S(2)}) copy-start(s32[2,1]{0,1:T(1,128)} %param.14) | copy-start | bytes 28
  2.9 31.4 %all-to-all-start = ((bf16[24,17,2,128]{3,2,1,0:T(2,128)(2,1)}), bf16[24,17,2,128]{3,2,1,0:T(2,128)(2,1)S(1)}, u32[]{:S(2)}, u32[]{:S(2)}) async-start(bf16[24,17,2,128]{3,2,1,0:T(2,128)(2,1)} %bitcast.16), calls=%async_computation | async-start | bytes 417792 | tf_op jit(solution)/shard_map/all_to_all | solution.py:404
  20.0 14.2 %collective-permute-start = (bf16[528,128]{1,0:T(8,128)(2,1)}, bf16[528,128]{1,0:T(8,128)(2,1)S(1)}, u32[]{:S(2)}, u32[]{:S(2)}) collective-permute-start(bf16[528,128]{1,0:T(8,128)(2,1)} %get-tuple-element.25), channel_id=1, source_target_pairs={{0,1},{1,0},{2,3},{3,2},{4,5},{5,4},{6,7},{7,6},{8,9},{9,8},{10,11... | collective-permute-start | bytes 405512 | tf_op jit(solution)/shard_map/ppermute | solution.py:413
  23.2 7.6 %collective-permute-start.1 = (bf16[512,128]{1,0:T(8,128)(2,1)}, bf16[512,128]{1,0:T(8,128)(2,1)S(1)}, u32[]{:S(2)}, u32[]{:S(2)}) collective-permute-start(bf16[512,128]{1,0:T(8,128)(2,1)} %get-tuple-element.26), channel_id=1, source_target_pairs={{0,1},{1,0},{2,3},{3,2},{4,5},{5,4},{6,7},{7,6},{8,9},{9,8},{10,11... | collective-permute-start | bytes 393224 | tf_op jit(solution)/shard_map/ppermute | solution.py:413
  25.3 8.9 %collective-permute-start.2 = (bf16[512,128]{1,0:T(8,128)(2,1)}, bf16[512,128]{1,0:T(8,128)(2,1)S(1)}, u32[]{:S(2)}, u32[]{:S(2)}) collective-permute-start(bf16[512,128]{1,0:T(8,128)(2,1)} %get-tuple-element.27), channel_id=1, source_target_pairs={{0,1},{1,0},{2,3},{3,2},{4,5},{5,4},{6,7},{7,6},{8,9},{9,8},{10,11... | collective-permute-start | bytes 393224 | tf_op jit(solution)/shard_map/ppermute | solution.py:413
  36.9 22.6 %all-to-all-start.1 = ((f16[24,32,128]{2,1,0:T(8,128)(2,1)}), f16[24,32,128]{2,1,0:T(8,128)(2,1)}, u32[]{:S(2)}, u32[]{:S(2)}) async-start(f16[24,32,128]{2,1,0:T(8,128)(2,1)} %convert_element_type.32), calls=%async_computation.1 | async-start | bytes 393216 | tf_op jit(solution)/shard_map/all_to_all | solution.py:404
  47.9 12.6 %copy-start.2 = (f32[16,256]{1,0:T(8,128)S(1)}, f32[16,256]{1,0:T(8,128)}, u32[]{:S(2)}) copy-start(f32[16,256]{1,0:T(8,128)} %held.1) | copy-start | bytes 49156
  47.9 12.6 %copy-start.5 = (f32[16,256]{1,0:T(8,128)S(1)}, f32[16,256]{1,0:T(8,128)}, u32[]{:S(2)}) copy-start(f32[16,256]{1,0:T(8,128)} %accum.1) | copy-start | bytes 49156
  47.9 12.5 %copy-start.7 = (s32[2,4]{1,0:T(2,128)S(1)}, s32[2,4]{1,0:T(2,128)}, u32[]{:S(2)}) copy-start(s32[2,4]{1,0:T(2,128)} %ids.1) | copy-start | bytes 100
  49.4 11.0 %collective-permute-start.3 = (f32[8,128]{1,0:T(8,128)S(1)}, f32[8,128]{1,0:T(8,128)S(1)}, u32[]{:S(2)}, u32[]{:S(2)}) collective-permute-start(f32[8,128]{1,0:T(8,128)S(1)} %get-tuple-element.33), channel_id=1, source_target_pairs={{0,1},{1,0},{2,3},{3,2},{4,5},{5,4},{6,7},{7,6},{8,9},{9,8},{10,11... | collective-permute-start | bytes 12296 | tf_op jit(solution)/shard_map/ppermute | solution.py:413
  82.7 30.8 %all-to-all-start.3 = ((f16[48,22,2,128]{3,2,1,0:T(2,128)(2,1)}), f16[48,22,2,128]{3,2,1,0:T(2,128)(2,1)S(1)}, u32[]{:S(2)}, u32[]{:S(2)}) async-start(f16[48,22,2,128]{3,2,1,0:T(2,128)(2,1)} %bitcast.3), calls=%async_computation.3 | async-start | bytes 1081344 | tf_op jit(solution)/shard_map/all_to_all | solution.py:404
  89.7 11.6 %collective-permute-start.4 = (f16[512,256]{1,0:T(8,128)(2,1)S(1)}, f16[512,256]{1,0:T(8,128)(2,1)S(1)}, u32[]{:S(2)}, u32[]{:S(2)}) collective-permute-start(f16[512,256]{1,0:T(8,128)(2,1)S(1)} %multiply_convert_fusion), channel_id=1, source_target_pairs={{0,1},{1,0},{2,3},{3,2},{4,5},{5,4},{6,7},{7,6},{8,9},{9,8},{10,11... | collective-permute-start | bytes 786440 | tf_op jit(solution)/shard_map/ppermute | solution.py:413
  92.7 13.0 %collective-permute-start.5 = (f32[32,256]{1,0:T(8,128)S(1)}, f32[32,256]{1,0:T(8,128)S(1)}, u32[]{:S(2)}, u32[]{:S(2)}) collective-permute-start(f32[32,256]{1,0:T(8,128)S(1)} %get-tuple-element.36), channel_id=1, source_target_pairs={{48,0},{96,48},{144,96},{192,144},{240,192},{288,240},{336,288},{3... | collective-permute-start | bytes 98312 | tf_op jit(solution)/shard_map/ppermute | solution.py:505
  145.5 11.3 %collective-permute-start.6 = (f32[32,256]{1,0:T(8,128)S(1)}, f32[32,256]{1,0:T(8,128)S(1)}, u32[]{:S(2)}, u32[]{:S(2)}) collective-permute-start(f32[32,256]{1,0:T(8,128)S(1)} %shard_map.111), channel_id=1, source_target_pairs={{48,0},{96,48},{144,96},{192,144},{240,192},{288,240},{336,288},{3... | collective-permute-start | bytes 98312 | tf_op jit(solution)/shard_map/ppermute | solution.py:521
